TPU v7x, 128 devices: a whole 4x4x4 slice. The times are simulated.
128 devices in a mesh: shard: 2 (over x_hi), ctx: 32 (over y, z, core), tp: 2 (over x_lo).
Axes of the slice: x: 4 (x_hi: 2, x_lo: 2; x = x_hi * 2 + x_lo), y: 4, z: 4, core: 2. Of those that a mesh axis runs over, the one named last changes fastest.
Arguments:
- tokens: bfloat16 [2, 4096, 2048], P('shard', 'ctx'), may hold values from -6 to 6
- segments: int32 [2, 4096], P('shard', 'ctx'), may hold values from 0 to 2, as said below
- decay_rate: float32 [8], P('tp'), may hold values from 2.4414063e-05 to 0.046875
- first_gain: float32 [2048], replicated, may hold values from 0.25 to 1.75
- first_bias: float32 [2048], replicated, may hold values from -3 to 3
- query_weight: bfloat16 [2048, 2048], P('shard', 'tp'), may hold values from -0.125 to 0.125
- key_weight: bfloat16 [2048, 2048], P('shard', 'tp'), may hold values from -0.125 to 0.125
- value_weight: bfloat16 [2048, 3456], P('shard', 'tp'), may hold values from -0.125 to 0.125
- gate_weight: bfloat16 [2048, 3456], P('shard', 'tp'), may hold values from -0.125 to 0.125
- out_weight: bfloat16 [3456, 2048], P('tp', 'shard'), may hold values from -0.15625 to 0.15625
- second_gain: float32 [2048], replicated, may hold values from 0.25 to 1.75
- second_bias: float32 [2048], replicated, may hold values from -3 to 3
- mlp_gate: bfloat16 [2048, 3456], P('shard', 'tp'), may hold values from -0.125 to 0.125
- mlp_up: bfloat16 [2048, 3456], P('shard', 'tp'), may hold values from -0.125 to 0.125
- mlp_down: bfloat16 [3456, 2048], P('tp', 'shard'), may hold values from -0.15625 to 0.15625
- upstream: bfloat16 [2, 4096, 2048], P('shard', 'ctx'), may hold values from -6 to 6
Outputs:
- layer_out: bfloat16 [2, 4096, 2048], P('shard', 'ctx')
- tokens_grad: float32 [2, 4096, 2048], P('shard', 'ctx')
- first_gain_grad: float32 [2048], P(('shard', 'ctx'))
- first_bias_grad: float32 [2048], P(('shard', 'ctx'))
- query_weight_grad: float32 [2048, 2048], P(('shard', 'ctx'), 'tp')
- key_weight_grad: float32 [2048, 2048], P(('shard', 'ctx'), 'tp')
- value_weight_grad: float32 [2048, 3456], P(('shard', 'ctx'), 'tp')
- gate_weight_grad: float32 [2048, 3456], P(('shard', 'ctx'), 'tp')
- out_weight_grad: float32 [3456, 2048], P('tp', ('shard', 'ctx'))
- second_gain_grad: float32 [2048], P(('shard', 'ctx'))
- second_bias_grad: float32 [2048], P(('shard', 'ctx'))
- mlp_gate_grad: float32 [2048, 3456], P(('shard', 'ctx'), 'tp')
- mlp_up_grad: float32 [2048, 3456], P(('shard', 'ctx'), 'tp')
- mlp_down_grad: float32 [3456, 2048], P('tp', ('shard', 'ctx'))
Inputs may be any that keep to these rules, and one draw needn't show every extreme that they name: `segments`: segment numbers start at 0 in every sequence and rise by one at the first token of each further document; a sequence holds at most three documents. In each aligned group of 1 sequence one, chosen by the seed, holds three documents: the first of 1 to 64 tokens, the last of 1 to 64 tokens, the middle one all the rest. In the other sequences every document but the last holds at least max(2, 204) tokens.
All inputs are finite; a program needn't handle non-finite values.
Results may differ from a plain program's by a relative error of at most 0.017.
The roundings to bfloat16 on the way count: a program that leaves them out, or rounds other values in their place, can miss the bound.
Values may be sent and summed in bfloat16 or wider, within the bound.
No kernel may reach another device: no remote copies, remote signals or barrier semaphores. Data moves between devices by JAX's collectives and lax.ppermute only.
A program may use at most 320 MiB of HBM per device.

v0:
```python
import jax
import jax.numpy as jnp
from jax import lax
from jax.sharding import PartitionSpec as P

KH = 256
VH = 432


EPS = 1e-05
HIGHEST_ACCURACY = lax.Precision.HIGHEST


def carried_in(value, axis, combine, identity, reverse):
    length, index = (lax.axis_size(axis), lax.axis_index(axis))
    everything = jax.tree.map(lambda part: lax.all_gather(part, axis), value)
    start = jax.tree.map(
        lambda part, zero: jnp.broadcast_to(jnp.asarray(zero, part.dtype), part.shape),
        value,
        identity,
    )

    def turn(k, before):
        at = length - 1 - k if reverse else k
        reached = at > index if reverse else at < index
        new = combine(before, jax.tree.map(lambda part: part[at], everything))
        return jax.tree.map(lambda a, b: jnp.where(reached, a, b), new, before)

    return lax.fori_loop(0, length, turn, start)


def product(left, right):
    return jnp.dot(left, right, preferred_element_type=jnp.float32)


def product_left(left, right):
    return lax.dot_general(
        left, right, (((0,), (0,)), ((), ())), preferred_element_type=jnp.float32
    )


def product_right(left, right):
    return lax.dot_general(
        left, right, (((1,), (1,)), ((), ())), preferred_element_type=jnp.float32
    )


def normalize(values):
    center = values - jnp.mean(values, -1, keepdims=True)
    inverse = lax.rsqrt(jnp.mean(center * center, -1, keepdims=True) + EPS)
    return (center * inverse, inverse)


def normalize_back(grad, normed, inverse):
    return inverse * (
        grad
        - jnp.mean(grad, -1, keepdims=True)
        - normed * jnp.mean(grad * normed, -1, keepdims=True)
    )


def silu_slope(values):
    sigma = jax.nn.sigmoid(values)
    return sigma * (1.0 + values * (1.0 - sigma))


def chain_join(earlier, later):
    earlier_factor, earlier_state, earlier_first, earlier_last = earlier
    later_factor, later_state, later_first, later_last = later
    joined = ((earlier_last == later_first) | (earlier_last < 0.0) | (later_first < 0.0)).astype(
        jnp.float32
    )
    passing = later_factor * joined[:, None]
    return (
        earlier_factor * passing,
        later_state + passing[:, :, None] * earlier_state,
        jnp.where(earlier_first < 0.0, later_first, earlier_first),
        jnp.where(later_last < 0.0, earlier_last, later_last),
    )


def grad_join(earlier, later):
    return (earlier[0] * later[0], later[1] + later[0][:, :, None] * earlier[1])


def body(
    tokens,
    segments,
    decay_rate,
    first_gain,
    first_bias,
    query_weight,
    key_weight,
    value_weight,
    gate_weight,
    out_weight,
    second_gain,
    second_bias,
    mlp_gate,
    mlp_up,
    mlp_down,
    upstream,
):
    seqs_here, piece, width = tokens.shape
    heads = decay_rate.shape[0]
    rows = seqs_here * piece
    full_query, full_key, full_value, full_gate, full_out, full_upgate, full_up, full_down = (
        lax.all_gather(query_weight, "shard", axis=0, tiled=True),
        lax.all_gather(key_weight, "shard", axis=0, tiled=True),
        lax.all_gather(value_weight, "shard", axis=0, tiled=True),
        lax.all_gather(gate_weight, "shard", axis=0, tiled=True),
        lax.all_gather(out_weight, "shard", axis=1, tiled=True),
        lax.all_gather(mlp_gate, "shard", axis=0, tiled=True),
        lax.all_gather(mlp_up, "shard", axis=0, tiled=True),
        lax.all_gather(mlp_down, "shard", axis=1, tiled=True),
    )
    inputs = tokens.reshape(rows, width).astype(jnp.float32)
    normed_first, inverse_first = normalize(inputs)
    lowered_first = (normed_first * first_gain + first_bias).astype(jnp.bfloat16)
    queries = product(lowered_first, full_query).astype(jnp.bfloat16)
    keys_all = product(lowered_first, full_key).astype(jnp.bfloat16)
    values = product(lowered_first, full_value).astype(jnp.bfloat16)
    gate_pre = product(lowered_first, full_gate)
    query_heads = queries.reshape(seqs_here, piece, heads, KH)
    key_heads = keys_all.reshape(seqs_here, piece, heads, KH)
    value_heads = values.reshape(seqs_here, piece, heads, VH)
    place = jnp.arange(piece)
    offset = place[:, None] - place[None, :]
    valid = (offset >= 0)[None] & (segments[:, :, None] == segments[:, None, :])
    decay = jnp.where(
        valid[:, None],
        jnp.exp(
            -decay_rate[None, :, None, None]
            * jnp.maximum(offset, 0).astype(jnp.float32)[None, None]
        ),
        0.0,
    )
    scores = jnp.einsum(
        "sihk,sjhk->shij", query_heads, key_heads, preferred_element_type=jnp.float32
    )
    masked = (scores * decay).astype(jnp.bfloat16)
    inner = jnp.einsum("shij,sjhv->sihv", masked, value_heads, preferred_element_type=jnp.float32)
    tail_portion = (
        jnp.exp(-decay_rate[None, None, :] * (piece - 1 - place).astype(jnp.float32)[None, :, None])
        * (segments == segments[:, -1:]).astype(jnp.float32)[:, :, None]
    )
    key_float = key_heads.astype(jnp.float32)
    value_float = value_heads.astype(jnp.float32)
    query_float = query_heads.astype(jnp.float32)
    key_tail = key_float * tail_portion[..., None]
    local_within = jnp.einsum("sjhk,sjhv->shkv", key_tail, value_float, precision=HIGHEST_ACCURACY)
    carry_factor = (
        jnp.exp(-decay_rate * piece)[None, :]
        * (segments[:, 0] == segments[:, -1]).astype(jnp.float32)[:, None]
    )
    first_id = segments[:, 0].astype(jnp.float32)
    last_id = segments[:, -1].astype(jnp.float32)
    chain_start = (
        jnp.ones_like(carry_factor),
        jnp.zeros((seqs_here, heads, KH * VH), jnp.float32),
        -jnp.ones_like(first_id),
        -jnp.ones_like(first_id),
    )
    _, incoming, _, before_id = carried_in(
        (carry_factor, local_within.reshape(seqs_here, heads, KH * VH), first_id, last_id),
        "ctx",
        chain_join,
        chain_start,
        False,
    )
    incoming = incoming.reshape(seqs_here, heads, KH, VH)
    reach_extent = (
        jnp.exp(-decay_rate[None, None, :] * (place + 1).astype(jnp.float32)[None, :, None])
        * (segments.astype(jnp.float32) == before_id[:, None]).astype(jnp.float32)[:, :, None]
    )
    outer_across = reach_extent[..., None] * jnp.einsum(
        "sihk,shkv->sihv", query_float, incoming, precision=HIGHEST_ACCURACY
    )
    grouped, inverse_group = normalize(inner + outer_across)
    grouped_rows = grouped.reshape(rows, heads * VH)
    gate_act = jax.nn.silu(gate_pre)
    mixed = (gate_act * grouped_rows).astype(jnp.bfloat16)
    middle = inputs + lax.psum(product(mixed, full_out), "tp")
    normed_second, inverse_second = normalize(middle)
    lowered_second = (normed_second * second_gain + second_bias).astype(jnp.bfloat16)
    up_gate = product(lowered_second, full_upgate)
    up_vals = product(lowered_second, full_up)
    silu_gate = jax.nn.silu(up_gate)
    hidden = (silu_gate * up_vals).astype(jnp.bfloat16)
    result = middle + lax.psum(product(hidden, full_down).astype(jnp.bfloat16), "tp").astype(
        jnp.float32
    )
    layer_out = result.astype(jnp.bfloat16).reshape(tokens.shape)
    upstream_rows = upstream.reshape(rows, width)
    grad_down = product_left(hidden, upstream_rows)
    grad_hidden = product_right(upstream_rows, full_down)
    grad_up_gate = (grad_hidden * up_vals * silu_slope(up_gate)).astype(jnp.bfloat16)
    grad_up_vals = (grad_hidden * silu_gate).astype(jnp.bfloat16)
    grad_mlp_gate = product_left(lowered_second, grad_up_gate)
    grad_mlp_up = product_left(lowered_second, grad_up_vals)
    part_second = product_right(grad_up_gate, full_upgate) + product_right(grad_up_vals, full_up)
    grad_lowered_second = lax.psum(part_second, "tp")
    grad_second_gain = jnp.sum(grad_lowered_second * normed_second, 0)
    grad_second_bias = jnp.sum(grad_lowered_second, 0)
    grad_middle = upstream_rows.astype(jnp.float32) + normalize_back(
        grad_lowered_second * second_gain, normed_second, inverse_second
    )
    grad_branch = grad_middle.astype(jnp.bfloat16)
    grad_out = product_left(mixed, grad_branch)
    grad_mixed = product_right(grad_branch, full_out)
    grad_gate_pre = (grad_mixed * grouped_rows * silu_slope(gate_pre)).astype(jnp.bfloat16)
    grad_grouped = (grad_mixed * gate_act).reshape(seqs_here, piece, heads, VH)
    grad_retained = normalize_back(grad_grouped, grouped, inverse_group).astype(jnp.bfloat16)
    grad_masked = jnp.einsum(
        "sihv,sjhv->shij", grad_retained, value_heads, preferred_element_type=jnp.float32
    )
    grad_scores = (grad_masked * decay).astype(jnp.bfloat16)
    grad_query = jnp.einsum(
        "shij,sjhk->sihk", grad_scores, key_heads, preferred_element_type=jnp.float32
    )
    grad_key = jnp.einsum(
        "shij,sihk->sjhk", grad_scores, query_heads, preferred_element_type=jnp.float32
    )
    grad_value = jnp.einsum(
        "shij,sihv->sjhv", masked, grad_retained, preferred_element_type=jnp.float32
    )
    reached = reach_extent[..., None] * grad_retained.astype(jnp.float32)
    grad_query = grad_query + jnp.einsum(
        "sihv,shkv->sihk", reached, incoming, precision=HIGHEST_ACCURACY
    )
    state_term = jnp.einsum("sihk,sihv->shkv", query_float, reached, precision=HIGHEST_ACCURACY)
    linked = (before_id == first_id).astype(jnp.float32)
    back_start = (jnp.ones_like(carry_factor), jnp.zeros((seqs_here, heads, KH * VH), jnp.float32))
    _, grad_outgoing = carried_in(
        (carry_factor * linked[:, None], state_term.reshape(seqs_here, heads, KH * VH)),
        "ctx",
        grad_join,
        back_start,
        True,
    )
    grad_outgoing = grad_outgoing.reshape(seqs_here, heads, KH, VH)
    grad_key = grad_key + tail_portion[..., None] * jnp.einsum(
        "sjhv,shkv->sjhk", value_float, grad_outgoing, precision=HIGHEST_ACCURACY
    )
    grad_value = grad_value + jnp.einsum(
        "sjhk,shkv->sjhv", key_tail, grad_outgoing, precision=HIGHEST_ACCURACY
    )
    grad_query_rows = grad_query.astype(jnp.bfloat16).reshape(rows, heads * KH)
    grad_key_rows = grad_key.astype(jnp.bfloat16).reshape(rows, heads * KH)
    grad_value_rows = grad_value.astype(jnp.bfloat16).reshape(rows, heads * VH)
    grad_query_weight = product_left(lowered_first, grad_query_rows)
    grad_key_weight = product_left(lowered_first, grad_key_rows)
    grad_value_weight = product_left(lowered_first, grad_value_rows)
    grad_gate_weight = product_left(lowered_first, grad_gate_pre)
    part_first = (
        product_right(grad_query_rows, full_query)
        + product_right(grad_key_rows, full_key)
        + product_right(grad_value_rows, full_value)
        + product_right(grad_gate_pre, full_gate)
    )
    grad_lowered_first = lax.psum(part_first, "tp")
    grad_first_gain = jnp.sum(grad_lowered_first * normed_first, 0)
    grad_first_bias = jnp.sum(grad_lowered_first, 0)
    tokens_grad = grad_middle + normalize_back(
        grad_lowered_first * first_gain, normed_first, inverse_first
    )
    summed = (
        lax.psum_scatter(grad_query_weight, ("shard", "ctx"), scatter_dimension=0, tiled=True),
        lax.psum_scatter(grad_key_weight, ("shard", "ctx"), scatter_dimension=0, tiled=True),
        lax.psum_scatter(grad_value_weight, ("shard", "ctx"), scatter_dimension=0, tiled=True),
        lax.psum_scatter(grad_gate_weight, ("shard", "ctx"), scatter_dimension=0, tiled=True),
        lax.psum_scatter(grad_out, ("shard", "ctx"), scatter_dimension=1, tiled=True),
        lax.psum_scatter(grad_mlp_gate, ("shard", "ctx"), scatter_dimension=0, tiled=True),
        lax.psum_scatter(grad_mlp_up, ("shard", "ctx"), scatter_dimension=0, tiled=True),
        lax.psum_scatter(grad_down, ("shard", "ctx"), scatter_dimension=1, tiled=True),
        lax.psum_scatter(grad_first_gain, ("shard", "ctx"), scatter_dimension=0, tiled=True),
        lax.psum_scatter(grad_first_bias, ("shard", "ctx"), scatter_dimension=0, tiled=True),
        lax.psum_scatter(grad_second_gain, ("shard", "ctx"), scatter_dimension=0, tiled=True),
        lax.psum_scatter(grad_second_bias, ("shard", "ctx"), scatter_dimension=0, tiled=True),
    )
    return (
        layer_out,
        tokens_grad.reshape(tokens.shape),
        summed[8],
        summed[9],
        summed[0],
        summed[1],
        summed[2],
        summed[3],
        summed[4],
        summed[10],
        summed[11],
        summed[5],
        summed[6],
        summed[7],
    )


def solution(mesh):
    in_specs = (
        P("shard", "ctx", None),
        P("shard", "ctx"),
        P("tp"),
        P(),
        P(),
        P("shard", "tp"),
        P("shard", "tp"),
        P("shard", "tp"),
        P("shard", "tp"),
        P("tp", "shard"),
        P(),
        P(),
        P("shard", "tp"),
        P("shard", "tp"),
        P("tp", "shard"),
        P("shard", "ctx", None),
    )
    out_specs = (
        P("shard", "ctx", None),
        P("shard", "ctx", None),
        P(("shard", "ctx")),
        P(("shard", "ctx")),
        P(("shard", "ctx"), "tp"),
        P(("shard", "ctx"), "tp"),
        P(("shard", "ctx"), "tp"),
        P(("shard", "ctx"), "tp"),
        P("tp", ("shard", "ctx")),
        P(("shard", "ctx")),
        P(("shard", "ctx")),
        P(("shard", "ctx"), "tp"),
        P(("shard", "ctx"), "tp"),
        P("tp", ("shard", "ctx")),
    )
    return jax.shard_map(body, mesh=mesh, in_specs=in_specs, out_specs=out_specs, check_vma=False)
```

profile of v0, /device:TPU:8, one launch (start us, length us, event | category | flops | bytes accessed | tf_op | source)
XLA Modules:
  0.0 4192.1 jit_solution(2793130392608014847)
XLA Ops:
  14.0 58.8 %all-gather.19.cloned.1.call-done = bf16[2048,1024]{1,0:T(8,128)(2,1)} async-done(((bf16[1024,1024]{1,0:T(8,128)(2,1)}), bf16[2048,1024]{1,0:T(8,128)(2,1)}) %all-gather.19.cloned.1.call-update) | async-done | bytes 4194320 | tf_op jit(solution)/shard_map/all_gather | solution.py:109
  75.8 91.4 %all-gather.15.cloned.1.call-done = bf16[2048,1728]{0,1:T(8,128)(2,1)} async-done(((bf16[1024,1728]{0,1:T(8,128)(2,1)}), bf16[2048,1728]{0,1:T(8,128)(2,1)}) %all-gather.15.cloned.1.call-update) | async-done | bytes 7077904 | tf_op jit(solution)/shard_map/all_gather | solution.py:110
  167.2 5.1 convolution_convert_fusion.1
  173.5 3.1 all_gather_reshape.6
  180.7 58.4 %all-reduce.9 = (f32[128]{0:T(128)S(1)}, f32[32]{0:T(128)S(1)}, f32[32]{0:T(128)S(1)}) all-reduce(f32[128]{0:T(128)S(1)} %get-tuple-element.427, f32[32]{0:T(128)S(1)} %bitcast_dynamic-update-slice_fusion.1, f32[32]{0:T(128)S(1)} %bitcast_dynamic-update-slice_fusion), channel_id=2, replica_groups=mesh['shard'=2,'ctx'=32,'tp'=2] {'ctx'}, use_global_device_ids=true, to_apply=%add | all-reduce | flops 192 | bytes 1536
  239.3 3.7 convolution_convert_fusion.3
  244.6 160.1 %all-gather.21.cloned.1.call-done = f32[32,1,4,110592]{3,2,1,0:T(4,128)} async-done(((f32[1,1,4,110592]{3,2,1,0:T(4,128)}), f32[32,1,4,110592]{3,2,1,0:T(4,128)}) %all-gather.21.cloned.1.call-update) | async-done | bytes 56623120 | tf_op jit(solution)/shard_map/all_gather | solution.py:16
  404.7 174.4 %while.32 = (s32[]{:T(128)}, f32[1,4,110592]{2,1,0:T(4,128)S(1)}, f32[1]{0:T(128)}, s32[]{:T(128)}, f32[32,1,4,110592]{3,2,1,0:T(4,128)}, /*index=5*/f32[32,1,4]...) while((s32[]{:T(128)}, f32[1,4,110592]{2,1,0:T(4,128)S(1)}, ...), condition=%wide.region_3.4_spmd.clone, body=%wide.region_2.3_spmd.clone.sunk | while | flops 1769489 | bytes 5308706 | solution.py:29
  579.1 3.9 reshape.592
  583.1 3.5 fusion.102
  587.6 6.3 fusion.39
  593.9 5.3 fusion.103
  601.9 43.2 %all-reduce.15.cloned.1.call-done = f32[128,2048]{1,0:T(8,128)} async-done(((f32[128,2048]{1,0:T(8,128)}), f32[128,2048]{1,0:T(8,128)}) %all-reduce.15.cloned.1.call-update) | async-done | bytes 1048592 | tf_op jit(solution)/shard_map/psum | solution.py:183
  647.0 94.1 %all-gather.25.cloned.1.call-done = bf16[2048,1728]{0,1:T(8,128)(2,1)} async-done(((bf16[1024,1728]{0,1:T(8,128)(2,1)}), bf16[2048,1728]{0,1:T(8,128)(2,1)}) %all-gather.25.cloned.1.call-update) | async-done | bytes 7077904 | tf_op jit(solution)/shard_map/all_gather | solution.py:113
  741.1 5.9 fusion.104
  747.0 88.6 %all-gather.27.cloned.1.call-done = bf16[2048,1728]{0,1:T(8,128)(2,1)} async-done(((bf16[1024,1728]{0,1:T(8,128)(2,1)}), bf16[2048,1728]{0,1:T(8,128)(2,1)}) %all-gather.27.cloned.1.call-update) | async-done | bytes 7077904 | tf_op jit(solution)/shard_map/all_gather | solution.py:114
  835.6 6.0 fusion.105
  841.5 88.4 %all-gather.29.cloned.1.call-done = bf16[1728,2048]{1,0:T(8,128)(2,1)} async-done(((bf16[1728,1024]{1,0:T(8,128)(2,1)}), bf16[1728,2048]{1,0:T(8,128)(2,1)}) %all-gather.29.cloned.1.call-update) | async-done | bytes 7077904 | tf_op jit(solution)/shard_map/all_gather | solution.py:115
  929.9 5.8 multiply_convert_fusion.1
  935.8 4.7 fusion.106
  943.5 5.0 convolution_convert_fusion
  948.7 41.0 all-reduce.19.cloned.1.call-done
  991.9 36.8 all-reduce.17.cloned.1.call-done
  1031.5 6.8 fusion.79
  1041.2 4.7 all_gather_reshape.7
  1047.8 57.1 %all-reduce.3 = f32[128]{0:T(128)} all-reduce(f32[128]{0:T(128)} %multiply_dynamic-update-slice_fusion), channel_id=3, replica_groups=mesh['shard'=2,'ctx'=32,'tp'=2] {'ctx'}, use_global_device_ids=true, to_apply=%add.3 | all-reduce | flops 128 | bytes 1024
  1115.8 5.5 fusion.109
  1121.3 100.1 %all-gather.31.cloned.1.call-done = f32[32,1,4,110592]{3,2,1,0:T(4,128)} async-done(((f32[1,1,4,110592]{3,2,1,0:T(4,128)}), f32[32,1,4,110592]{3,2,1,0:T(4,128)}) %all-gather.31.cloned.1.call-update) | async-done | bytes 56623120 | tf_op jit(solution)/shard_map/all_gather | solution.py:16
  1221.4 107.9 %while.33 = (s32[]{:T(128)}, f32[1,4,110592]{2,1,0:T(4,128)S(1)}, s32[]{:T(128)}, f32[32,1,4,110592]{3,2,1,0:T(4,128)}, f32[32,1,4]{2,1,0:T(1,128)}, /*index=5*/s32[]{:T(128)}, s32[]{:T(128)}, s32[]{:T(128)}, s32[]{:T(128)}) while((s32[]{:T(128)}, f32[1,4,110592]{2,1,0:T(4,128)S(1)}, s32[]{:T(128)}, ...), condition=%wide.region_16.17_spmd.clone, body=%wide.region_15.16_spmd.clone.sunk | while | flops 1769480 | bytes 5308639 | solution.py:29
  1329.4 3.8 reshape.600
  1336.0 4.8 fusion.10
  1341.2 4.3 fusion.108
  1348.5 4.7 fusion.89
  1354.2 7.3 fusion.110
  1362.5 7.2 fusion.111
  1371.0 7.3 fusion.46
  1379.3 7.3 fusion.91
  1388.0 7.2 fusion.65
  1395.3 4.6 fusion.87
  1400.1 7.4 fusion.85
  1411.1 301.3 %all-reduce.8 = (f32[2048]{0:T(1024)S(1)}, f32[2048]{0:T(1024)S(1)}, f32[2048]{0:T(1024)S(1)}, f32[2048]{0:T(1024)S(1)}) all-reduce(f32[2048]{0:T(1024)S(1)} %get-tuple-element.375, f32[2048]{0:T(1024)S(1)} %get-tuple-element.380, f32[2048]{0:T(1024)S(1)} %get-tuple-element.373, ...), channel_id=4, replica_groups=mesh['shard'=2,'ctx'=32,'tp'=2] {'shard','ctx'}, use_global_device_ids=true, to_apply=%region_21.22.clone | all-reduce | flops 8192 | bytes 65536
  1717.4 352.9 %reduce-scatter.19.cloned.1.call-done = f32[32,1728]{1,0:T(8,128)} async-done(((f32[2048,1728]{1,0:T(8,128)}), f32[32,1728]{1,0:T(8,128)}) %reduce-scatter.19.cloned.1.call-update) | async-done | bytes 221200 | tf_op jit(solution)/shard_map/reduce_scatter | solution.py:273
  2070.3 354.1 %reduce-scatter.21.cloned.1.call-done = f32[32,1728]{1,0:T(8,128)} async-done(((f32[2048,1728]{1,0:T(8,128)}), f32[32,1728]{1,0:T(8,128)}) %reduce-scatter.21.cloned.1.call-update) | async-done | bytes 221200 | tf_op jit(solution)/shard_map/reduce_scatter | solution.py:274
  2424.4 354.1 %reduce-scatter.23.cloned.1.call-done = f32[1728,32]{0,1:T(8,128)} async-done(((f32[1728,2048]{0,1:T(8,128)}), f32[1728,32]{0,1:T(8,128)}) %reduce-scatter.23.cloned.1.call-update) | async-done | bytes 221200 | tf_op jit(solution)/shard_map/reduce_scatter | solution.py:275
  2778.5 354.3 %reduce-scatter.15.cloned.1.call-done = f32[32,1728]{1,0:T(8,128)} async-done(((f32[2048,1728]{1,0:T(8,128)}), f32[32,1728]{1,0:T(8,128)}) %reduce-scatter.15.cloned.1.call-update) | async-done | bytes 221200 | tf_op jit(solution)/shard_map/reduce_scatter | solution.py:271
  3132.8 354.1 %reduce-scatter.17.cloned.1.call-done = f32[1728,32]{0,1:T(8,128)} async-done(((f32[1728,2048]{0,1:T(8,128)}), f32[1728,32]{0,1:T(8,128)}) %reduce-scatter.17.cloned.1.call-update) | async-done | bytes 221200 | tf_op jit(solution)/shard_map/reduce_scatter | solution.py:272
  3486.9 344.4 %reduce-scatter.11.cloned.1.call-done = f32[32,1024]{1,0:T(8,128)} async-done(((f32[2048,1024]{1,0:T(8,128)}), f32[32,1024]{1,0:T(8,128)}) %reduce-scatter.11.cloned.1.call-update) | async-done | bytes 131088 | tf_op jit(solution)/shard_map/reduce_scatter | solution.py:269
  3831.3 353.8 %reduce-scatter.13.cloned.1.call-done = f32[32,1728]{1,0:T(8,128)} async-done(((f32[2048,1728]{1,0:T(8,128)}), f32[32,1728]{1,0:T(8,128)}) %reduce-scatter.13.cloned.1.call-update) | async-done | bytes 221200 | tf_op jit(solution)/shard_map/reduce_scatter | solution.py:270
  (372 shorter events, 259.2 us)
Async XLA Ops:
  7.2 5.5 copy-start.1
  7.2 6.6 copy-start.46
  7.2 65.6 %copy-start.31 = (f32[2048]{0:T(1024)S(1)}, f32[2048]{0:T(1024)}, u32[]{:S(2)}) copy-start(f32[2048]{0:T(1024)} %param.23) | copy-start | bytes 24580
  7.2 65.6 %copy-start.33 = (f32[2048]{0:T(1024)S(1)}, f32[2048]{0:T(1024)}, u32[]{:S(2)}) copy-start(f32[2048]{0:T(1024)} %param.24) | copy-start | bytes 24580
  7.2 65.6 %all-gather.19.cloned.1.call-start = ((), (), s32[]{:S(2)}) async-start(), calls=%async_computation.11 | async-start | bytes 6291456 | tf_op jit(solution)/shard_map/all_gather | solution.py:109
  8.0 159.2 %all-gather.15.cloned.1.call-start = ((), (), s32[]{:S(2)}) async-start(), calls=%async_computation.9 | async-start | bytes 10616832 | tf_op jit(solution)/shard_map/all_gather | solution.py:110
  8.7 230.6 %all-gather.17.cloned.1.call-start = ((), (), s32[]{:S(2)}) async-start(), calls=%async_computation.10 | async-start | bytes 6291456 | tf_op jit(solution)/shard_map/all_gather | solution.py:108
  9.5 395.2 %all-gather.21.cloned.1.call-start = ((), (), s32[]{:S(2)}) async-start(), calls=%async_computation.12 | async-start | bytes 58392576 | tf_op jit(solution)/shard_map/all_gather | solution.py:16
  13.9 569.1 %copy-start.45 = (f32[4]{0:T(128)}, f32[4]{0:T(128)S(1)}, u32[]{:S(2)}) copy-start(f32[4]{0:T(128)S(1)} %get-tuple-element.428) | copy-start | bytes 52
  14.0 158.3 %copy-start.40 = (f32[128,4]{0,1:T(4,128)}, f32[128,4]{0,1:T(4,128)S(1)}, u32[]{:S(2)}) copy-start(f32[128,4]{0,1:T(4,128)S(1)} %exponential_multiply_fusion) | copy-start | bytes 6148
  172.3 70.9 %copy-start.12 = (bf16[128,1728]{0,1:T(8,128)(2,1)}, bf16[128,1728]{0,1:T(8,128)(2,1)S(1)}, u32[]{:S(2)}) copy-start(bf16[128,1728]{0,1:T(8,128)(2,1)S(1)} %convolution_convert_fusion.1) | copy-start | bytes 1327108
  176.6 410.9 %all-gather.13.cloned.1.call-start = ((), (), s32[]{:S(2)}) async-start(), calls=%async_computation.8 | async-start | bytes 10616832 | tf_op jit(solution)/shard_map/all_gather | solution.py:111
  177.2 416.7 %all-gather.23.cloned.1.call-start = ((), (), s32[]{:S(2)}) async-start(), calls=%async_computation.13 | async-start | bytes 10616832 | tf_op jit(solution)/shard_map/all_gather | solution.py:112
  177.8 467.3 %all-reduce.15.cloned.1.call-start = ((), (), s32[]{:S(2)}) async-start(), calls=%async_computation.14 | async-start | bytes 2097152 | tf_op jit(solution)/shard_map/psum | solution.py:183
  177.9 226.8 %copy-start.38 = (f32[128,128]{1,0:T(8,128)}, f32[128,128]{1,0:T(8,128)S(1)}, u32[]{:S(2)}) copy-start(f32[128,128]{1,0:T(8,128)S(1)} %maximum_convert_fusion) | copy-start | bytes 196612
  179.3 225.3 %copy-start.42 = (pred[128,128]{1,0:T(8,128)(4,1)}, pred[128,128]{1,0:T(8,128)(4,1)S(1)}, u32[]{:S(2)}) copy-start(pred[128,128]{1,0:T(8,128)(4,1)S(1)} %fusion.81) | copy-start | bytes 49156
  243.0 161.7 %copy-start.25 = (bf16[128,1024]{1,0:T(8,128)(2,1)}, bf16[128,1024]{1,0:T(8,128)(2,1)S(1)}, u32[]{:S(2)}) copy-start(bf16[128,1024]{1,0:T(8,128)(2,1)S(1)} %convolution_convert_fusion.3) | copy-start | bytes 786436
  243.2 161.4 %copy-start.34 = (bf16[4,128,128]{2,1,0:T(8,128)(2,1)}, bf16[4,128,128]{2,1,0:T(8,128)(2,1)S(1)}, u32[]{:S(2)}) copy-start(bf16[4,128,128]{2,1,0:T(8,128)(2,1)S(1)} %fusion.21) | copy-start | bytes 393220
  583.1 455.7 %copy-start.41 = (f32[128,4]{0,1:T(4,128)}, f32[128,4]{0,1:T(4,128)S(1)}, u32[]{:S(2)}) copy-start(f32[128,4]{0,1:T(4,128)S(1)} %exponential_multiply_fusion.1) | copy-start | bytes 6148
  587.5 6.4 copy-start.32
  593.9 5.3 copy-start.15
  599.2 141.9 %all-gather.25.cloned.1.call-start = ((), (), s32[]{:S(2)}) async-start(), calls=%async_computation.15 | async-start | bytes 10616832 | tf_op jit(solution)/shard_map/all_gather | solution.py:113
  600.0 235.6 %all-gather.27.cloned.1.call-start = ((), (), s32[]{:S(2)}) async-start(), calls=%async_computation.16 | async-start | bytes 10616832 | tf_op jit(solution)/shard_map/all_gather | solution.py:114
  600.7 46.0 %copy-start.37 = (f32[2048]{0:T(1024)S(1)}, f32[2048]{0:T(1024)}, u32[]{:S(2)}) copy-start(f32[2048]{0:T(1024)} %param.30) | copy-start | bytes 24580
  600.7 46.0 %copy-start.43 = (f32[2048]{0:T(1024)S(1)}, f32[2048]{0:T(1024)}, u32[]{:S(2)}) copy-start(f32[2048]{0:T(1024)} %param.31) | copy-start | bytes 24580
  600.7 329.2 %all-gather.29.cloned.1.call-start = ((), (), s32[]{:S(2)}) async-start(), calls=%async_computation.17 | async-start | bytes 10616832 | tf_op jit(solution)/shard_map/all_gather | solution.py:115
  601.3 388.3 %all-reduce.19.cloned.1.call-start = ((), (), s32[]{:S(2)}) async-start(), calls=%async_computation.19 | async-start | bytes 2097152 | tf_op jit(solution)/shard_map/psum | solution.py:202
  935.8 7.7 copy-start.17
  935.8 5.5 copy-start
  943.4 85.3 %all-reduce.17.cloned.1.call-start = ((), (), s32[]{:S(2)}) async-start(), calls=%async_computation.18 | async-start | bytes 1048576 | tf_op jit(solution)/shard_map/psum | solution.py:190
  948.4 272.9 %all-gather.31.cloned.1.call-start = ((), (), s32[]{:S(2)}) async-start(), calls=%async_computation.20 | async-start | bytes 58392576 | tf_op jit(solution)/shard_map/all_gather | solution.py:16
  1031.5 6.9 copy-start.6
  1031.5 6.9 copy-start.3
  1031.5 7.3 copy-start.26
  1045.9 363.5 %all-reduce.21.cloned.1.call-start = ((), (), s32[]{:S(2)}) async-start(), calls=%async_computation.21 | async-start | bytes 2097152 | tf_op jit(solution)/shard_map/psum | solution.py:261
  1106.2 7.1 copy-start.10
  1107.8 5.5 copy-start.35
  1221.4 111.7 %copy-start.13 = (bf16[128,1728]{0,1:T(8,128)(2,1)S(1)}, bf16[128,1728]{0,1:T(8,128)(2,1)}, u32[]{:S(2)}) copy-start(bf16[128,1728]{0,1:T(8,128)(2,1)} %copy-done.12) | copy-start | bytes 1327108
  1333.1 7.7 copy-start.27
  1333.1 7.7 copy-start.36
  1348.5 368.9 %reduce-scatter.9.cloned.1.call-start = ((), (), s32[]{:S(2)}) async-start(), calls=%async_computation.22 | async-start | bytes 8519680 | tf_op jit(solution)/shard_map/reduce_scatter | solution.py:268
  1353.2 717.1 %reduce-scatter.19.cloned.1.call-start = ((), (), s32[]{:S(2)}) async-start(), calls=%async_computation.27 | async-start | bytes 14909440 | tf_op jit(solution)/shard_map/reduce_scatter | solution.py:273
  1361.5 1062.9 %reduce-scatter.21.cloned.1.call-start = ((), (), s32[]{:S(2)}) async-start(), calls=%async_computation.28 | async-start | bytes 14909440 | tf_op jit(solution)/shard_map/reduce_scatter | solution.py:274
  1369.8 1408.7 %reduce-scatter.23.cloned.1.call-start = ((), (), s32[]{:S(2)}) async-start(), calls=%async_computation.29 | async-start | bytes 14909440 | tf_op jit(solution)/shard_map/reduce_scatter | solution.py:275
  1378.3 1754.5 %reduce-scatter.15.cloned.1.call-start = ((), (), s32[]{:S(2)}) async-start(), calls=%async_computation.25 | async-start | bytes 14909440 | tf_op jit(solution)/shard_map/reduce_scatter | solution.py:271
  1386.7 2100.3 %reduce-scatter.17.cloned.1.call-start = ((), (), s32[]{:S(2)}) async-start(), calls=%async_computation.26 | async-start | bytes 14909440 | tf_op jit(solution)/shard_map/reduce_scatter | solution.py:272
  1395.2 2436.1 %reduce-scatter.11.cloned.1.call-start = ((), (), s32[]{:S(2)}) async-start(), calls=%async_computation.23 | async-start | bytes 8519680 | tf_op jit(solution)/shard_map/reduce_scatter | solution.py:269
  1399.9 2785.2 %reduce-scatter.13.cloned.1.call-start = ((), (), s32[]{:S(2)}) async-start(), calls=%async_computation.24 | async-start | bytes 14909440 | tf_op jit(solution)/shard_map/reduce_scatter | solution.py:270
  (23 other events, 64.1 us)
Sparse Core Ops, SparseCore 0:
  9.7 63.0 all-gather.18
  74.5 92.6 all-gather.14
  168.9 60.2 all-gather.16
  231.2 173.3 all-gather.20
  406.1 92.2 all-gather.12
  499.9 92.6 all-gather.22
  599.3 45.6 all-reduce.14
  646.8 94.2 all-gather.24
  742.8 92.6 all-gather.26
  837.2 92.6 all-gather.28
  943.5 46.0 all-reduce.18
  992.5 36.1 all-reduce.16
  1046.0 175.3 all-gather.30
  1348.6 45.5 all-reduce.20
  1397.0 319.7 reduce-scatter.8
  1719.6 350.6 reduce-scatter.18
  2073.1 351.2 reduce-scatter.20
  2427.3 351.2 reduce-scatter.22
  2781.5 351.2 reduce-scatter.14
  3135.6 351.2 reduce-scatter.16
  3489.9 341.3 reduce-scatter.10
  3834.3 350.7 reduce-scatter.12
where the time goes:
time: 4230 us; the launch traced here: 4190 us
  waiting for transfers between devices  3280 us (78%)
  blocking collectives  417 us (10%)
  other arithmetic  155 us (4%)
  matrix products  151 us (4%)
  local copies, waits for them, and re-layouts  86.8 us (2%)
  loops' own time  85.7 us (2%)
    unnamed x3, blocking collectives  417 us
    reduce_scatter x1, waiting for transfers between devices, body(): lax.psum_scatter(grad_gate_weight, ('shard', 'ctx'), scatter_dimension=0,...  354 us
    reduce_scatter x1, waiting for transfers between devices, body(): lax.psum_scatter(grad_down, ('shard', 'ctx'), scatter_dimension=1, tiled=...  354 us
    reduce_scatter x1, waiting for transfers between devices, body(): lax.psum_scatter(grad_mlp_up, ('shard', 'ctx'), scatter_dimension=0, tile...  354 us
    reduce_scatter x1, waiting for transfers between devices, body(): lax.psum_scatter(grad_out, ('shard', 'ctx'), scatter_dimension=1, tiled=T...  354 us
    reduce_scatter x1, waiting for transfers between devices, body(): lax.psum_scatter(grad_value_weight, ('shard', 'ctx'), scatter_dimension=0...  354 us
    reduce_scatter x1, waiting for transfers between devices, body(): lax.psum_scatter(grad_mlp_gate, ('shard', 'ctx'), scatter_dimension=0, ti...  353 us
    reduce_scatter x1, waiting for transfers between devices, body(): lax.psum_scatter(grad_key_weight, ('shard', 'ctx'), scatter_dimension=0,...  344 us
  transfers between devices with their start and end apart: 22, of which 17 were waited for; matrix products, arithmetic and copies ran while one was open for 5% of the time, Pallas kernels for 0%

commit v1 on v0

v1 whole, which is shorter than its diff:
```python
import functools

import jax
import jax.numpy as jnp
from jax import lax
from jax.experimental import pallas as pl
from jax.experimental.pallas import tpu as pltpu
from jax.sharding import PartitionSpec as P

KH = 256
VH = 432
EPS = 1e-05
BF = jnp.bfloat16
F32 = jnp.float32
F16 = jnp.float16
NC = 32
BLOCK = 32
HALF = 1024
VW = 1728
VPAD = 1792
HEADS = 4
PIECE = 128
QKV = 2 * HALF + VW
GATHERED = 3
PACKED = GATHERED * VPAD
WIDE = 2048

SWAP = [(0, 1), (1, 0)]
CORE = [(index, index ^ 1) for index in range(NC)]
SHARD_TP = [(0, 3), (1, 2), (2, 1), (3, 0)]
SHARD_CORE = [(index, (index ^ 1) ^ NC) for index in range(2 * NC)]
PLANE = [[2 * chip + core for chip in range(16)] for core in range(2)]
ANY = pl.BlockSpec(memory_space=pl.ANY)
SMEM = pl.BlockSpec(memory_space=pltpu.SMEM)


def product(left, right):
    return jnp.dot(left, right, preferred_element_type=F32)


def product_left(left, right):
    return lax.dot_general(left, right, (((0,), (0,)), ((), ())), preferred_element_type=F32)


def product_right(left, right):
    return lax.dot_general(left, right, (((1,), (1,)), ((), ())), preferred_element_type=F32)


def from_shard(part):
    return lax.ppermute(part, "shard", SWAP)


def half_from_shard(part):
    return lax.ppermute(part.astype(F16), "shard", SWAP).astype(F32)


def from_tp(part):
    return lax.ppermute(part, "tp", SWAP)


def core_swap(part):
    return lax.ppermute(part, "ctx", CORE)


def shape(*dims, kind=BF):
    return jax.ShapeDtypeStruct(dims, kind)


def whole(array):
    return pl.BlockSpec(array.shape, lambda i, rank=len(array.shape): (0,) * rank)


def run(kernel, outs, scalars, blocks, far=(), scratch=(), flops=0):
    single = not isinstance(outs, tuple)
    outs = (outs,) if single else outs
    got = pl.pallas_call(
        kernel,
        out_shape=outs,
        grid=(1,),
        in_specs=[SMEM] * len(scalars) + [whole(a) for a in blocks] + [ANY] * len(far),
        out_specs=tuple(whole(a) for a in outs),
        scratch_shapes=list(scratch),
        compiler_params=pltpu.CompilerParams(vmem_limit_bytes=56 * 1024 * 1024),
        cost_estimate=pl.CostEstimate(flops=flops, bytes_accessed=0, transcendentals=0),
    )(*scalars, *blocks, *far)
    return got[0] if single else got


def hold(arrays, *others):
    count = len(arrays)
    return pl.pallas_call(
        lambda *refs: None,
        out_shape=tuple(shape(*a.shape, kind=a.dtype) for a in arrays),
        in_specs=[ANY] * (count + len(others)),
        out_specs=(ANY,) * count,
        input_output_aliases={k: k for k in range(count)},
        cost_estimate=pl.CostEstimate(flops=0, bytes_accessed=0, transcendentals=0),
    )(*arrays, *others)


def after(array, *others):
    return hold((array,), *others)[0]


def fetch(sources, holders, semaphores):
    copies = [pltpu.make_async_copy(src, dst, semaphores.at[k]) for k, (src, dst) in enumerate(zip(sources, holders))]
    for copy in copies:
        copy.start()
    return copies


def part_of(others, k):
    return others.at[:, k * VPAD : (k + 1) * VPAD]


def own_first(shard, array):
    a, b = array[:, :HALF], array[:, HALF:]
    return jnp.where(shard == 0, a, b), jnp.where(shard == 0, b, a)


def normed_of(own, oth):
    mean = (jnp.sum(own, 1, keepdims=True) + jnp.sum(oth, 1, keepdims=True)) / WIDE
    own, oth = own - mean, oth - mean
    var = (jnp.sum(own * own, 1, keepdims=True) + jnp.sum(oth * oth, 1, keepdims=True)) / WIDE
    inverse = lax.rsqrt(var + EPS)
    return own * inverse, oth * inverse, inverse


def norm_back(grads, gains, normed, inverse):
    grads = [grad * gain for grad, gain in zip(grads, gains)]
    mean = sum(jnp.sum(g, 1, keepdims=True) for g in grads) / WIDE
    slant = sum(jnp.sum(g * n, 1, keepdims=True) for g, n in zip(grads, normed)) / WIDE
    return [inverse * (g - mean - n * slant) for g, n in zip(grads, normed)]


def first_kernel(place, shard, tokens, gain, bias, *refs):
    weights, (normed, inverse, low_own, low_oth, packed, columns, semaphores) = refs[:GATHERED], refs[GATHERED:]
    begin = pl.multiple_of(place[0] // 4 * 128, 128)
    copies = fetch([w.at[:, pl.ds(begin, 128)] for w in weights], [columns.at[k] for k in range(GATHERED)], semaphores)
    own, oth = own_first(shard[0], tokens[...].astype(F32))
    own, oth, scale = normed_of(own, oth)
    gains, biases = own_first(shard[0], gain[...]), own_first(shard[0], bias[...])
    normed[:, :HALF] = own
    normed[:, HALF:] = oth
    inverse[...] = jnp.broadcast_to(scale, inverse.shape)
    low_own[...] = (own * gains[0] + biases[0]).astype(BF)
    low_oth[...] = (oth * gains[1] + biases[1]).astype(BF)
    packed[...] = jnp.zeros_like(packed)
    column = lax.broadcasted_iota(jnp.int32, (BLOCK, 128), 1)
    wanted = lax.broadcasted_iota(jnp.int32, (BLOCK, 128), 0) + (place[0] % 4) * BLOCK
    chosen = (column == wanted).astype(F32).astype(BF)
    for k in range(GATHERED):
        copies[k].wait()
        packed[:, k * VPAD : k * VPAD + VW] = product_right(chosen, columns[k]).astype(BF)


def turn_kernel(shard, array, own, oth):
    own[...], oth[...] = own_first(shard[0], array[...])


def help_kernel(low, key_weight, value_weight, key, value):
    key[...] = product(low[...], key_weight[...])
    value[...] = product_right(low[...], value_weight[...])


def help_more_kernel(low, query_weight, gate_weight, query, gate):
    query[...] = product(low[...], query_weight[...])
    gate[...] = product_right(low[...], gate_weight[...])


def base_kernel(low, query_weight, key_weight, value_weight, gate_weight, _, query, key, value, gate):
    query[...] = product(low[...], query_weight[...])
    key[...] = product(low[...], key_weight[...])
    value[...] = product_right(low[...], value_weight[...])
    gate[...] = product_right(low[...], gate_weight[...])


def hidden_kernel(own, theirs, weight, base, helped):
    both = jnp.concatenate([own[...], theirs[...]], 0)
    total = product_right(both, weight[...])
    base[...] = total[:PIECE]
    helped[...] = total[PIECE:]


def window(head):
    begin = head * VH // 128 * 128
    end = -(-(head + 1) * VH // 128) * 128
    return begin, end


def inside(head, rows):
    begin, end = window(head)
    column = lax.broadcasted_iota(jnp.int32, (rows, end - begin), 1) + begin
    return (column >= head * VH) & (column < (head + 1) * VH)


def head_part(ref, head, rows):
    begin, end = window(head)
    return jnp.where(inside(head, rows), ref[:, begin:end].astype(F32), 0.0)


def decay_of(rate, seg_column, seg_row):
    down = lax.broadcasted_iota(jnp.int32, (PIECE, PIECE), 0) - lax.broadcasted_iota(jnp.int32, (PIECE, PIECE), 1)
    near = jnp.exp(-rate * jnp.maximum(down, 0).astype(F32))
    return jnp.where((down >= 0) & (seg_column == seg_row), near, 0.0)


def tail_of(rate, seg_column, seg_row):
    left = (PIECE - 1 - lax.broadcasted_iota(jnp.int32, (PIECE, 1), 0)).astype(F32)
    return jnp.where(seg_column == seg_row[:, PIECE - 1 :], jnp.exp(-rate * left), 0.0)


def reach_of(rate, seg_column, before):
    passed = (lax.broadcasted_iota(jnp.int32, (PIECE, 1), 0) + 1).astype(F32)
    return jnp.where(seg_column == before, jnp.exp(-rate * passed), 0.0)


def with_marks(total, seg_row):
    column = lax.broadcasted_iota(jnp.int32, total.shape, 1)
    marked = jnp.where(column == VW, seg_row[:, :1], jnp.where(column == VW + 1, seg_row[:, PIECE - 1 :], 0.0))
    return jnp.where(column < VW, total, marked).astype(BF)


def mark(states, offset):
    column = lax.broadcasted_iota(jnp.int32, (states.shape[0], 128), 1)
    return jnp.sum(jnp.where(column == VW - (VPAD - 128) + offset, states[:, VPAD - 128 :], 0.0), 1, keepdims=True)


def local_kernel(rates, seg_column, seg_row, base_key, base_value, helped_key, helped_value, _, keys, values, local, total):
    keys[...] = (base_key[...] + helped_key[...].astype(F32)).astype(BF)
    values[:, :VW] = (base_value[...] + helped_value[...].astype(F32)).astype(BF)
    values[:, VW:] = jnp.zeros((PIECE, VPAD - VW), BF)
    total[...] = jnp.zeros_like(total)
    for head in range(HEADS):
        begin, end = window(head)
        own = slice(head * KH, (head + 1) * KH)
        value = head_part(values, head, PIECE).astype(BF)
        key_tail = (keys[:, own].astype(F32) * tail_of(rates[head], seg_column[...], seg_row[...])).astype(BF)
        total[:, begin:end] += product_left(key_tail, value)
    local[...] = with_marks(total[...], seg_row[...])


def inner_kernel(rates, seg_column, seg_row, base_query, helped_query, keys, values, queries, inner, masked):
    queries[...] = (base_query[...] + helped_query[...].astype(F32)).astype(BF)
    inner[...] = jnp.zeros_like(inner)
    for head in range(HEADS):
        begin, end = window(head)
        own = slice(head * KH, (head + 1) * KH)
        scores = product_right(queries[:, own], keys[:, own])
        kept = (scores * decay_of(rates[head], seg_column[...], seg_row[...])).astype(BF)
        masked[head] = kept
        inner[:, begin:end] += product(kept, head_part(values, head, PIECE).astype(BF))


def scan_kernel(reverse, rates, states, *refs):
    out = refs[-1]
    column = lax.broadcasted_iota(jnp.int32, (8, VPAD), 1)
    rate = jnp.full((8, VPAD), rates[HEADS - 1], F32)
    for head in range(HEADS - 1):
        rate = jnp.where((column >= head * VH) & (column < (head + 1) * VH), rates[head], rate)
    factor = jnp.exp(-rate * PIECE)
    edges = [states[p, :, VPAD - 128 :].astype(F32) for p in range(NC)]

    def mark_of(p, offset):
        lane = lax.broadcasted_iota(jnp.int32, (8, 128), 1)
        return jnp.sum(jnp.where(lane == VW - (VPAD - 128) + offset, edges[p], 0.0), 1, keepdims=True)

    firsts = [mark_of(p, 0) for p in range(NC)]
    lasts = [mark_of(p, 1) for p in range(NC)]
    befores = [jnp.full((8, 1), -1.0, F32)] + lasts[:-1]
    carry = jnp.zeros((8, VPAD), F32)
    for k in range(NC):
        p = NC - 1 - k if reverse else k
        out[p] = jnp.where(column < VW, carry, befores[p]).astype(BF)
        keep = jnp.where((firsts[p] == lasts[p]) & (firsts[p] == befores[p]), factor, 0.0)
        carry = states[p].astype(F32) + keep * carry


def mix_kernel(
    rates, seg_column, queries, inner, incoming, base_gate, helped_gate, out_weight, others, _,
    gate, grouped, inverse, mixed, part, total, held, near, semaphores,
):
    copies = fetch([out_weight, part_of(others, 2)], [near, held], semaphores)
    gate[...] = base_gate[...] + helped_gate[...].astype(F32)
    before = mark(incoming[:16].astype(F32), 0)[:1]
    total[...] = inner[...]
    for head in range(HEADS):
        begin, end = window(head)
        own = slice(head * KH, (head + 1) * KH)
        across = product(queries[:, own], incoming[:, begin:end])
        total[:, begin:end] += jnp.where(
            inside(head, PIECE), reach_of(rates[head], seg_column[...], before) * across, 0.0
        )
    lane = lax.broadcasted_iota(jnp.int32, (PIECE, 128), 1)
    scales = jnp.zeros((PIECE, 128), F32)
    grouped[...] = jnp.zeros_like(grouped)
    for head in range(HEADS):
        begin, end = window(head)
        here = inside(head, PIECE)
        retained = jnp.where(here, total[:, begin:end], 0.0)
        center = jnp.where(here, retained - jnp.sum(retained, 1, keepdims=True) / VH, 0.0)
        scale = lax.rsqrt(jnp.sum(center * center, 1, keepdims=True) / VH + EPS)
        grouped[:, begin:end] += center * scale
        scales = jnp.where(lane == head, scale, scales)
    inverse[...] = scales
    mixed[:, :VW] = (jax.nn.silu(gate[...]) * grouped[:, :VW]).astype(BF)
    mixed[:, VW:] = jnp.zeros((PIECE, VPAD - VW), BF)
    copies[0].wait()
    part[:, :HALF] = product(mixed[:, :VW], near[...]).astype(BF)
    copies[1].wait()
    part[:, HALF:] = product_right(mixed[...], held[...]).astype(BF)


def mlp_kernel(
    shard, tokens, mine, theirs, gain, bias, base_hidden, helped_hidden, mixed, gate_weight, up_weight, others, _up, _low,
    middle, normed, inverse, low_own, low_oth, grads, part,
    near_gate, near_up, far_gate, far_up, semaphores,
):
    copies = fetch(
        [gate_weight, part_of(others, 0), up_weight, part_of(others, 1)],
        [near_gate, far_gate, near_up, far_up],
        semaphores,
    )
    own, oth = own_first(shard[0], tokens[...].astype(F32))
    own = own + (mine[:, :HALF].astype(F32) + theirs[:, :HALF].astype(F32))
    oth = oth + (mine[:, HALF:].astype(F32) + theirs[:, HALF:].astype(F32))
    middle[:, :HALF] = own
    middle[:, HALF:] = oth
    own, oth, scale = normed_of(own, oth)
    gains, biases = own_first(shard[0], gain[...]), own_first(shard[0], bias[...])
    normed[:, :HALF] = own
    normed[:, HALF:] = oth
    inverse[...] = jnp.broadcast_to(scale, inverse.shape)
    low_own[...] = (own * gains[0] + biases[0]).astype(BF)
    low_oth[...] = (oth * gains[1] + biases[1]).astype(BF)
    copies[0].wait()
    up_gate = product_right(low_own[...], near_gate[...])
    copies[1].wait()
    up_gate += product(low_oth[...], far_gate[:, :VW])
    copies[2].wait()
    up_vals = product_right(low_own[...], near_up[...])
    copies[3].wait()
    up_vals += product(low_oth[...], far_up[:, :VW])
    grad_hidden = base_hidden[...] + helped_hidden[...].astype(F32)
    sigma = jax.nn.sigmoid(up_gate)
    silu = up_gate * sigma
    none = jnp.zeros((PIECE, VPAD - VW), BF)
    for k, array in enumerate(
        (silu * up_vals, grad_hidden * up_vals * (sigma * (1.0 + up_gate * (1.0 - sigma))), grad_hidden * silu)
    ):
        grads[:, k * VPAD : k * VPAD + VW] = array.astype(BF)
        grads[:, k * VPAD + VW : (k + 1) * VPAD] = none
    grads[:, 3 * VPAD :] = mixed[...]
    total = product(grads[:, VPAD : VPAD + VW], near_gate[...])
    total += product(grads[:, 2 * VPAD : 2 * VPAD + VW], near_up[...])
    part[:, :HALF] = total.astype(BF)
    total = product_right(grads[:, VPAD : 2 * VPAD], far_gate[...])
    total += product_right(grads[:, 2 * VPAD : 3 * VPAD], far_up[...])
    part[:, HALF:] = total.astype(BF)


def down_kernel(own, theirs, weight, part):
    both = jnp.concatenate([own[:, :VW], theirs[:, :VW]], 0)
    part[...] = product(both, weight[...]).astype(BF)


def down_sum_kernel(mine, theirs, own, gone):
    own[...] = mine[:PIECE].astype(F32) + theirs[:PIECE].astype(F32)
    gone[...] = (mine[PIECE:].astype(F32) + theirs[PIECE:].astype(F32)).astype(BF)


def result_kernel(shard, middle, own, oth, out):
    total = [middle[:, :HALF] + own[...], middle[:, HALF:] + oth[...].astype(F32)]
    out[:, :HALF] = jnp.where(shard[0] == 0, total[0], total[1]).astype(BF)
    out[:, HALF:] = jnp.where(shard[0] == 0, total[1], total[0]).astype(BF)


def unmix_kernel(
    shard, rates, mine, theirs, normed, inverse, gain, up_own, up_oth, seg_column, seg_row, queries, incoming, gate,
    grouped, scales, out_weight, others,
    grad_middle, branch_own, branch_oth, vectors, grad_gate, grad_retained, term,
    held, total, near, far, semaphores,
):
    copies = fetch([out_weight, part_of(others, 2)], [near, far], semaphores)
    grads = [mine[:, cut].astype(F32) + theirs[:, cut].astype(F32) for cut in (slice(0, HALF), slice(HALF, WIDE))]
    norms = [normed[:, :HALF], normed[:, HALF:]]
    vectors[...] = jnp.zeros_like(vectors)
    for k in range(2):
        cut = slice(k * HALF, (k + 1) * HALF)
        vectors[0:1, cut] = jnp.sum(grads[k] * norms[k], 0, keepdims=True)
        vectors[1:2, cut] = jnp.sum(grads[k], 0, keepdims=True)
    back = norm_back(grads, own_first(shard[0], gain[...]), norms, inverse[:, :1])
    own, oth = up_own[...].astype(F32) + back[0], up_oth[...].astype(F32) + back[1]
    grad_middle[:, :HALF] = own
    grad_middle[:, HALF:] = oth
    branch_own[...] = own.astype(BF)
    branch_oth[...] = oth.astype(BF)
    before = mark(incoming[:16].astype(F32), 0)[:1]
    sigma = jax.nn.sigmoid(gate[...])
    copies[0].wait()
    grad_mixed = product_right(branch_own[...], near[...])
    copies[1].wait()
    grad_mixed += product(branch_oth[...], far[:, :VW])
    slope = sigma * (1.0 + gate[...] * (1.0 - sigma))
    none = jnp.zeros((PIECE, VPAD - VW), F32)
    grad_gate[:, :VW] = (grad_mixed * grouped[:, :VW] * slope).astype(BF)
    grad_gate[:, VW:] = none.astype(BF)
    held[:, :VW] = grad_mixed * (gate[...] * sigma)
    held[:, VW:] = none
    lane = lax.broadcasted_iota(jnp.int32, (PIECE, 128), 1)
    total[...] = jnp.zeros_like(total)
    for head in range(HEADS):
        begin, end = window(head)
        here = inside(head, PIECE)
        grad = head_part(held, head, PIECE)
        group = head_part(grouped, head, PIECE)
        scale = jnp.sum(jnp.where(lane == head, scales[...], 0.0), 1, keepdims=True)
        back = grad - jnp.sum(grad, 1, keepdims=True) / VH - group * (jnp.sum(grad * group, 1, keepdims=True) / VH)
        total[:PIECE, begin:end] += jnp.where(here, scale * back, 0.0)
    grad_retained[...] = total[:PIECE].astype(BF)
    total[...] = jnp.zeros_like(total)
    for head in range(HEADS):
        begin, end = window(head)
        own = slice(head * KH, (head + 1) * KH)
        reached = reach_of(rates[head], seg_column[...], before) * head_part(grad_retained, head, PIECE)
        total[:, begin:end] += product_left(queries[:, own], reached.astype(BF))
    term[...] = with_marks(total[...], seg_row[...])


def back_kernel(
    rates, seg_column, seg_row, queries, keys, values, masked, incoming, grad_retained, grad_gate, gb, low2,
    gate_query, parcel, base_key, base_value,
):
    before = mark(incoming[:16].astype(F32), 0)[:1]
    gate_query[:, :VPAD] = grad_gate[...]
    base_value[...] = jnp.zeros_like(base_value)
    for head in range(HEADS):
        rate = rates[head]
        begin, end = window(head)
        own = slice(head * KH, (head + 1) * KH)
        value = head_part(values, head, PIECE).astype(BF)
        grad = head_part(grad_retained, head, PIECE).astype(BF)
        decay = decay_of(rate, seg_column[...], seg_row[...])
        reach = reach_of(rate, seg_column[...], before)
        grad_scores = (product_right(grad, value) * decay).astype(BF)
        grad_query = product(grad_scores, keys[:, own])
        grad_query += reach * product_right(grad, incoming[:, begin:end])
        gate_query[:, VPAD + head * KH : VPAD + (head + 1) * KH] = grad_query.astype(BF)
        base_key[:, own] = product_left(grad_scores, queries[:, own])
        base_value[:, begin:end] += product_left(masked[head], grad)
    parcel[:, :HALF] = gb[...]
    parcel[:, HALF : 2 * HALF] = low2[...]
    parcel[:, 2 * HALF :] = gate_query[...]


def later_kernel(rates, seg_column, seg_row, keys, values, outgoing, base_key, base_value, out, total):
    total[...] = base_value[...]
    for head in range(HEADS):
        begin, end = window(head)
        own = slice(head * KH, (head + 1) * KH)
        value = head_part(values, head, PIECE).astype(BF)
        tail = tail_of(rates[head], seg_column[...], seg_row[...])
        grad_key = base_key[:, own] + tail * product_right(value, outgoing[:, begin:end])
        out[:, own] = grad_key.astype(BF)
        total[:, begin:end] += jnp.where(inside(head, PIECE), tail * product(keys[:, own], outgoing[:, begin:end]), 0.0)
    out[:, HALF:] = total[...].astype(BF)


def first_back_kernel(
    gate_query, gate_query_theirs, key_value, key_value_theirs, query_weight, key_weight, value_weight, gate_weight,
    part, helped,
):
    both = jnp.concatenate([gate_query[...], gate_query_theirs[...]], 0)
    total = product_right(both[:, VPAD:], query_weight[...])
    total += product(both[:, :VW], gate_weight[...])
    both = jnp.concatenate([key_value[...], key_value_theirs[...]], 0)
    total += product_right(both[:, :HALF], key_weight[...])
    total += product(both[:, HALF : HALF + VW], value_weight[...])
    part[...] = total[:PIECE].astype(BF)
    helped[...] = total[PIECE:].astype(BF)


def last_kernel(
    shard, mine, theirs, helped, helped_other, normed, inverse, gain, grad_middle, vectors, out, vec_own, vec_oth
):
    grads = [
        mine[...].astype(F32) + theirs[...].astype(F32),
        helped[...].astype(F32) + helped_other[...].astype(F32),
    ]
    norms = [normed[:, :HALF], normed[:, HALF:]]
    for k, vec in enumerate((vec_own, vec_oth)):
        cut = slice(k * HALF, (k + 1) * HALF)
        rows = [jnp.sum(grads[k] * norms[k], 0, keepdims=True), jnp.sum(grads[k], 0, keepdims=True)]
        rows += [vectors[0:1, cut], vectors[1:2, cut], jnp.zeros((12, HALF), F32)]
        vec[...] = jnp.concatenate(rows, 0).astype(BF)
    back = norm_back(grads, own_first(shard[0], gain[...]), norms, inverse[:, :1])
    total = [grad_middle[:, :HALF] + back[0], grad_middle[:, HALF:] + back[1]]
    out[:, :HALF] = jnp.where(shard[0] == 0, total[0], total[1])
    out[:, HALF:] = jnp.where(shard[0] == 0, total[1], total[0])


def rows_of(core):
    column = lax.broadcasted_iota(jnp.int32, (HALF // 2, HALF), 1)
    row = lax.broadcasted_iota(jnp.int32, (HALF // 2, HALF), 0)
    source = (row // BLOCK * 2 + core) * BLOCK + row % BLOCK
    return (column == source).astype(F32).astype(BF)


def rows_kernel(core, *refs):
    count = (len(refs) - 2) // 2
    for chosen, out in ((core[0], refs[-2]), (1 - core[0], refs[-1])):
        pick = rows_of(chosen)
        for k in range(2 * count):
            out[:, k * PIECE : (k + 1) * PIECE] = product_right(pick, refs[k][...]).astype(BF)


def rows_more_kernel(core, low2, gb, sent, *refs):
    kept, gone, gate_query = refs[-3:]
    parts = [low2, sent.at[:, HALF : 2 * HALF], gb, sent.at[:, :HALF]]
    for chosen, out in ((core[0], kept), (1 - core[0], gone)):
        pick = rows_of(chosen)
        for k in range(4):
            out[:, k * PIECE : (k + 1) * PIECE] = product_right(pick, parts[k][...]).astype(BF)
    gate_query[...] = sent[:, 2 * HALF :]


def features_of(core, own, received):
    both = shape(HALF // 2, 2 * PIECE)
    kept, gone = run(rows_kernel, (both, both), [core], [own, received])
    return kept, core_swap(gone)


def all_tokens(array, other):
    return (array, other, core_swap(array), core_swap(other))


CHUNK = 896


def outer(features, groups, plan, chunk=CHUNK, vectors=None, core=None, later=()):
    steps = len(plan)
    flat = [a for kept, got, _ in features for a in (kept, got)]
    flat += [a for group in groups for a in group] + list(vectors or ())
    specs = []
    for _, _, block in features:
        specs += [pl.BlockSpec((HALF // 2, 2 * PIECE), lambda i, c, block=block: (0, block))] * 2
    for g in range(len(groups)):
        mine = [k for k in range(steps) if plan[k][1] == g]
        first, count, block = mine[0], len(mine), plan[mine[0]][2]
        assert mine == list(range(first, first + count))

        def place(i, c, first=first, count=count, block=block):
            return (0, block + jnp.clip(i - first, 0, count - 1))

        specs += [pl.BlockSpec((PIECE, chunk), place)] * 4
    specs += [pl.BlockSpec((16, HALF), lambda i, c: (0, 0))] * len(vectors or ())
    specs += [ANY] * len(later)
    flat += list(later)

    def chosen(step, column, choices):
        value = choices[plan[0][column]]
        for k in range(1, steps):
            if plan[k][column] != plan[k - 1][column]:
                value = jnp.where(step >= k, choices[plan[k][column]], value)
        return value

    def kernel(core, *refs):
        out = refs[-1]
        step = pl.program_id(0)
        count = 2 * len(features)
        left = [
            jnp.concatenate([refs[2 * k][...], refs[2 * k + 1][...]], 1) for k in range(len(features))
        ]
        right = [
            jnp.concatenate([refs[count + 4 * k + j][...] for j in range(4)], 0) for k in range(len(groups))
        ]
        out[...] = product(chosen(step, 0, left), chosen(step, 1, right)).astype(BF)
        if vectors is not None:

            @pl.when(step == steps - 1)
            def _():
                rows = refs[count + 4 * len(groups) :]
                total = (rows[0][...].astype(F32) + rows[1][...].astype(F32)) + (
                    rows[2][...].astype(F32) + rows[3][...].astype(F32)
                )
                column = lax.broadcasted_iota(jnp.int32, (16, 128), 1)
                row = lax.broadcasted_iota(jnp.int32, (16, 128), 0)
                shift = (column == row + 64).astype(F32).astype(BF)
                moved = product(product_right(rows_of(core[0]), total.astype(BF)).astype(BF), shift)
                out[:, chunk - 128 :] = (out[:, chunk - 128 :].astype(F32) + moved).astype(BF)

    if core is None:
        core = jnp.zeros((1,), jnp.int32)
    part = pl.pallas_call(
        kernel,
        out_shape=shape(HALF // 2, steps * chunk),
        grid_spec=pltpu.PrefetchScalarGridSpec(
            num_scalar_prefetch=1,
            grid=(steps,),
            in_specs=specs,
            out_specs=pl.BlockSpec((HALF // 2, chunk), lambda i, c: (0, i)),
        ),
        compiler_params=pltpu.CompilerParams(vmem_limit_bytes=56 * 1024 * 1024),
        cost_estimate=pl.CostEstimate(flops=0, bytes_accessed=0, transcendentals=0),
    )(core, *flat)
    return part.reshape(16, BLOCK, steps * chunk)


def sent(part):
    return lax.all_to_all(part, "ctx", 0, 0, axis_index_groups=PLANE, tiled=True)


def added(parts):
    return jnp.sum(parts.astype(F32), 0)


def body(
    tokens,
    segments,
    decay_rate,
    first_gain,
    first_bias,
    query_weight,
    key_weight,
    value_weight,
    gate_weight,
    out_weight,
    second_gain,
    second_bias,
    mlp_gate,
    mlp_up,
    mlp_down,
    upstream,
):
    shard = lax.axis_index("shard").astype(jnp.int32).reshape(1)
    ctx = lax.axis_index("ctx").astype(jnp.int32).reshape(1)
    core = ctx % 2
    tokens, upstream = tokens[0], upstream[0]
    value_turned, gate_turned, mlp_gate_turned, mlp_up_turned = value_weight.T, gate_weight.T, mlp_gate.T, mlp_up.T
    gain1, bias1, gain2, bias2 = first_gain[None], first_bias[None], second_gain[None], second_bias[None]
    seg = segments[0].astype(F32)
    seg_column, seg_row = seg[:, None], seg[None, :]
    weight = pltpu.VMEM((VW, HALF), BF)
    held = pltpu.VMEM((HALF, VPAD), BF)
    small = shape(PIECE, HALF)
    wide = shape(PIECE, WIDE)
    scale = shape(PIECE, 128, kind=F32)

    def dma(count):
        return pltpu.SemaphoreType.DMA((count,))

    normed1, inverse1, low1_own, low1_oth, packed = run(
        first_kernel,
        (shape(PIECE, WIDE, kind=F32), scale, small, small, shape(BLOCK, PACKED)),
        [ctx, shard],
        [tokens, gain1, bias1],
        [mlp_gate_turned, mlp_up_turned, out_weight],
        [pltpu.VMEM((GATHERED, VW, 128), BF), dma(GATHERED)],
    )
    low1_theirs = from_shard(low1_oth)
    packed = from_shard(after(packed, low1_theirs))
    theirs_key, theirs_value = run(
        help_kernel,
        (shape(PIECE, HALF, kind=F32), shape(PIECE, VW, kind=F32)),
        [],
        [low1_theirs, key_weight, value_turned],
    )
    helped_key, helped_value = half_from_shard(theirs_key), half_from_shard(theirs_value)
    theirs_query, theirs_gate = run(
        help_more_kernel,
        (shape(PIECE, HALF, kind=F32), shape(PIECE, VW, kind=F32)),
        [],
        [low1_theirs, query_weight, gate_turned],
    )
    helped_query, helped_gate = half_from_shard(theirs_query), half_from_shard(theirs_gate)
    base_query, base_key, base_value, base_gate = run(
        base_kernel,
        tuple(shape(PIECE, n, kind=F32) for n in (HALF, HALF, VW, VW)),
        [],
        [low1_own, query_weight, key_weight, value_turned, gate_turned],
        [theirs_key],
    )

    up_own, up_oth = run(turn_kernel, (small, small), [shard], [upstream])
    up_theirs = from_shard(up_oth)
    others = lax.all_gather(after(packed, theirs_value, up_theirs), "ctx", axis=0, tiled=True)


    def exchange(states, reverse, *before):
        mine = lax.all_to_all(states.reshape(NC, KH // NC, VPAD), "ctx", 0, 0, tiled=True)
        done = run(functools.partial(scan_kernel, reverse), shape(NC, KH // NC, VPAD), [decay_rate], [mine], before)
        return lax.all_to_all(done, "ctx", 0, 0, tiled=True).reshape(KH, VPAD), mine, done

    keys, values, local = run(
        local_kernel,
        (small, shape(PIECE, VPAD), shape(KH, VPAD)),
        [decay_rate],
        [seg_column, seg_row, base_key, base_value, helped_key, helped_value],
        [theirs_query],
        scratch=[pltpu.VMEM((KH, VPAD), F32)],
    )
    base_hidden, theirs_hidden = run(
        hidden_kernel,
        (shape(PIECE, VW, kind=F32), shape(PIECE, VW, kind=F32)),
        [],
        [up_own, up_theirs, mlp_down],
    )
    helped_hidden = half_from_shard(theirs_hidden)
    incoming, _, _ = exchange(local, False, helped_query, helped_gate, theirs_hidden)
    queries, inner, masked = run(
        inner_kernel,
        (small, shape(PIECE, VPAD, kind=F32), shape(HEADS, PIECE, PIECE)),
        [decay_rate],
        [seg_column, seg_row, base_query, helped_query, keys, values],
    )
    up_features = features_of(core, up_own, up_theirs)
    low1_features = features_of(core, low1_own, low1_theirs)
    gate_pre, grouped, scales, mixed, part = run(
        mix_kernel,
        (shape(PIECE, VW, kind=F32), shape(PIECE, VPAD, kind=F32), scale, shape(PIECE, VPAD), wide),
        [decay_rate],
        [seg_column, queries, inner, incoming, base_gate, helped_gate],
        [out_weight, others, helped_hidden],
        [pltpu.VMEM((PIECE, VPAD), F32), held, weight, dma(2)],
    )
    theirs = from_tp(part)
    middle, normed2, inverse2, low2_own, low2_oth, mlp_parts, part = run(
        mlp_kernel,
        (shape(PIECE, WIDE, kind=F32), shape(PIECE, WIDE, kind=F32), scale, small, small, shape(PIECE, 4 * VPAD), wide),
        [shard],
        [tokens, part, theirs, gain2, bias2, base_hidden, helped_hidden, mixed],
        [mlp_gate_turned, mlp_up_turned, others, up_features[1], low1_features[1]],
        [weight, weight, held, held, dma(4)],
    )
    theirs = from_tp(part)
    mlp_parts = after(mlp_parts, theirs)
    mlp_theirs = from_shard(mlp_parts)
    grad_middle, gb_own, gb_oth, vectors, grad_gate, grad_retained, term = run(
        unmix_kernel,
        (
            shape(PIECE, WIDE, kind=F32),
            small,
            small,
            shape(8, WIDE, kind=F32),
            shape(PIECE, VPAD),
            shape(PIECE, VPAD),
            shape(KH, VPAD),
        ),
        [shard, decay_rate],
        [part, theirs, normed2, inverse2, gain2, up_own, up_oth]
        + [seg_column, seg_row, queries, incoming, gate_pre, grouped, scales],
        [out_weight, others],
        [pltpu.VMEM((PIECE, VPAD), F32), pltpu.VMEM((KH, VPAD), F32), weight, held, dma(2)],
    )

    gate_query, parcel, base_key_grad, base_value_grad = run(
        back_kernel,
        (
            shape(PIECE, VPAD + HALF),
            shape(PIECE, 2 * HALF + VPAD + HALF),
            shape(PIECE, HALF, kind=F32),
            shape(PIECE, VPAD, kind=F32),
        ),
        [decay_rate],
        [seg_column, seg_row, queries, keys, values, masked, incoming, grad_retained, grad_gate, gb_oth, low2_oth],
    )
    parcel = from_shard(parcel)
    outgoing, _, scanned = exchange(term, True, gate_query)
    key_value = run(
        later_kernel,
        shape(PIECE, HALF + VPAD),
        [decay_rate],
        [seg_column, seg_row, keys, values, outgoing, base_key_grad, base_value_grad],
        scratch=[pltpu.VMEM((PIECE, VPAD), F32)],
    )
    key_value_theirs = from_shard(key_value)

    mlp_parts, mlp_theirs = hold((mlp_parts, mlp_theirs), scanned)
    both = shape(HALF // 2, 4 * PIECE)
    kept, gone, gate_query_theirs = run(
        rows_more_kernel, (both, both, shape(PIECE, VPAD + HALF)), [core], [low2_own, gb_own, parcel], [scanned]
    )
    got = core_swap(gone)
    early_part = outer(
        [(*up_features, 0), (kept, got, 0), (kept, got, 1)],
        [all_tokens(mlp_parts, mlp_theirs)],
        [(0, 0, 0), (1, 0, 1), (1, 0, 2), (2, 0, 3)],
        VPAD,
    )
    early = lax.psum_scatter(
        after(early_part, outgoing), "ctx", scatter_dimension=0, axis_index_groups=PLANE, tiled=False
    )
    early = early.astype(F32)
    gate_query, gate_query_theirs = hold((gate_query, gate_query_theirs), key_value)
    gate_query_parts = sent(
        outer(
            [(*low1_features, 0)],
            [all_tokens(gate_query, gate_query_theirs)],
            [(0, 0, 0), (0, 0, 1)],
            (VPAD + HALF) // 2,
        )
    )
    first_weights = [query_weight, key_weight, value_turned, gate_turned]
    part, helped = run(
        first_back_kernel,
        (small, small),
        [],
        [gate_query, gate_query_theirs, key_value, key_value_theirs] + first_weights,
    )
    tokens_grad, vec_own, vec_oth = run(
        last_kernel,
        (shape(PIECE, WIDE, kind=F32), shape(16, HALF), shape(16, HALF)),
        [shard],
        [part, from_tp(part), from_shard(helped), lax.ppermute(helped, ("shard", "tp"), SHARD_TP)]
        + [normed1, inverse1, gain1, grad_middle, vectors],
    )
    sums = (
        vec_own,
        from_shard(vec_oth),
        core_swap(vec_own),
        lax.ppermute(vec_oth, ("shard", "ctx"), SHARD_CORE),
    )
    key_value_parts = sent(
        outer(
            [(*low1_features, 0)],
            [all_tokens(key_value, key_value_theirs)],
            [(0, 0, 0), (0, 0, 1)],
            (HALF + VPAD) // 2,
            vectors=sums,
            core=core,
            later=(gate_query_parts,),
        )
    )

    part = run(down_kernel, shape(2 * PIECE, HALF), [], [mlp_parts, mlp_theirs, mlp_down])
    down_own, down_gone = run(
        down_sum_kernel, (shape(PIECE, HALF, kind=F32), small), [], [part, from_tp(part)]
    )
    layer_out = run(result_kernel, wide, [shard], [middle, down_own, from_shard(down_gone)])

    gate_query_sums, key_value_sums = added(gate_query_parts), added(key_value_parts)
    norms = key_value_sums[:, HALF + VW : HALF + VW + 4].T
    early = [early[:, k * VPAD : k * VPAD + VW] for k in range(4)]
    return (
        layer_out[None],
        tokens_grad[None],
        norms[0],
        norms[1],
        gate_query_sums[:, VPAD:],
        key_value_sums[:, :HALF],
        key_value_sums[:, HALF : HALF + VW],
        gate_query_sums[:, :VW],
        early[3].T,
        norms[2],
        norms[3],
        early[1],
        early[2],
        early[0].T,
    )


def solution(mesh):
    in_specs = (
        P("shard", "ctx", None),
        P("shard", "ctx"),
        P("tp"),
        P(),
        P(),
        P("shard", "tp"),
        P("shard", "tp"),
        P("shard", "tp"),
        P("shard", "tp"),
        P("tp", "shard"),
        P(),
        P(),
        P("shard", "tp"),
        P("shard", "tp"),
        P("tp", "shard"),
        P("shard", "ctx", None),
    )
    out_specs = (
        P("shard", "ctx", None),
        P("shard", "ctx", None),
        P(("shard", "ctx")),
        P(("shard", "ctx")),
        P(("shard", "ctx"), "tp"),
        P(("shard", "ctx"), "tp"),
        P(("shard", "ctx"), "tp"),
        P(("shard", "ctx"), "tp"),
        P("tp", ("shard", "ctx")),
        P(("shard", "ctx")),
        P(("shard", "ctx")),
        P(("shard", "ctx"), "tp"),
        P(("shard", "ctx"), "tp"),
        P("tp", ("shard", "ctx")),
    )
    return jax.shard_map(body, mesh=mesh, in_specs=in_specs, out_specs=out_specs, check_vma=False)
```

time: 4230 us -> 421 us (0.10)
  waiting for transfers between devices: 3280 us -> 149 us
  blocking collectives: 417 us -> 0 us
  matrix products: 151 us -> 0 us
  other arithmetic: 155 us -> 8.45 us
  Pallas kernels: 0 us -> 133 us
  loops' own time: 85.7 us -> 0 us
  starting transfers between devices: 2.16 us -> 87.3 us
  local copies, waits for them, and re-layouts: 86.8 us -> 21.1 us
    reduce_scatter x8 -> x0, waiting for transfers between devices: 2470 us -> none  [the longest x1 354 us: body(): lax.psum_scatter(grad_gate_weight, ('shard', 'ctx'), scatter_dimension=0,...]
    all_gather x10 -> x1, waiting for transfers between devices: 682 us -> 0.01 us  [body(): lax.all_gather(after(packed, theirs_value, up_theirs), 'ctx', axis=0, til...]
    unnamed x3 -> x0, blocking collectives: 417 us -> none
    dot_general x36 -> x0, matrix products: 151 us -> none  [the longest x8 53.1 us: product_left(): lax.dot_general(left, right, (((0,), (0,)), ((), ())), preferred_element_...]
    select_n x64 -> x0, other arithmetic: 140 us -> none  [turn(): return jax.tree.map(lambda a, b: jnp.where(reached, a, b), new, before)]
    pallas_call x0 -> x32, Pallas kernels: none -> 133 us  [the longest x23 114 us: run(): pl.pallas_call(kernel, out_shape=outs, grid=(1,), in_specs=[SMEM] * len(s...]
    ppermute x0 -> x30, waiting for transfers between devices: none -> 127 us  [the longest x9 62.5 us: from_shard(): return lax.ppermute(part, 'shard', SWAP)]
    psum x4 -> x0, waiting for transfers between devices: 121 us -> none  [the longest x1 43.2 us: body(): middle = inputs + lax.psum(product(mixed, full_out), 'tp')]
  transfers between devices with their start and end apart: 22 -> 38, of which waited for: 17 -> 23; matrix products, arithmetic and copies ran while one was open for 5% -> 3% of each run, Pallas kernels for 0% -> 26%
where the time goes in v1:
time: 421 us; the launch traced here: 413 us
  waiting for transfers between devices  149 us (35%)
  Pallas kernels  133 us (32%)
  starting transfers between devices  87.3 us (21%)
  local copies, waits for them, and re-layouts  21.1 us (5%)
  between operations  14.8 us (4%)
  other arithmetic  8.45 us (2%)
    pallas_call x23, Pallas kernels, run(): pl.pallas_call(kernel, out_shape=outs, grid=(1,), in_specs=[SMEM] * len(s...  114 us
    ppermute x9, waiting for transfers between devices, from_shard(): return lax.ppermute(part, 'shard', SWAP)  62.5 us
    ppermute x4, waiting for transfers between devices, from_tp(): return lax.ppermute(part, 'tp', SWAP)  31 us
    ppermute x9, starting transfers between devices, from_shard(): return lax.ppermute(part, 'shard', SWAP)  20.6 us
    pallas_call x3, Pallas kernels, outer(): pl.pallas_call(kernel, out_shape=shape(HALF // 2, steps * chunk), grid_sp...  19.3 us
    ppermute x5, waiting for transfers between devices, half_from_shard(): return lax.ppermute(part.astype(F16), 'shard', SWAP).astype(F32)  19.2 us
    all_to_all x2, starting transfers between devices, exchange(): lax.all_to_all(states.reshape(NC, KH // NC, VPAD), 'ctx', 0, 0, tiled=True)  16 us
    unnamed x66, local copies, waits for them, and re-layouts  15.9 us
  transfers between devices with their start and end apart: 38, of which 23 were waited for; matrix products, arithmetic and copies ran while one was open for 3% of the time, Pallas kernels for 26%

profile of v1, /device:TPU:8, one launch (start us, length us, event | category | flops | bytes accessed | tf_op | source)
XLA Modules:
  0.0 413.1 jit_solution(1646738095661185390)
XLA Ops:
  7.2 4.0 shard_map.263
  11.2 3.1 collective-permute-start
  14.3 6.7 %collective-permute-done.low.refs_1_ = bf16[128,1024]{1,0:T(8,128)(2,1)S(1)} collective-permute-done((bf16[128,1024]{1,0:T(8,128)(2,1)}, bf16[128,1024]{1,0:T(8,128)(2,1)S(1)}, u32[]{:S(2)}, u32[]{:S(2)}) %collective-permute-start) | collective-permute-done | bytes 262176 | tf_op jit(solution)/shard_map/ppermute | solution.py:50
  21.7 3.0 collective-permute-start.6
  27.2 5.2 %shard_map.264 = (f32[128,1024]{1,0:T(8,128)}, f32[128,1728]{1,0:T(8,128)}) custom-call(bf16[128,1024]{1,0:T(8,128)(2,1)} %copy-done.5, bf16[1024,1024]{1,0:T(8,128)(2,1)} %key_weight.5, bf16[1728,1024]{1,0:T(8,128)(2,1)} %bitcast.34), custom_call_target="tpu_custom_call" | custom-call | tf_op jit(solution)/shard_map/pallas_call | solution.py:76
  32.3 5.7 %collective-permute-done.5.theirs.refs_2_.refs_1_ = bf16[128,1024]{1,0:T(8,128)(2,1)S(1)} collective-permute-done((bf16[128,1024]{1,0:T(8,128)(2,1)}, bf16[128,1024]{1,0:T(8,128)(2,1)S(1)}, u32[]{:S(2)}, u32[]{:S(2)}) %collective-permute-start.5) | collective-permute-done | bytes 262176 | tf_op jit(solution)/shard_map/ppermute | solution.py:50
  40.1 3.1 collective-permute-start.3
  45.1 8.2 %shard_map.265 = (f32[128,1024]{1,0:T(8,128)}, f32[128,1024]{1,0:T(8,128)}, f32[128,1728]{1,0:T(8,128)}, f32[128,1728]{1,0:T(8,128)}) custom-call(bf16[128,1024]{1,0:T(8,128)(2,1)} %get-tuple-element.78.low.refs_0_, bf16[1024,1024]{1,0:T(8,128)(2,1)} %query_weight.5, bf16[1024,1024]{1,0:T(8,128)(2,1)} %key_weight.5, bf16[1728,1024]{1,0:T(8,128)(2,1)} %bitcast.35, ...), custom_call_target="tpu_custom_call" | custom-call | tf_op jit(solution)/shard_map/pallas_call | solution.py:76
  53.3 5.2 %shard_map.266 = (f32[128,1024]{1,0:T(8,128)}, f32[128,1728]{1,0:T(8,128)}) custom-call(bf16[128,1024]{1,0:T(8,128)(2,1)} %copy-done.5, bf16[1024,1024]{1,0:T(8,128)(2,1)} %query_weight.5, bf16[1728,1024]{1,0:T(8,128)(2,1)} %bitcast.38), custom_call_target="tpu_custom_call" | custom-call | tf_op jit(solution)/shard_map/pallas_call | solution.py:76
  60.3 3.7 shard_map.267
  64.0 8.6 %all-to-all-start = ((bf16[32,8,1792]{2,1,0:T(8,128)(2,1)}), bf16[32,8,1792]{2,1,0:T(8,128)(2,1)S(1)}, u32[]{:S(2)}, u32[]{:S(2)}) async-start(bf16[32,8,1792]{2,1,0:T(8,128)(2,1)} %bitcast.53), calls=%async_computation | async-start | bytes 1835008 | tf_op jit(solution)/shard_map/all_to_all | solution.py:690
  72.7 3.1 collective-permute-start.4
  76.4 4.5 %shard_map.270 = (f32[128,1728]{1,0:T(8,128)}, f32[128,1728]{1,0:T(8,128)}) custom-call(bf16[128,1024]{1,0:T(8,128)(2,1)} %get-tuple-element.92.own.refs_0_.up_own, bf16[128,1024]{1,0:T(8,128)(2,1)} %copy-done.11, bf16[1728,1024]{1,0:T(8,128)(2,1)} %weight.3), custom_call_target="tpu_custom_call" | custom-call | tf_op jit(solution)/shard_map/pallas_call | solution.py:76
  80.9 11.5 %collective-permute-done.1 = f16[128,1024]{1,0:T(8,128)(2,1)S(1)} collective-permute-done((f16[128,1024]{1,0:T(8,128)(2,1)S(1)}, f16[128,1024]{1,0:T(8,128)(2,1)S(1)}, u32[]{:S(2)}, u32[]{:S(2)}) %collective-permute-start.1) | collective-permute-done | bytes 262176 | tf_op jit(solution)/shard_map/ppermute | solution.py:54
  98.9 6.5 %all-to-all-start.1 = ((bf16[32,8,1792]{2,1,0:T(8,128)(2,1)}), bf16[32,8,1792]{2,1,0:T(8,128)(2,1)S(1)}, u32[]{:S(2)}, u32[]{:S(2)}) async-start(bf16[32,8,1792]{2,1,0:T(8,128)(2,1)} %shard_map.271), calls=%async_computation.1 | async-start | bytes 1835008 | tf_op jit(solution)/shard_map/all_to_all | solution.py:692
  105.5 3.3 collective-permute-start.7
  108.8 3.4 shard_map.268
  112.1 7.7 %collective-permute-done.7 = f16[128,1728]{1,0:T(8,128)(2,1)S(1)} collective-permute-done((f16[128,1728]{1,0:T(8,128)(2,1)S(1)}, f16[128,1728]{1,0:T(8,128)(2,1)S(1)}, u32[]{:S(2)}, u32[]{:S(2)}) %collective-permute-start.7) | collective-permute-done | bytes 442400 | tf_op jit(solution)/shard_map/ppermute | solution.py:54
  121.7 7.4 %shard_map.274 = (f32[128,1728]{1,0:T(8,128)}, f32[128,1792]{1,0:T(8,128)}, f32[128,128]{1,0:T(8,128)}, bf16[128,1792]{1,0:T(8,128)(2,1)}, bf16[128,2048]{1,0:T(8,128)(2,1)}) custom-call(f32[4]{0:T(128)} %rates.15, f32[128,1]{1,0:T(8,128)} %copy.52.seg_column, bf16[128,1024]{1,0:T(8,128)(2,1)} %get-tuple-element.88.queries, ...), custom_call_target="tpu_custom_call" | custom-call | tf_op jit(solution)/shard_map/pallas_call | solution.py:76
  130.7 3.0 shard_map.275
  138.6 4.0 collective-permute-done.8.theirs
  143.4 14.5 %shard_map.277 = (f32[128,2048]{1,0:T(8,128)}, f32[128,2048]{1,0:T(8,128)}, f32[128,128]{1,0:T(8,128)}, bf16[128,1024]{1,0:T(8,128)(2,1)}, bf16[128,1024]{1,0:T(...) custom-call(s32[1]{0:T(128)} %bitcast.shard, bf16[128,2048]{1,0:T(8,128)(2,1)} %bitcast.52, ...), custom_call_target="tpu_custom_call" | custom-call | tf_op jit(solution)/shard_map/pallas_call | solution.py:76
  159.6 11.0 %collective-permute-done.11.refs_1_.theirs = bf16[128,2048]{1,0:T(8,128)(2,1)S(1)} collective-permute-done((bf16[128,2048]{1,0:T(8,128)(2,1)}, bf16[128,2048]{1,0:T(8,128)(2,1)S(1)}, u32[]{:S(2)}, u32[]{:S(2)}) %collective-permute-start.11) | collective-permute-done | bytes 524320 | tf_op jit(solution)/shard_map/ppermute | solution.py:58
  174.4 9.2 %shard_map.279 = (f32[128,2048]{1,0:T(8,128)}, bf16[128,1024]{1,0:T(8,128)(2,1)}, bf16[128,1024]{1,0:T(8,128)(2,1)}, f32[8,2048]{1,0:T(8,128)}, bf16[128,1792]{1...) custom-call(s32[1]{0:T(128)} %bitcast.shard, f32[4]{0:T(128)} %rates.15, ...), custom_call_target="tpu_custom_call" | custom-call | tf_op jit(solution)/shard_map/pallas_call | solution.py:76
  183.6 7.4 %all-to-all-start.2 = ((bf16[32,8,1792]{2,1,0:T(8,128)(2,1)}), bf16[32,8,1792]{2,1,0:T(8,128)(2,1)S(1)}, u32[]{:S(2)}, u32[]{:S(2)}) async-start(bf16[32,8,1792]{2,1,0:T(8,128)(2,1)} %bitcast.54), calls=%async_computation.2 | async-start | bytes 1835008 | tf_op jit(solution)/shard_map/all_to_all | solution.py:690
  191.1 5.0 %shard_map.280 = (bf16[128,2816]{1,0:T(8,128)(2,1)}, bf16[128,4864]{1,0:T(8,128)(2,1)}, f32[128,1024]{1,0:T(8,128)}, f32[128,1792]{1,0:T(8,128)}) custom-call(f32[4]{0:T(128)} %rates.15, f32[128,1]{1,0:T(8,128)} %copy.52.seg_column, f32[1,128]{1,0:T(1,128)} %get-tuple-element.150.seg_row, bf16[128,1024]{1,0:T(8,128)(2,1)} %get-tuple-element.88.queries, ...), custom_call_target="tpu_custom_call" | custom-call | tf_op jit(solution)/shard_map/pallas_call | solution.py:76
  196.1 8.1 %all-to-all-done.2.states = bf16[32,8,1792]{2,1,0:T(8,128)(2,1)S(1)} async-done(((bf16[32,8,1792]{2,1,0:T(8,128)(2,1)}), bf16[32,8,1792]{2,1,0:T(8,128)(2,1)S(1)}, u32[]{:S(2)}, u32[]{:S(2)}) %all-to-all-start.2) | async-done | bytes 917536 | tf_op jit(solution)/shard_map/all_to_all | solution.py:690
  207.6 4.9 %collective-permute-done.12.refs_1_ = bf16[128,7168]{1,0:T(8,128)(2,1)S(1)} collective-permute-done((bf16[128,7168]{1,0:T(8,128)(2,1)}, bf16[128,7168]{1,0:T(8,128)(2,1)S(1)}, u32[]{:S(2)}, u32[]{:S(2)}) %collective-permute-start.12) | collective-permute-done | bytes 1835040 | tf_op jit(solution)/shard_map/ppermute | solution.py:50
  217.3 7.4 %all-to-all-start.3 = ((bf16[32,8,1792]{2,1,0:T(8,128)(2,1)}), bf16[32,8,1792]{2,1,0:T(8,128)(2,1)S(1)}, u32[]{:S(2)}, u32[]{:S(2)}) async-start(bf16[32,8,1792]{2,1,0:T(8,128)(2,1)} %shard_map.281.refs_2_.refs_0_), calls=%async_computation.3 | async-start | bytes 1835008 | tf_op jit(solution)/shard_map/all_to_all | solution.py:692
  224.8 20.6 %collective-permute-done.15.sent = bf16[128,4864]{1,0:T(8,128)(2,1)} collective-permute-done((bf16[128,4864]{1,0:T(8,128)(2,1)}, bf16[128,4864]{1,0:T(8,128)(2,1)}, u32[]{:S(2)}, u32[]{:S(2)}) %collective-permute-start.15) | collective-permute-done | bytes 1245216 | tf_op jit(solution)/shard_map/ppermute | solution.py:50
  245.4 4.9 %shard_map.286 = (bf16[512,512]{1,0:T(8,128)(2,1)}, bf16[512,512]{1,0:T(8,128)(2,1)}, bf16[128,2816]{1,0:T(8,128)(2,1)}) custom-call(s32[1]{0:T(128)S(6)} %select_n.7.core, bf16[128,1024]{1,0:T(8,128)(2,1)} %get-tuple-element.121.low2, bf16[128,1024]{1,0:T(8,128)(2,1)} %get-tuple-element.122.gb, bf16[128,4864]{1,0:T(8,128)(2,1)} %collective-permute-done.15.sent, ...), custom_call_target="tpu_custom_call" | custom-call | tf_op jit(solution)/shard_map/pallas_call | solution.py:76
  253.9 9.1 %shard_map.293 = bf16[512,7168]{1,0:T(8,128)(2,1)} custom-call(s32[1]{0:T(128)} %constant.28.clone.1.core, bf16[512,256]{1,0:T(8,128)(2,1)} %get-tuple-element.139.refs_0_, bf16[512,256]{1,0:T(8,128)(2,1)} %copy-done.18, bf16[512,512]{1,0:T(8,128)(2,1)} %get-tuple-element.140.refs_2_.refs_4_, bf16[512,512]{1,0:T(8,128)(2,1)} %copy-done.12, ...), custom_call_target="tpu_custom_call" | custom-call | tf_op jit(solution)/shard_map/pallas_call | solution.py:594
  264.0 3.4 shard_map.287.refs_2_.key_value
  271.6 4.8 %shard_map.291 = bf16[512,2816]{1,0:T(8,128)(2,1)} custom-call(s32[1]{0:T(128)} %constant.28.clone.1.core, bf16[512,256]{1,0:T(8,128)(2,1)} %get-tuple-element.136.refs_0_, bf16[512,256]{1,0:T(8,128)(2,1)} %copy-done.10, bf16[128,2816]{1,0:T(8,128)(2,1)} %get-tuple-element.127.gate_query.refs_2_, ...), custom_call_target="tpu_custom_call" | custom-call | tf_op jit(solution)/shard_map/pallas_call | solution.py:594
  276.4 7.2 %all-to-all-start.4 = ((bf16[16,32,2816]{2,1,0:T(8,128)(2,1)}), bf16[16,32,2816]{2,1,0:T(8,128)(2,1)S(1)}, u32[]{:S(2)}, u32[]{:S(2)}) async-start(bf16[16,32,2816]{2,1,0:T(8,128)(2,1)} %bitcast.47), calls=%async_computation.4 | async-start | bytes 5767168 | tf_op jit(solution)/shard_map/all_to_all | solution.py:610
  283.6 3.3 collective-permute-start.16
  286.9 16.2 %collective-permute-done.16.key_value_theirs.refs_3_ = bf16[128,2816]{1,0:T(8,128)(2,1)S(1)} collective-permute-done((bf16[128,2816]{1,0:T(8,128)(2,1)}, bf16[128,2816]{1,0:T(8,128)(2,1)S(1)}, u32[]{:S(2)}, u32[]{:S(2)}) %collective-permute-start.16) | collective-permute-done | bytes 720928 | tf_op jit(solution)/shard_map/ppermute | solution.py:50
  304.0 9.0 %shard_map.289 = (bf16[128,1024]{1,0:T(8,128)(2,1)}, bf16[128,1024]{1,0:T(8,128)(2,1)}) custom-call(bf16[128,2816]{1,0:T(8,128)(2,1)} %get-tuple-element.127.gate_query.refs_2_, bf16[128,2816]{1,0:T(8,128)(2,1)} %get-tuple-element.128.gate_query_theirs.refs_3_, bf16[128,2816]{1,0:T(8,128)(2,1)} %shard_map.287.refs_2_.key_value, bf16[128,2816]{1,0:T(8,128)(2,1)} %copy-done.9, ...), custom_call_target="tpu_custom_call" | custom-call | tf_op jit(solution)/shard_map/pallas_call | solution.py:76
  317.4 5.1 %collective-permute-done.17.theirs = bf16[128,1024]{1,0:T(8,128)(2,1)S(1)} collective-permute-done((bf16[128,1024]{1,0:T(8,128)(2,1)}, bf16[128,1024]{1,0:T(8,128)(2,1)S(1)}, u32[]{:S(2)}, u32[]{:S(2)}) %collective-permute-start.17) | collective-permute-done | bytes 262176 | tf_op jit(solution)/shard_map/ppermute | solution.py:58
  322.5 6.8 %collective-permute-done.19.helped_other = bf16[128,1024]{1,0:T(8,128)(2,1)S(1)} collective-permute-done((bf16[128,1024]{1,0:T(8,128)(2,1)}, bf16[128,1024]{1,0:T(8,128)(2,1)S(1)}, u32[]{:S(2)}, u32[]{:S(2)}) %collective-permute-start.19) | collective-permute-done | bytes 262176 | tf_op jit(solution)/shard_map/ppermute | solution.py:814
  330.0 3.5 shard_map.290
  343.3 5.5 %shard_map.292 = bf16[512,2816]{1,0:T(8,128)(2,1)} custom-call(s32[1]{0:T(128)S(6)} %select_n.7.core, bf16[512,256]{1,0:T(8,128)(2,1)} %get-tuple-element.136.refs_0_, bf16[512,256]{1,0:T(8,128)(2,1)} %copy-done.10, bf16[128,2816]{1,0:T(8,128)(2,1)} %shard_map.287.refs_2_.key_value, bf16[128,2816]{1,0:T(8,128)(2,1)} %copy-done.9, ...), custom_call_target="tpu_custom_call" | custom-call | tf_op jit(solution)/shard_map/pallas_call | solution.py:594
  348.7 7.1 %all-to-all-start.5 = ((bf16[16,32,2816]{2,1,0:T(8,128)(2,1)}), bf16[16,32,2816]{2,1,0:T(8,128)(2,1)S(1)}, u32[]{:S(2)}, u32[]{:S(2)}) async-start(bf16[16,32,2816]{2,1,0:T(8,128)(2,1)} %bitcast.48), calls=%async_computation.5 | async-start | bytes 5767168 | tf_op jit(solution)/shard_map/all_to_all | solution.py:610
  355.8 5.1 %shard_map.283.mine = bf16[256,1024]{1,0:T(8,128)(2,1)} custom-call(bf16[128,7168]{1,0:T(8,128)(2,1)} %get-tuple-element.117.own.refs_6_, bf16[128,7168]{1,0:T(8,128)(2,1)} %get-tuple-element.118.theirs.refs_7_, bf16[1728,1024]{1,0:T(8,128)(2,1)} %weight.3), custom_call_target="tpu_custom_call" | custom-call | tf_op jit(solution)/shard_map/pallas_call | solution.py:76
  362.3 10.9 %collective-permute-done.13.theirs = bf16[256,1024]{1,0:T(8,128)(2,1)S(1)} collective-permute-done((bf16[256,1024]{1,0:T(8,128)(2,1)}, bf16[256,1024]{1,0:T(8,128)(2,1)S(1)}, u32[]{:S(2)}, u32[]{:S(2)}) %collective-permute-start.13) | collective-permute-done | bytes 524320 | tf_op jit(solution)/shard_map/ppermute | solution.py:58
  378.4 5.9 %collective-permute-done.14.oth = bf16[128,1024]{1,0:T(8,128)(2,1)S(1)} collective-permute-done((bf16[128,1024]{1,0:T(8,128)(2,1)}, bf16[128,1024]{1,0:T(8,128)(2,1)S(1)}, u32[]{:S(2)}, u32[]{:S(2)}) %collective-permute-start.14) | collective-permute-done | bytes 262176 | tf_op jit(solution)/shard_map/ppermute | solution.py:50
  389.1 3.0 all-to-all-done.5
  394.7 9.0 %reduce-scatter.4.cloned.1.call-done = bf16[1,32,7168]{2,1,0:T(8,128)(2,1)} async-done(((bf16[16,32,7168]{2,1,0:T(8,128)(2,1)}), bf16[1,32,7168]{2,1,0:T(8,128)(2,1)}) %reduce-scatter.4.cloned.1.call-update) | async-done | bytes 458768
  (150 shorter events, 79.5 us)
Async XLA Ops:
  7.2 113.7 %all-gather.2.cloned.1.call-start = ((), (), s32[]{:S(2)}) async-start(), calls=%async_computation.7 | async-start | bytes 11354112 | tf_op jit(solution)/shard_map/all_gather | solution.py:686
  11.2 9.8 %collective-permute-start = (bf16[128,1024]{1,0:T(8,128)(2,1)}, bf16[128,1024]{1,0:T(8,128)(2,1)S(1)}, u32[]{:S(2)}, u32[]{:S(2)}) collective-permute-start(bf16[128,1024]{1,0:T(8,128)(2,1)} %get-tuple-element.79), channel_id=1, source_target_pairs={{0,64},{64,0},{1,65},{65,1},{2,66},{66,2},{3,67},{67,3},{4,68},{68... | collective-permute-start | bytes 786440 | tf_op jit(solution)/shard_map/ppermute | solution.py:50
  21.7 16.3 %collective-permute-start.6 = (bf16[32,5376]{1,0:T(8,128)(2,1)}, bf16[32,5376]{1,0:T(8,128)(2,1)S(1)}, u32[]{:S(2)}, u32[]{:S(2)}) collective-permute-start(bf16[32,5376]{1,0:T(8,128)(2,1)} %shard_map.272), channel_id=1, source_target_pairs={{0,64},{64,0},{1,65},{65,1},{2,66},{66,2},{3,67},{67,3},{4,68},{68... | collective-permute-start | bytes 1032200 | tf_op jit(solution)/shard_map/ppermute | solution.py:50
  26.7 11.3 %collective-permute-start.5 = (bf16[128,1024]{1,0:T(8,128)(2,1)}, bf16[128,1024]{1,0:T(8,128)(2,1)S(1)}, u32[]{:S(2)}, u32[]{:S(2)}) collective-permute-start(bf16[128,1024]{1,0:T(8,128)(2,1)} %get-tuple-element.93.up_oth), channel_id=1, source_target_pairs={{0,64},{64,0},{1,65},{65,1},{2,66},{66,2},{3,67},{67,3},{4,68},{68... | collective-permute-start | bytes 786440 | tf_op jit(solution)/shard_map/ppermute | solution.py:50
  32.3 10.9 %copy-start.13 = (f32[128,1024]{1,0:T(8,128)S(1)}, f32[128,1024]{1,0:T(8,128)}, u32[]{:S(2)}) copy-start(f32[128,1024]{1,0:T(8,128)} %get-tuple-element.80._) | copy-start | bytes 1572868
  32.3 11.5 %copy-start.32 = (s32[1,128]{1,0:T(1,128)S(1)}, s32[1,128]{1,0:T(1,128)}, u32[]{:S(2)}) copy-start(s32[1,128]{1,0:T(1,128)} %param.17) | copy-start | bytes 1540
  40.1 19.2 %collective-permute-start.3 = (f16[128,1728]{1,0:T(8,128)(2,1)S(1)}, f16[128,1728]{1,0:T(8,128)(2,1)S(1)}, u32[]{:S(2)}, u32[]{:S(2)}) collective-permute-start(f16[128,1728]{1,0:T(8,128)(2,1)S(1)} %convert_element_type.62), channel_id=1, source_target_pairs={{0,64},{64,0},{1,65},{65,1},{2,66},{66,2},{3,67},{67,3},{4,68},{68... | collective-permute-start | bytes 1327112 | tf_op jit(solution)/shard_map/ppermute | solution.py:54
  43.2 15.2 %collective-permute-start.2 = (f16[128,1024]{1,0:T(8,128)(2,1)S(1)}, f16[128,1024]{1,0:T(8,128)(2,1)S(1)}, u32[]{:S(2)}, u32[]{:S(2)}) collective-permute-start(f16[128,1024]{1,0:T(8,128)(2,1)S(1)} %convert_element_type.60), channel_id=1, source_target_pairs={{0,64},{64,0},{1,65},{65,1},{2,66},{66,2},{3,67},{67,3},{4,68},{68... | collective-permute-start | bytes 786440 | tf_op jit(solution)/shard_map/ppermute | solution.py:54
  60.3 12.3 %copy-start.19 = (f32[128,1728]{1,0:T(8,128)S(1)}, f32[128,1728]{1,0:T(8,128)}, u32[]{:S(2)}) copy-start(f32[128,1728]{1,0:T(8,128)} %get-tuple-element.91) | copy-start | bytes 2654212
  60.3 15.5 %copy-start.14 = (f32[128,1024]{1,0:T(8,128)S(1)}, f32[128,1024]{1,0:T(8,128)}, u32[]{:S(2)}) copy-start(f32[128,1024]{1,0:T(8,128)} %get-tuple-element.82._) | copy-start | bytes 1572868
  64.0 31.4 %all-to-all-start = ((bf16[32,8,1792]{2,1,0:T(8,128)(2,1)}), bf16[32,8,1792]{2,1,0:T(8,128)(2,1)S(1)}, u32[]{:S(2)}, u32[]{:S(2)}) async-start(bf16[32,8,1792]{2,1,0:T(8,128)(2,1)} %bitcast.53), calls=%async_computation | async-start | bytes 1835008 | tf_op jit(solution)/shard_map/all_to_all | solution.py:690
  72.7 20.6 %collective-permute-start.4 = (f16[128,1728]{1,0:T(8,128)(2,1)S(1)}, f16[128,1728]{1,0:T(8,128)(2,1)S(1)}, u32[]{:S(2)}, u32[]{:S(2)}) collective-permute-start(f16[128,1728]{1,0:T(8,128)(2,1)S(1)} %convert_element_type.64), channel_id=1, source_target_pairs={{0,64},{64,0},{1,65},{65,1},{2,66},{66,2},{3,67},{67,3},{4,68},{68... | collective-permute-start | bytes 1327112 | tf_op jit(solution)/shard_map/ppermute | solution.py:54
  75.8 16.6 %collective-permute-start.1 = (f16[128,1024]{1,0:T(8,128)(2,1)S(1)}, f16[128,1024]{1,0:T(8,128)(2,1)S(1)}, u32[]{:S(2)}, u32[]{:S(2)}) collective-permute-start(f16[128,1024]{1,0:T(8,128)(2,1)S(1)} %convert_element_type.58), channel_id=1, source_target_pairs={{0,64},{64,0},{1,65},{65,1},{2,66},{66,2},{3,67},{67,3},{4,68},{68... | collective-permute-start | bytes 786440 | tf_op jit(solution)/shard_map/ppermute | solution.py:54
  96.3 9.1 %copy-start.7 = (f32[128,1728]{1,0:T(8,128)S(1)}, f32[128,1728]{1,0:T(8,128)}, u32[]{:S(2)}) copy-start(f32[128,1728]{1,0:T(8,128)} %get-tuple-element.94.refs_2_) | copy-start | bytes 2654212
  98.9 21.9 %all-to-all-start.1 = ((bf16[32,8,1792]{2,1,0:T(8,128)(2,1)}), bf16[32,8,1792]{2,1,0:T(8,128)(2,1)S(1)}, u32[]{:S(2)}, u32[]{:S(2)}) async-start(bf16[32,8,1792]{2,1,0:T(8,128)(2,1)} %shard_map.271), calls=%async_computation.1 | async-start | bytes 1835008 | tf_op jit(solution)/shard_map/all_to_all | solution.py:692
  105.5 14.3 %collective-permute-start.7 = (f16[128,1728]{1,0:T(8,128)(2,1)S(1)}, f16[128,1728]{1,0:T(8,128)(2,1)S(1)}, u32[]{:S(2)}, u32[]{:S(2)}) collective-permute-start(f16[128,1728]{1,0:T(8,128)(2,1)S(1)} %convert_element_type.66), channel_id=1, source_target_pairs={{0,64},{64,0},{1,65},{65,1},{2,66},{66,2},{3,67},{67,3},{4,68},{68... | collective-permute-start | bytes 1327112 | tf_op jit(solution)/shard_map/ppermute | solution.py:54
  129.1 13.4 %collective-permute-start.8 = (bf16[128,2048]{1,0:T(8,128)(2,1)}, bf16[128,2048]{1,0:T(8,128)(2,1)S(1)}, u32[]{:S(2)}, u32[]{:S(2)}) collective-permute-start(bf16[128,2048]{1,0:T(8,128)(2,1)} %get-tuple-element.97.mine), channel_id=1, source_target_pairs={{0,1},{1,0},{2,3},{3,2},{4,5},{5,4},{6,7},{7,6},{8,9},{9,8},{10,11... | collective-permute-start | bytes 1572872 | tf_op jit(solution)/shard_map/ppermute | solution.py:58
  133.7 3.5 collective-permute-start.9
  136.7 1.9 collective-permute-start.10
  137.2 5.4 %copy-start.18 = (bf16[512,256]{1,0:T(8,128)(2,1)}, bf16[512,256]{1,0:T(8,128)(2,1)S(1)}, u32[]{:S(2)}) copy-start(bf16[512,256]{1,0:T(8,128)(2,1)S(1)} %collective-permute-done.9._up.refs_1_) | copy-start | bytes 786436
  138.6 4.0 copy-start.10
  157.9 12.7 %collective-permute-start.11 = (bf16[128,2048]{1,0:T(8,128)(2,1)}, bf16[128,2048]{1,0:T(8,128)(2,1)S(1)}, u32[]{:S(2)}, u32[]{:S(2)}) collective-permute-start(bf16[128,2048]{1,0:T(8,128)(2,1)} %get-tuple-element.104.mine), channel_id=1, source_target_pairs={{0,1},{1,0},{2,3},{3,2},{4,5},{5,4},{6,7},{7,6},{8,9},{9,8},{10,11... | collective-permute-start | bytes 1572872 | tf_op jit(solution)/shard_map/ppermute | solution.py:58
  171.4 41.1 %collective-permute-start.12 = (bf16[128,7168]{1,0:T(8,128)(2,1)}, bf16[128,7168]{1,0:T(8,128)(2,1)S(1)}, u32[]{:S(2)}, u32[]{:S(2)}) collective-permute-start(bf16[128,7168]{1,0:T(8,128)(2,1)} %shard_map.278.refs_0_), channel_id=1, source_target_pairs={{0,64},{64,0},{1,65},{65,1},{2,66},{66,2},{3,67},{67,3},{4,68},{68... | collective-permute-start | bytes 5505032 | tf_op jit(solution)/shard_map/ppermute | solution.py:50
  183.6 20.6 %all-to-all-start.2 = ((bf16[32,8,1792]{2,1,0:T(8,128)(2,1)}), bf16[32,8,1792]{2,1,0:T(8,128)(2,1)S(1)}, u32[]{:S(2)}, u32[]{:S(2)}) async-start(bf16[32,8,1792]{2,1,0:T(8,128)(2,1)} %bitcast.54), calls=%async_computation.2 | async-start | bytes 1835008 | tf_op jit(solution)/shard_map/all_to_all | solution.py:690
  213.8 38.6 %collective-permute-start.28 = (bf16[128,7168]{1,0:T(8,128)(2,1)}, bf16[128,7168]{1,0:T(8,128)(2,1)S(1)}, u32[]{:S(2)}, u32[]{:S(2)}) collective-permute-start(bf16[128,7168]{1,0:T(8,128)(2,1)} %get-tuple-element.117.own.refs_6_), channel_id=1, source_target_pairs={{0,2},{2,0},{4,6},{6,4},{8,10},{10,8},{12,14},{14,12},{16,18},{18,... | collective-permute-start | bytes 5505032 | tf_op jit(solution)/shard_map/ppermute | solution.py:62
  213.8 38.6 %collective-permute-start.29 = (bf16[128,7168]{1,0:T(8,128)(2,1)}, bf16[128,7168]{1,0:T(8,128)(2,1)}, u32[]{:S(2)}, u32[]{:S(2)}) collective-permute-start(bf16[128,7168]{1,0:T(8,128)(2,1)} %get-tuple-element.118.theirs.refs_7_), channel_id=1, source_target_pairs={{0,2},{2,0},{4,6},{6,4},{8,10},{10,8},{12,14},{14,12},{16,18},{18,... | collective-permute-start | bytes 5505032 | tf_op jit(solution)/shard_map/ppermute | solution.py:62
  214.3 31.1 %collective-permute-start.15 = (bf16[128,4864]{1,0:T(8,128)(2,1)}, bf16[128,4864]{1,0:T(8,128)(2,1)}, u32[]{:S(2)}, u32[]{:S(2)}) collective-permute-start(bf16[128,4864]{1,0:T(8,128)(2,1)} %get-tuple-element.123), channel_id=1, source_target_pairs={{0,64},{64,0},{1,65},{65,1},{2,66},{66,2},{3,67},{67,3},{4,68},{68... | collective-permute-start | bytes 3735560 | tf_op jit(solution)/shard_map/ppermute | solution.py:50
  217.3 45.7 %all-to-all-start.3 = ((bf16[32,8,1792]{2,1,0:T(8,128)(2,1)}), bf16[32,8,1792]{2,1,0:T(8,128)(2,1)S(1)}, u32[]{:S(2)}, u32[]{:S(2)}) async-start(bf16[32,8,1792]{2,1,0:T(8,128)(2,1)} %shard_map.281.refs_2_.refs_0_), calls=%async_computation.3 | async-start | bytes 1835008 | tf_op jit(solution)/shard_map/all_to_all | solution.py:692
  224.8 179.0 %reduce-scatter.4.cloned.1.call-start = ((), (), s32[]{:S(2)}) async-start(), calls=%async_computation.8 | async-start | bytes 7798784
  250.3 2.1 collective-permute-start.27
  267.3 2.4 collective-permute-start.25
  267.5 3.3 collective-permute-start.26
  276.4 64.6 %all-to-all-start.4 = ((bf16[16,32,2816]{2,1,0:T(8,128)(2,1)}), bf16[16,32,2816]{2,1,0:T(8,128)(2,1)S(1)}, u32[]{:S(2)}, u32[]{:S(2)}) async-start(bf16[16,32,2816]{2,1,0:T(8,128)(2,1)} %bitcast.47), calls=%async_computation.4 | async-start | bytes 5767168 | tf_op jit(solution)/shard_map/all_to_all | solution.py:610
  283.6 19.6 %collective-permute-start.16 = (bf16[128,2816]{1,0:T(8,128)(2,1)}, bf16[128,2816]{1,0:T(8,128)(2,1)S(1)}, u32[]{:S(2)}, u32[]{:S(2)}) collective-permute-start(bf16[128,2816]{1,0:T(8,128)(2,1)} %shard_map.287.refs_2_.key_value), channel_id=1, source_target_pairs={{0,64},{64,0},{1,65},{65,1},{2,66},{66,2},{3,67},{67,3},{4,68},{68... | collective-permute-start | bytes 2162696 | tf_op jit(solution)/shard_map/ppermute | solution.py:50
  286.9 50.3 %collective-permute-start.20 = (bf16[128,2816]{1,0:T(8,128)(2,1)}, bf16[128,2816]{1,0:T(8,128)(2,1)S(1)}, u32[]{:S(2)}, u32[]{:S(2)}) collective-permute-start(bf16[128,2816]{1,0:T(8,128)(2,1)} %shard_map.287.refs_2_.key_value), channel_id=1, source_target_pairs={{0,2},{2,0},{4,6},{6,4},{8,10},{10,8},{12,14},{14,12},{16,18},{18,... | collective-permute-start | bytes 2162696 | tf_op jit(solution)/shard_map/ppermute | solution.py:62
  303.1 37.9 %collective-permute-start.21 = (bf16[128,2816]{1,0:T(8,128)(2,1)S(1)}, bf16[128,2816]{1,0:T(8,128)(2,1)}, u32[]{:S(2)}, u32[]{:S(2)}) collective-permute-start(bf16[128,2816]{1,0:T(8,128)(2,1)S(1)} %collective-permute-done.16.key_value_theirs.refs_3_), channel_id=1, source_target_pairs={{0,2},{2,0},{4,6},{6,4},{8,10},{10,8},{12,14},{14,12},{16,18},{18,... | collective-permute-start | bytes 2162696 | tf_op jit(solution)/shard_map/ppermute | solution.py:62
  313.0 9.4 %collective-permute-start.17 = (bf16[128,1024]{1,0:T(8,128)(2,1)}, bf16[128,1024]{1,0:T(8,128)(2,1)S(1)}, u32[]{:S(2)}, u32[]{:S(2)}) collective-permute-start(bf16[128,1024]{1,0:T(8,128)(2,1)} %get-tuple-element.129.mine), channel_id=1, source_target_pairs={{0,1},{1,0},{2,3},{3,2},{4,5},{5,4},{6,7},{7,6},{8,9},{9,8},{10,11... | collective-permute-start | bytes 786440 | tf_op jit(solution)/shard_map/ppermute | solution.py:58
  314.6 14.7 %collective-permute-start.19 = (bf16[128,1024]{1,0:T(8,128)(2,1)}, bf16[128,1024]{1,0:T(8,128)(2,1)S(1)}, u32[]{:S(2)}, u32[]{:S(2)}) collective-permute-start(bf16[128,1024]{1,0:T(8,128)(2,1)} %get-tuple-element.130), channel_id=1, source_target_pairs={{0,65},{1,64},{64,1},{65,0},{2,67},{3,66},{66,3},{67,2},{4,69},{5,... | collective-permute-start | bytes 786440 | tf_op jit(solution)/shard_map/ppermute | solution.py:814
  316.7 12.5 %collective-permute-start.18 = (bf16[128,1024]{1,0:T(8,128)(2,1)}, bf16[128,1024]{1,0:T(8,128)(2,1)S(1)}, u32[]{:S(2)}, u32[]{:S(2)}) collective-permute-start(bf16[128,1024]{1,0:T(8,128)(2,1)} %get-tuple-element.130), channel_id=1, source_target_pairs={{0,64},{64,0},{1,65},{65,1},{2,66},{66,2},{3,67},{67,3},{4,68},{68... | collective-permute-start | bytes 786440 | tf_op jit(solution)/shard_map/ppermute | solution.py:50
  322.5 6.8 %copy-start.26 = (bf16[128,1024]{1,0:T(8,128)(2,1)}, bf16[128,1024]{1,0:T(8,128)(2,1)S(1)}, u32[]{:S(2)}) copy-start(bf16[128,1024]{1,0:T(8,128)(2,1)S(1)} %collective-permute-done.17.theirs) | copy-start | bytes 786436
  333.6 3.7 collective-permute-start.23
  333.6 5.1 %collective-permute-start.24 = (bf16[16,1024]{1,0:T(8,128)(2,1)}, bf16[16,1024]{1,0:T(8,128)(2,1)S(1)}, u32[]{:S(2)}, u32[]{:S(2)}) collective-permute-start(bf16[16,1024]{1,0:T(8,128)(2,1)} %get-tuple-element.138), channel_id=1, source_target_pairs={{0,66},{2,64},{4,70},{6,68},{8,74},{10,72},{12,78},{14,76},{16,82}... | collective-permute-start | bytes 98312 | tf_op jit(solution)/shard_map/ppermute | solution.py:821
  335.4 5.6 %collective-permute-start.22 = (bf16[16,1024]{1,0:T(8,128)(2,1)}, bf16[16,1024]{1,0:T(8,128)(2,1)S(1)}, u32[]{:S(2)}, u32[]{:S(2)}) collective-permute-start(bf16[16,1024]{1,0:T(8,128)(2,1)} %get-tuple-element.138), channel_id=1, source_target_pairs={{0,64},{64,0},{1,65},{65,1},{2,66},{66,2},{3,67},{67,3},{4,68},{68... | collective-permute-start | bytes 98312 | tf_op jit(solution)/shard_map/ppermute | solution.py:50
  337.2 3.8 copy-start.29
  348.7 43.4 %all-to-all-start.5 = ((bf16[16,32,2816]{2,1,0:T(8,128)(2,1)}), bf16[16,32,2816]{2,1,0:T(8,128)(2,1)S(1)}, u32[]{:S(2)}, u32[]{:S(2)}) async-start(bf16[16,32,2816]{2,1,0:T(8,128)(2,1)} %bitcast.48), calls=%async_computation.5 | async-start | bytes 5767168 | tf_op jit(solution)/shard_map/all_to_all | solution.py:610
  360.9 26.4 %copy-start.1 = (bf16[16,32,2816]{2,1,0:T(8,128)(2,1)S(1)}, bf16[16,32,2816]{2,1,0:T(8,128)(2,1)}, u32[]{:S(2)}) copy-start(bf16[16,32,2816]{2,1,0:T(8,128)(2,1)} %copy-done) | copy-start | bytes 8650756
  360.9 12.3 %collective-permute-start.13 = (bf16[256,1024]{1,0:T(8,128)(2,1)}, bf16[256,1024]{1,0:T(8,128)(2,1)S(1)}, u32[]{:S(2)}, u32[]{:S(2)}) collective-permute-start(bf16[256,1024]{1,0:T(8,128)(2,1)} %shard_map.283.mine), channel_id=1, source_target_pairs={{0,1},{1,0},{2,3},{3,2},{4,5},{5,4},{6,7},{7,6},{8,9},{9,8},{10,11... | collective-permute-start | bytes 1572872 | tf_op jit(solution)/shard_map/ppermute | solution.py:58
  376.2 8.1 %collective-permute-start.14 = (bf16[128,1024]{1,0:T(8,128)(2,1)}, bf16[128,1024]{1,0:T(8,128)(2,1)S(1)}, u32[]{:S(2)}, u32[]{:S(2)}) collective-permute-start(bf16[128,1024]{1,0:T(8,128)(2,1)} %get-tuple-element.120), channel_id=1, source_target_pairs={{0,64},{64,0},{1,65},{65,1},{2,66},{66,2},{3,67},{67,3},{4,68},{68... | collective-permute-start | bytes 786440 | tf_op jit(solution)/shard_map/ppermute | solution.py:50
  (23 other events, 25.4 us)
Sparse Core Ops, SparseCore 0:
  39.0 71.2 all-gather.1
  264.1 139.6 reduce-scatter.3

commit v2 on v1

--- a/solution.py
+++ b/solution.py
@@ -312,8 +312,8 @@
 
 
 def mlp_kernel(
-    shard, tokens, mine, theirs, gain, bias, base_hidden, helped_hidden, mixed, gate_weight, up_weight, others, _up, _low,
-    middle, normed, inverse, low_own, low_oth, grads, part,
+    shard, tokens, mine, theirs, gain, bias, base_hidden, helped_hidden, gate_weight, up_weight, others, _up, _low,
+    middle, normed, inverse, low_own, grads, part,
     near_gate, near_up, far_gate, far_up, semaphores,
 ):
     copies = fetch(
@@ -332,15 +332,16 @@
     normed[:, HALF:] = oth
     inverse[...] = jnp.broadcast_to(scale, inverse.shape)
     low_own[...] = (own * gains[0] + biases[0]).astype(BF)
-    low_oth[...] = (oth * gains[1] + biases[1]).astype(BF)
+    low_oth = (oth * gains[1] + biases[1]).astype(BF)
+    grads[:, 3 * VPAD :] = low_oth
     copies[0].wait()
     up_gate = product_right(low_own[...], near_gate[...])
     copies[1].wait()
-    up_gate += product(low_oth[...], far_gate[:, :VW])
+    up_gate += product(low_oth, far_gate[:, :VW])
     copies[2].wait()
     up_vals = product_right(low_own[...], near_up[...])
     copies[3].wait()
-    up_vals += product(low_oth[...], far_up[:, :VW])
+    up_vals += product(low_oth, far_up[:, :VW])
     grad_hidden = base_hidden[...] + helped_hidden[...].astype(F32)
     sigma = jax.nn.sigmoid(up_gate)
     silu = up_gate * sigma
@@ -350,7 +351,6 @@
     ):
         grads[:, k * VPAD : k * VPAD + VW] = array.astype(BF)
         grads[:, k * VPAD + VW : (k + 1) * VPAD] = none
-    grads[:, 3 * VPAD :] = mixed[...]
     total = product(grads[:, VPAD : VPAD + VW], near_gate[...])
     total += product(grads[:, 2 * VPAD : 2 * VPAD + VW], near_up[...])
     part[:, :HALF] = total.astype(BF)
@@ -428,7 +428,7 @@
 
 
 def back_kernel(
-    rates, seg_column, seg_row, queries, keys, values, masked, incoming, grad_retained, grad_gate, gb, low2,
+    rates, seg_column, seg_row, queries, keys, values, masked, incoming, grad_retained, grad_gate, gb, mixed,
     gate_query, parcel, base_key, base_value,
 ):
     before = mark(incoming[:16].astype(F32), 0)[:1]
@@ -448,12 +448,11 @@
         gate_query[:, VPAD + head * KH : VPAD + (head + 1) * KH] = grad_query.astype(BF)
         base_key[:, own] = product_left(grad_scores, queries[:, own])
         base_value[:, begin:end] += product_left(masked[head], grad)
-    parcel[:, :HALF] = gb[...]
-    parcel[:, HALF : 2 * HALF] = low2[...]
-    parcel[:, 2 * HALF :] = gate_query[...]
-
-
-def later_kernel(rates, seg_column, seg_row, keys, values, outgoing, base_key, base_value, out, total):
+    parcel[:, :VPAD] = mixed[...]
+    parcel[:, VPAD:] = gb[...]
+
+
+def later_kernel(rates, seg_column, seg_row, keys, values, outgoing, base_key, base_value, _theirs, _early, out, total):
     total[...] = base_value[...]
     for head in range(HEADS):
         begin, end = window(head)
@@ -471,7 +470,7 @@
     part, helped,
 ):
     both = jnp.concatenate([gate_query[...], gate_query_theirs[...]], 0)
-    total = product_right(both[:, VPAD:], query_weight[...])
+    total = product_right(both[:, VPAD : VPAD + HALF], query_weight[...])
     total += product(both[:, :VW], gate_weight[...])
     both = jnp.concatenate([key_value[...], key_value_theirs[...]], 0)
     total += product_right(both[:, :HALF], key_weight[...])
@@ -514,14 +513,12 @@
             out[:, k * PIECE : (k + 1) * PIECE] = product_right(pick, refs[k][...]).astype(BF)
 
 
-def rows_more_kernel(core, low2, gb, sent, *refs):
-    kept, gone, gate_query = refs[-3:]
-    parts = [low2, sent.at[:, HALF : 2 * HALF], gb, sent.at[:, :HALF]]
+def rows_cut_kernel(start, core, own, sent, *refs):
+    kept, gone = refs[-2:]
     for chosen, out in ((core[0], kept), (1 - core[0], gone)):
         pick = rows_of(chosen)
-        for k in range(4):
-            out[:, k * PIECE : (k + 1) * PIECE] = product_right(pick, parts[k][...]).astype(BF)
-    gate_query[...] = sent[:, 2 * HALF :]
+        out[:, :PIECE] = product_right(pick, own[...]).astype(BF)
+        out[:, PIECE:] = product_right(pick, sent[:, start : start + HALF]).astype(BF)
 
 
 def features_of(core, own, received):
@@ -530,20 +527,21 @@
     return kept, core_swap(gone)
 
 
+def features_in(core, own, sent, start, *later):
+    both = shape(HALF // 2, 2 * PIECE)
+    kept, gone = run(functools.partial(rows_cut_kernel, start), (both, both), [core], [own, sent], later)
+    return kept, core_swap(gone)
+
+
 def all_tokens(array, other):
     return (array, other, core_swap(array), core_swap(other))
 
 
-CHUNK = 896
-
-
-def outer(features, groups, plan, chunk=CHUNK, vectors=None, core=None, later=()):
+def outer(features, groups, plan, chunk, width, vectors=None, core=None, later=(), flops=0):
     steps = len(plan)
-    flat = [a for kept, got, _ in features for a in (kept, got)]
+    flat = [a for pair in features for a in pair]
     flat += [a for group in groups for a in group] + list(vectors or ())
-    specs = []
-    for _, _, block in features:
-        specs += [pl.BlockSpec((HALF // 2, 2 * PIECE), lambda i, c, block=block: (0, block))] * 2
+    specs = [pl.BlockSpec((HALF // 2, 2 * PIECE), lambda i, c: (0, 0))] * (2 * len(features))
     for g in range(len(groups)):
         mine = [k for k in range(steps) if plan[k][1] == g]
         first, count, block = mine[0], len(mine), plan[mine[0]][2]
@@ -593,7 +591,7 @@
         core = jnp.zeros((1,), jnp.int32)
     part = pl.pallas_call(
         kernel,
-        out_shape=shape(HALF // 2, steps * chunk),
+        out_shape=shape(HALF // 2, width),
         grid_spec=pltpu.PrefetchScalarGridSpec(
             num_scalar_prefetch=1,
             grid=(steps,),
@@ -601,9 +599,18 @@
             out_specs=pl.BlockSpec((HALF // 2, chunk), lambda i, c: (0, i)),
         ),
         compiler_params=pltpu.CompilerParams(vmem_limit_bytes=56 * 1024 * 1024),
-        cost_estimate=pl.CostEstimate(flops=0, bytes_accessed=0, transcendentals=0),
+        cost_estimate=pl.CostEstimate(flops=flops, bytes_accessed=0, transcendentals=0),
     )(core, *flat)
-    return part.reshape(16, BLOCK, steps * chunk)
+    return part.reshape(16, BLOCK, width)
+
+
+def sum_kernel(parts, key, value, norms):
+    total = parts[0].astype(F32)
+    for k in range(1, 16):
+        total += parts[k].astype(F32)
+    key[...] = total[:, :HALF]
+    value[...] = total[:, HALF : HALF + VW]
+    norms[...] = total[:, HALF + VPAD - 128 :]
 
 
 def sent(part):
@@ -724,11 +731,11 @@
         [pltpu.VMEM((PIECE, VPAD), F32), held, weight, dma(2)],
     )
     theirs = from_tp(part)
-    middle, normed2, inverse2, low2_own, low2_oth, mlp_parts, part = run(
+    middle, normed2, inverse2, low2_own, mlp_parts, part = run(
         mlp_kernel,
-        (shape(PIECE, WIDE, kind=F32), shape(PIECE, WIDE, kind=F32), scale, small, small, shape(PIECE, 4 * VPAD), wide),
+        (shape(PIECE, WIDE, kind=F32), shape(PIECE, WIDE, kind=F32), scale, small, shape(PIECE, 3 * VPAD + HALF), wide),
         [shard],
-        [tokens, part, theirs, gain2, bias2, base_hidden, helped_hidden, mixed],
+        [tokens, part, theirs, gain2, bias2, base_hidden, helped_hidden],
         [mlp_gate_turned, mlp_up_turned, others, up_features[1], low1_features[1]],
         [weight, weight, held, held, dma(4)],
     )
@@ -757,36 +764,39 @@
         back_kernel,
         (
             shape(PIECE, VPAD + HALF),
-            shape(PIECE, 2 * HALF + VPAD + HALF),
+            shape(PIECE, VPAD + HALF),
             shape(PIECE, HALF, kind=F32),
             shape(PIECE, VPAD, kind=F32),
         ),
         [decay_rate],
-        [seg_column, seg_row, queries, keys, values, masked, incoming, grad_retained, grad_gate, gb_oth, low2_oth],
-    )
-    parcel = from_shard(parcel)
+        [seg_column, seg_row, queries, keys, values, masked, incoming, grad_retained, grad_gate, gb_oth, mixed],
+    )
+    parcel_theirs = from_shard(parcel)
+    gate_query_theirs = from_shard(gate_query)
     outgoing, _, scanned = exchange(term, True, gate_query)
+    mlp_parts, mlp_theirs = hold((mlp_parts, mlp_theirs), scanned)
+    mlp_all = all_tokens(mlp_parts, mlp_theirs)
+    early_part = outer(
+        [
+            up_features,
+            features_in(core, low2_own, mlp_theirs, 3 * VPAD),
+            features_in(core, gb_own, parcel_theirs, VPAD, scanned),
+        ],
+        [mlp_all, all_tokens(parcel, parcel_theirs)],
+        [(0, 0, 0), (1, 0, 1), (1, 0, 2), (2, 1, 0)],
+        VPAD,
+        4 * VPAD,
+    )
     key_value = run(
         later_kernel,
         shape(PIECE, HALF + VPAD),
         [decay_rate],
         [seg_column, seg_row, keys, values, outgoing, base_key_grad, base_value_grad],
+        [gate_query_theirs, early_part],
         scratch=[pltpu.VMEM((PIECE, VPAD), F32)],
     )
     key_value_theirs = from_shard(key_value)
 
-    mlp_parts, mlp_theirs = hold((mlp_parts, mlp_theirs), scanned)
-    both = shape(HALF // 2, 4 * PIECE)
-    kept, gone, gate_query_theirs = run(
-        rows_more_kernel, (both, both, shape(PIECE, VPAD + HALF)), [core], [low2_own, gb_own, parcel], [scanned]
-    )
-    got = core_swap(gone)
-    early_part = outer(
-        [(*up_features, 0), (kept, got, 0), (kept, got, 1)],
-        [all_tokens(mlp_parts, mlp_theirs)],
-        [(0, 0, 0), (1, 0, 1), (1, 0, 2), (2, 0, 3)],
-        VPAD,
-    )
     early = lax.psum_scatter(
         after(early_part, outgoing), "ctx", scatter_dimension=0, axis_index_groups=PLANE, tiled=False
     )
@@ -794,10 +804,12 @@
     gate_query, gate_query_theirs = hold((gate_query, gate_query_theirs), key_value)
     gate_query_parts = sent(
         outer(
-            [(*low1_features, 0)],
+            [low1_features],
             [all_tokens(gate_query, gate_query_theirs)],
             [(0, 0, 0), (0, 0, 1)],
             (VPAD + HALF) // 2,
+            VPAD + HALF,
+            flops=40 * 10**9,
         )
     )
     first_weights = [query_weight, key_weight, value_turned, gate_turned]
@@ -822,10 +834,11 @@
     )
     key_value_parts = sent(
         outer(
-            [(*low1_features, 0)],
+            [low1_features],
             [all_tokens(key_value, key_value_theirs)],
             [(0, 0, 0), (0, 0, 1)],
             (HALF + VPAD) // 2,
+            HALF + VPAD,
             vectors=sums,
             core=core,
             later=(gate_query_parts,),
@@ -838,8 +851,14 @@
     )
     layer_out = run(result_kernel, wide, [shard], [middle, down_own, from_shard(down_gone)])
 
-    gate_query_sums, key_value_sums = added(gate_query_parts), added(key_value_parts)
-    norms = key_value_sums[:, HALF + VW : HALF + VW + 4].T
+    gate_query_sums = added(gate_query_parts)
+    key_sums, value_sums, norms = run(
+        sum_kernel,
+        (shape(BLOCK, HALF, kind=F32), shape(BLOCK, VW, kind=F32), shape(BLOCK, 128, kind=F32)),
+        [],
+        [key_value_parts],
+    )
+    norms = norms[:, 64:68].T
     early = [early[:, k * VPAD : k * VPAD + VW] for k in range(4)]
     return (
         layer_out[None],
@@ -847,8 +866,8 @@
         norms[0],
         norms[1],
         gate_query_sums[:, VPAD:],
-        key_value_sums[:, :HALF],
-        key_value_sums[:, HALF : HALF + VW],
+        key_sums,
+        value_sums,
         gate_query_sums[:, :VW],
         early[3].T,
         norms[2],

time: 421 us -> 435 us (1.033)
  the two profiles are of different devices: /device:TPU:8 before, /device:TPU:86 now
where the time goes in v2:
time: 435 us; the launch traced here: 427 us
  waiting for transfers between devices  154 us (35%)
  Pallas kernels  137 us (31%)
  starting transfers between devices  80.9 us (19%)
  local copies, waits for them, and re-layouts  31.3 us (7%)
  between operations  14.8 us (3%)
  other arithmetic  8.03 us (2%)
    pallas_call x25, Pallas kernels, run(): pl.pallas_call(kernel, out_shape=outs, grid=(1,), in_specs=[SMEM] * len(s...  118 us
    ppermute x10, waiting for transfers between devices, from_shard(): return lax.ppermute(part, 'shard', SWAP)  71.3 us
    ppermute x4, waiting for transfers between devices, from_tp(): return lax.ppermute(part, 'tp', SWAP)  33 us
    unnamed x79, local copies, waits for them, and re-layouts  26.8 us
    ppermute x5, waiting for transfers between devices, half_from_shard(): return lax.ppermute(part.astype(F16), 'shard', SWAP).astype(F32)  20.8 us
    pallas_call x3, Pallas kernels, outer(): pl.pallas_call(kernel, out_shape=shape(HALF // 2, width), grid_spec=pltpu...  19.6 us
    ppermute x10, starting transfers between devices, from_shard(): return lax.ppermute(part, 'shard', SWAP)  18.9 us
    all_to_all x2, starting transfers between devices, exchange(): lax.all_to_all(done, 'ctx', 0, 0, tiled=True).reshape(KH, VPAD)  15.1 us
  transfers between devices with their start and end apart: 42, of which 22 were waited for; matrix products, arithmetic and copies ran while one was open for 4% of the time, Pallas kernels for 26%

profile of v2, /device:TPU:86, one launch (start us, length us, event | category | flops | bytes accessed | tf_op | source)
XLA Modules:
  0.0 426.8 jit_solution(15462735470099687923)
XLA Ops:
  7.2 3.9 shard_map.263
  12.7 8.4 %collective-permute-done.low.refs_1_ = bf16[128,1024]{1,0:T(8,128)(2,1)S(1)} collective-permute-done((bf16[128,1024]{1,0:T(8,128)(2,1)}, bf16[128,1024]{1,0:T(8,128)(2,1)S(1)}, u32[]{:S(2)}, u32[]{:S(2)}) %collective-permute-start) | collective-permute-done | bytes 262176 | tf_op jit(solution)/shard_map/ppermute | solution.py:50
  27.2 5.2 %shard_map.264 = (f32[128,1024]{1,0:T(8,128)}, f32[128,1728]{1,0:T(8,128)}) custom-call(bf16[128,1024]{1,0:T(8,128)(2,1)} %copy-done.8, bf16[1024,1024]{1,0:T(8,128)(2,1)} %key_weight.5, bf16[1728,1024]{1,0:T(8,128)(2,1)} %bitcast.35), custom_call_target="tpu_custom_call" | custom-call | tf_op jit(solution)/shard_map/pallas_call | solution.py:76
  32.4 5.6 %collective-permute-done.5.theirs.refs_2_.refs_1_ = bf16[128,1024]{1,0:T(8,128)(2,1)S(1)} collective-permute-done((bf16[128,1024]{1,0:T(8,128)(2,1)}, bf16[128,1024]{1,0:T(8,128)(2,1)S(1)}, u32[]{:S(2)}, u32[]{:S(2)}) %collective-permute-start.5) | collective-permute-done | bytes 262176 | tf_op jit(solution)/shard_map/ppermute | solution.py:50
  45.1 8.2 %shard_map.265 = (f32[128,1024]{1,0:T(8,128)}, f32[128,1024]{1,0:T(8,128)}, f32[128,1728]{1,0:T(8,128)}, f32[128,1728]{1,0:T(8,128)}) custom-call(bf16[128,1024]{1,0:T(8,128)(2,1)} %get-tuple-element.81.low.refs_0_, bf16[1024,1024]{1,0:T(8,128)(2,1)} %query_weight.5, bf16[1024,1024]{1,0:T(8,128)(2,1)} %key_weight.5, bf16[1728,1024]{1,0:T(8,128)(2,1)} %bitcast.36, ...), custom_call_target="tpu_custom_call" | custom-call | tf_op jit(solution)/shard_map/pallas_call | solution.py:76
  53.3 5.3 %shard_map.266 = (f32[128,1024]{1,0:T(8,128)}, f32[128,1728]{1,0:T(8,128)}) custom-call(bf16[128,1024]{1,0:T(8,128)(2,1)} %copy-done.8, bf16[1024,1024]{1,0:T(8,128)(2,1)} %query_weight.5, bf16[1728,1024]{1,0:T(8,128)(2,1)} %bitcast.39), custom_call_target="tpu_custom_call" | custom-call | tf_op jit(solution)/shard_map/pallas_call | solution.py:76
  60.5 3.6 shard_map.267
  64.1 7.6 %all-to-all-start = ((bf16[32,8,1792]{2,1,0:T(8,128)(2,1)}), bf16[32,8,1792]{2,1,0:T(8,128)(2,1)S(1)}, u32[]{:S(2)}, u32[]{:S(2)}) async-start(bf16[32,8,1792]{2,1,0:T(8,128)(2,1)} %bitcast.54), calls=%async_computation | async-start | bytes 1835008 | tf_op jit(solution)/shard_map/all_to_all | solution.py:697
  75.5 4.5 %shard_map.270 = (f32[128,1728]{1,0:T(8,128)}, f32[128,1728]{1,0:T(8,128)}) custom-call(bf16[128,1024]{1,0:T(8,128)(2,1)} %get-tuple-element.95.own.refs_0_.up_own, bf16[128,1024]{1,0:T(8,128)(2,1)} %copy-done.14, bf16[1728,1024]{1,0:T(8,128)(2,1)} %weight.3), custom_call_target="tpu_custom_call" | custom-call | tf_op jit(solution)/shard_map/pallas_call | solution.py:76
  80.0 11.5 %collective-permute-done.1 = f16[128,1024]{1,0:T(8,128)(2,1)S(1)} collective-permute-done((f16[128,1024]{1,0:T(8,128)(2,1)S(1)}, f16[128,1024]{1,0:T(8,128)(2,1)S(1)}, u32[]{:S(2)}, u32[]{:S(2)}) %collective-permute-start.1) | collective-permute-done | bytes 262176 | tf_op jit(solution)/shard_map/ppermute | solution.py:54
  94.3 2.6 shard_map.271
  96.9 7.6 %all-to-all-start.1 = ((bf16[32,8,1792]{2,1,0:T(8,128)(2,1)}), bf16[32,8,1792]{2,1,0:T(8,128)(2,1)S(1)}, u32[]{:S(2)}, u32[]{:S(2)}) async-start(bf16[32,8,1792]{2,1,0:T(8,128)(2,1)} %shard_map.271), calls=%async_computation.1 | async-start | bytes 1835008 | tf_op jit(solution)/shard_map/all_to_all | solution.py:699
  106.2 3.3 shard_map.268
  109.6 9.3 %collective-permute-done.7 = f16[128,1728]{1,0:T(8,128)(2,1)S(1)} collective-permute-done((f16[128,1728]{1,0:T(8,128)(2,1)S(1)}, f16[128,1728]{1,0:T(8,128)(2,1)S(1)}, u32[]{:S(2)}, u32[]{:S(2)}) %collective-permute-start.7) | collective-permute-done | bytes 442400 | tf_op jit(solution)/shard_map/ppermute | solution.py:54
  120.8 7.4 %shard_map.274 = (f32[128,1728]{1,0:T(8,128)}, f32[128,1792]{1,0:T(8,128)}, f32[128,128]{1,0:T(8,128)}, bf16[128,1792]{1,0:T(8,128)(2,1)}, bf16[128,2048]{1,0:T(8,128)(2,1)}) custom-call(f32[4]{0:T(128)} %rates.15, f32[128,1]{1,0:T(8,128)} %copy.52.seg_column, bf16[128,1024]{1,0:T(8,128)(2,1)} %get-tuple-element.91.queries, ...), custom_call_target="tpu_custom_call" | custom-call | tf_op jit(solution)/shard_map/pallas_call | solution.py:76
  129.1 3.0 shard_map.275
  132.1 3.0 shard_map.276
  137.0 4.6 %collective-permute-done.8.theirs = bf16[128,2048]{1,0:T(8,128)(2,1)S(1)} collective-permute-done((bf16[128,2048]{1,0:T(8,128)(2,1)}, bf16[128,2048]{1,0:T(8,128)(2,1)S(1)}, u32[]{:S(2)}, u32[]{:S(2)}) %collective-permute-start.8) | collective-permute-done | bytes 524320 | tf_op jit(solution)/shard_map/ppermute | solution.py:58
  142.5 13.8 %shard_map.277 = (f32[128,2048]{1,0:T(8,128)}, f32[128,2048]{1,0:T(8,128)}, f32[128,128]{1,0:T(8,128)}, bf16[128,1024]{1,0:T(8,128)(2,1)}, bf16[128,6400]{1,0:T(8,128)(2,1)}, /*index=5*/bf16[128,2048]{1,0:T(8,128)(2,1)}) custom-call(s32[1]{0:T(128)} %bitcast.shard, bf16[128,2048]{1,0:T(8,128)(2,1)} %bitcast.53, bf16[128,2048]{1,0:T(8,128)(2,1)} %get-tuple-element.100.mine, ...), custom_call_target="tpu_custom_call" | custom-call | tf_op jit(solution)/shard_map/pallas_call | solution.py:76
  157.4 11.6 %collective-permute-done.11.refs_1_.theirs = bf16[128,2048]{1,0:T(8,128)(2,1)S(1)} collective-permute-done((bf16[128,2048]{1,0:T(8,128)(2,1)}, bf16[128,2048]{1,0:T(8,128)(2,1)S(1)}, u32[]{:S(2)}, u32[]{:S(2)}) %collective-permute-start.11) | collective-permute-done | bytes 524320 | tf_op jit(solution)/shard_map/ppermute | solution.py:58
  171.2 9.4 %shard_map.279 = (f32[128,2048]{1,0:T(8,128)}, bf16[128,1024]{1,0:T(8,128)(2,1)}, bf16[128,1024]{1,0:T(8,128)(2,1)}, f32[8,2048]{1,0:T(8,128)}, bf16[128,1792]{1...) custom-call(s32[1]{0:T(128)} %bitcast.shard, f32[4]{0:T(128)} %rates.15, ...), custom_call_target="tpu_custom_call" | custom-call | tf_op jit(solution)/shard_map/pallas_call | solution.py:76
  180.6 7.4 %all-to-all-start.2 = ((bf16[32,8,1792]{2,1,0:T(8,128)(2,1)}), bf16[32,8,1792]{2,1,0:T(8,128)(2,1)S(1)}, u32[]{:S(2)}, u32[]{:S(2)}) async-start(bf16[32,8,1792]{2,1,0:T(8,128)(2,1)} %bitcast.55), calls=%async_computation.2 | async-start | bytes 1835008 | tf_op jit(solution)/shard_map/all_to_all | solution.py:697
  188.0 5.0 %shard_map.280 = (bf16[128,2816]{1,0:T(8,128)(2,1)}, bf16[128,2816]{1,0:T(8,128)(2,1)}, f32[128,1024]{1,0:T(8,128)}, f32[128,1792]{1,0:T(8,128)}) custom-call(f32[4]{0:T(128)} %rates.15, f32[128,1]{1,0:T(8,128)} %copy.52.seg_column, f32[1,128]{1,0:T(1,128)} %get-tuple-element.156.seg_row, bf16[128,1024]{1,0:T(8,128)(2,1)} %get-tuple-element.91.queries, ...), custom_call_target="tpu_custom_call" | custom-call | tf_op jit(solution)/shard_map/pallas_call | solution.py:76
  192.9 6.7 %all-to-all-done.2.states = bf16[32,8,1792]{2,1,0:T(8,128)(2,1)S(1)} async-done(((bf16[32,8,1792]{2,1,0:T(8,128)(2,1)}), bf16[32,8,1792]{2,1,0:T(8,128)(2,1)S(1)}, u32[]{:S(2)}, u32[]{:S(2)}) %all-to-all-start.2) | async-done | bytes 917536 | tf_op jit(solution)/shard_map/all_to_all | solution.py:697
  203.0 3.6 collective-permute-done.12.refs_1_
  209.9 7.5 %all-to-all-start.3 = ((bf16[32,8,1792]{2,1,0:T(8,128)(2,1)}), bf16[32,8,1792]{2,1,0:T(8,128)(2,1)S(1)}, u32[]{:S(2)}, u32[]{:S(2)}) async-start(bf16[32,8,1792]{2,1,0:T(8,128)(2,1)} %shard_map.281.refs_2_.refs_0_), calls=%async_computation.3 | async-start | bytes 1835008 | tf_op jit(solution)/shard_map/all_to_all | solution.py:699
  217.4 10.7 %collective-permute-done.17.sent.refs_11_ = bf16[128,2816]{1,0:T(8,128)(2,1)S(1)} collective-permute-done((bf16[128,2816]{1,0:T(8,128)(2,1)}, bf16[128,2816]{1,0:T(8,128)(2,1)S(1)}, u32[]{:S(2)}, u32[]{:S(2)}) %collective-permute-start.17) | collective-permute-done | bytes 720928 | tf_op jit(solution)/shard_map/ppermute | solution.py:50
  229.0 3.2 shard_map.287
  232.2 3.5 shard_map.286
  238.8 9.4 %shard_map.288 = bf16[512,7168]{1,0:T(8,128)(2,1)} custom-call(s32[1]{0:T(128)} %constant.28.clone.1.core, bf16[512,256]{1,0:T(8,128)(2,1)} %get-tuple-element.125.refs_0_, bf16[512,256]{1,0:T(8,128)(2,1)} %copy-done.20, bf16[512,256]{1,0:T(8,128)(2,1)} %get-tuple-element.127.refs_2_, bf16[512,256]{1,0:T(8,128)(2,1)} %copy-done.28, ...), custom_call_target="tpu_custom_call" | custom-call | tf_op jit(solution)/shard_map/pallas_call | solution.py:592
  248.2 6.7 %copy.63.refs_0_ = bf16[16,32,7168]{2,1,0:T(8,128)(2,1)} copy(bf16[16,32,7168]{2,1,0:T(8,128)(2,1)} %bitcast.33) | data formatting | bytes 14680064
  258.7 18.4 %collective-permute-done.15._theirs.refs_1_ = bf16[128,2816]{1,0:T(8,128)(2,1)S(1)} collective-permute-done((bf16[128,2816]{1,0:T(8,128)(2,1)S(1)}, bf16[128,2816]{1,0:T(8,128)(2,1)S(1)}, u32[]{:S(2)}, u32[]{:S(2)}) %collective-permute-start.15) | collective-permute-done | bytes 720928 | tf_op jit(solution)/shard_map/ppermute | solution.py:50
  277.9 3.7 shard_map.289.refs_2_.key_value
  285.9 4.8 %shard_map.293 = bf16[512,2816]{1,0:T(8,128)(2,1)} custom-call(s32[1]{0:T(128)} %constant.28.clone.1.core, bf16[512,256]{1,0:T(8,128)(2,1)} %get-tuple-element.142.refs_0_, bf16[512,256]{1,0:T(8,128)(2,1)} %copy-done.21, bf16[128,2816]{1,0:T(8,128)(2,1)} %get-tuple-element.133.gate_query.refs_2_, ...), custom_call_target="tpu_custom_call" | custom-call | flops 40000000000 | tf_op jit(solution)/shard_map/pallas_call | solution.py:592
  290.7 7.2 %all-to-all-start.4 = ((bf16[16,32,2816]{2,1,0:T(8,128)(2,1)}), bf16[16,32,2816]{2,1,0:T(8,128)(2,1)S(1)}, u32[]{:S(2)}, u32[]{:S(2)}) async-start(bf16[16,32,2816]{2,1,0:T(8,128)(2,1)} %bitcast.51), calls=%async_computation.4 | async-start | bytes 5767168 | tf_op jit(solution)/shard_map/all_to_all | solution.py:617
  299.4 17.9 %collective-permute-done.23.key_value_theirs.refs_3_ = bf16[128,2816]{1,0:T(8,128)(2,1)S(1)} collective-permute-done((bf16[128,2816]{1,0:T(8,128)(2,1)}, bf16[128,2816]{1,0:T(8,128)(2,1)S(1)}, u32[]{:S(2)}, u32[]{:S(2)}) %collective-permute-start.23) | collective-permute-done | bytes 720928 | tf_op jit(solution)/shard_map/ppermute | solution.py:50
  318.2 9.2 %shard_map.291 = (bf16[128,1024]{1,0:T(8,128)(2,1)}, bf16[128,1024]{1,0:T(8,128)(2,1)}) custom-call(bf16[128,2816]{1,0:T(8,128)(2,1)} %get-tuple-element.133.gate_query.refs_2_, bf16[128,2816]{1,0:T(8,128)(2,1)} %get-tuple-element.134.gate_query_theirs.refs_3_, bf16[128,2816]{1,0:T(8,128)(2,1)} %shard_map.289.refs_2_.key_value, ...), custom_call_target="tpu_custom_call" | custom-call | tf_op jit(solution)/shard_map/pallas_call | solution.py:76
  331.5 5.3 %collective-permute-done.24.theirs = bf16[128,1024]{1,0:T(8,128)(2,1)S(1)} collective-permute-done((bf16[128,1024]{1,0:T(8,128)(2,1)}, bf16[128,1024]{1,0:T(8,128)(2,1)S(1)}, u32[]{:S(2)}, u32[]{:S(2)}) %collective-permute-start.24) | collective-permute-done | bytes 262176 | tf_op jit(solution)/shard_map/ppermute | solution.py:58
  336.8 6.0 %collective-permute-done.26.helped_other = bf16[128,1024]{1,0:T(8,128)(2,1)S(1)} collective-permute-done((bf16[128,1024]{1,0:T(8,128)(2,1)}, bf16[128,1024]{1,0:T(8,128)(2,1)S(1)}, u32[]{:S(2)}, u32[]{:S(2)}) %collective-permute-start.26) | collective-permute-done | bytes 262176 | tf_op jit(solution)/shard_map/ppermute | solution.py:826
  343.6 3.6 shard_map.292
  347.8 3.2 collective-permute-start.29
  355.6 5.4 %shard_map.294 = bf16[512,2816]{1,0:T(8,128)(2,1)} custom-call(s32[1]{0:T(128)S(6)} %select_n.7.core, bf16[512,256]{1,0:T(8,128)(2,1)} %get-tuple-element.142.refs_0_, bf16[512,256]{1,0:T(8,128)(2,1)} %copy-done.21, bf16[128,2816]{1,0:T(8,128)(2,1)} %shard_map.289.refs_2_.key_value, bf16[128,2816]{1,0:T(8,128)(2,1)} %copy-done.12, ...), custom_call_target="tpu_custom_call" | custom-call | tf_op jit(solution)/shard_map/pallas_call | solution.py:592
  361.0 7.2 %all-to-all-start.5 = ((bf16[16,32,2816]{2,1,0:T(8,128)(2,1)}), bf16[16,32,2816]{2,1,0:T(8,128)(2,1)S(1)}, u32[]{:S(2)}, u32[]{:S(2)}) async-start(bf16[16,32,2816]{2,1,0:T(8,128)(2,1)} %bitcast.48), calls=%async_computation.5 | async-start | bytes 5767168 | tf_op jit(solution)/shard_map/all_to_all | solution.py:617
  368.2 4.9 %shard_map.283.mine = bf16[256,1024]{1,0:T(8,128)(2,1)} custom-call(bf16[128,6400]{1,0:T(8,128)(2,1)} %get-tuple-element.119.own.refs_6_, bf16[128,6400]{1,0:T(8,128)(2,1)} %get-tuple-element.120.theirs.sent.refs_7_, bf16[1728,1024]{1,0:T(8,128)(2,1)} %weight.3), custom_call_target="tpu_custom_call" | custom-call | tf_op jit(solution)/shard_map/pallas_call | solution.py:76
  374.8 11.4 %collective-permute-done.13.theirs = bf16[256,1024]{1,0:T(8,128)(2,1)S(1)} collective-permute-done((bf16[256,1024]{1,0:T(8,128)(2,1)}, bf16[256,1024]{1,0:T(8,128)(2,1)S(1)}, u32[]{:S(2)}, u32[]{:S(2)}) %collective-permute-start.13) | collective-permute-done | bytes 524320 | tf_op jit(solution)/shard_map/ppermute | solution.py:58
  391.7 5.5 %collective-permute-done.14.oth = bf16[128,1024]{1,0:T(8,128)(2,1)S(1)} collective-permute-done((bf16[128,1024]{1,0:T(8,128)(2,1)}, bf16[128,1024]{1,0:T(8,128)(2,1)S(1)}, u32[]{:S(2)}, u32[]{:S(2)}) %collective-permute-start.14) | collective-permute-done | bytes 262176 | tf_op jit(solution)/shard_map/ppermute | solution.py:50
  402.1 9.5 %all-to-all-done.5.parts = bf16[16,32,2816]{2,1,0:T(8,128)(2,1)S(1)} async-done(((bf16[16,32,2816]{2,1,0:T(8,128)(2,1)}), bf16[16,32,2816]{2,1,0:T(8,128)(2,1)S(1)}, u32[]{:S(2)}, u32[]{:S(2)}) %all-to-all-start.5) | async-done | bytes 2883616 | tf_op jit(solution)/shard_map/all_to_all | solution.py:617
  413.1 2.8 shard_map.295
  (170 shorter events, 82.9 us)
Async XLA Ops:
  7.2 112.7 %all-gather.2.cloned.1.call-start = ((), (), s32[]{:S(2)}) async-start(), calls=%async_computation.7 | async-start | bytes 11354112 | tf_op jit(solution)/shard_map/all_gather | solution.py:693
  11.2 9.8 %collective-permute-start = (bf16[128,1024]{1,0:T(8,128)(2,1)}, bf16[128,1024]{1,0:T(8,128)(2,1)S(1)}, u32[]{:S(2)}, u32[]{:S(2)}) collective-permute-start(bf16[128,1024]{1,0:T(8,128)(2,1)} %get-tuple-element.82), channel_id=1, source_target_pairs={{0,64},{64,0},{1,65},{65,1},{2,66},{66,2},{3,67},{67,3},{4,68},{68... | collective-permute-start | bytes 786440 | tf_op jit(solution)/shard_map/ppermute | solution.py:50
  21.8 16.3 %collective-permute-start.6 = (bf16[32,5376]{1,0:T(8,128)(2,1)}, bf16[32,5376]{1,0:T(8,128)(2,1)S(1)}, u32[]{:S(2)}, u32[]{:S(2)}) collective-permute-start(bf16[32,5376]{1,0:T(8,128)(2,1)} %shard_map.272), channel_id=1, source_target_pairs={{0,64},{64,0},{1,65},{65,1},{2,66},{66,2},{3,67},{67,3},{4,68},{68... | collective-permute-start | bytes 1032200 | tf_op jit(solution)/shard_map/ppermute | solution.py:50
  25.0 13.0 %collective-permute-start.5 = (bf16[128,1024]{1,0:T(8,128)(2,1)}, bf16[128,1024]{1,0:T(8,128)(2,1)S(1)}, u32[]{:S(2)}, u32[]{:S(2)}) collective-permute-start(bf16[128,1024]{1,0:T(8,128)(2,1)} %get-tuple-element.96.up_oth), channel_id=1, source_target_pairs={{0,64},{64,0},{1,65},{65,1},{2,66},{66,2},{3,67},{67,3},{4,68},{68... | collective-permute-start | bytes 786440 | tf_op jit(solution)/shard_map/ppermute | solution.py:50
  32.4 9.3 %copy-start.15 = (f32[128,1024]{1,0:T(8,128)S(1)}, f32[128,1024]{1,0:T(8,128)}, u32[]{:S(2)}) copy-start(f32[128,1024]{1,0:T(8,128)} %get-tuple-element.83._) | copy-start | bytes 1572868
  32.4 11.5 %copy-start.38 = (s32[1,128]{1,0:T(1,128)S(1)}, s32[1,128]{1,0:T(1,128)}, u32[]{:S(2)}) copy-start(s32[1,128]{1,0:T(1,128)} %param.17) | copy-start | bytes 1540
  40.1 19.3 %collective-permute-start.3 = (f16[128,1728]{1,0:T(8,128)(2,1)S(1)}, f16[128,1728]{1,0:T(8,128)(2,1)S(1)}, u32[]{:S(2)}, u32[]{:S(2)}) collective-permute-start(f16[128,1728]{1,0:T(8,128)(2,1)S(1)} %convert_element_type.59), channel_id=1, source_target_pairs={{0,64},{64,0},{1,65},{65,1},{2,66},{66,2},{3,67},{67,3},{4,68},{68... | collective-permute-start | bytes 1327112 | tf_op jit(solution)/shard_map/ppermute | solution.py:54
  41.7 17.0 %collective-permute-start.2 = (f16[128,1024]{1,0:T(8,128)(2,1)S(1)}, f16[128,1024]{1,0:T(8,128)(2,1)S(1)}, u32[]{:S(2)}, u32[]{:S(2)}) collective-permute-start(f16[128,1024]{1,0:T(8,128)(2,1)S(1)} %convert_element_type.57), channel_id=1, source_target_pairs={{0,64},{64,0},{1,65},{65,1},{2,66},{66,2},{3,67},{67,3},{4,68},{68... | collective-permute-start | bytes 786440 | tf_op jit(solution)/shard_map/ppermute | solution.py:54
  60.5 11.2 %copy-start.22 = (f32[128,1728]{1,0:T(8,128)S(1)}, f32[128,1728]{1,0:T(8,128)}, u32[]{:S(2)}) copy-start(f32[128,1728]{1,0:T(8,128)} %get-tuple-element.94) | copy-start | bytes 2654212
  60.5 12.8 %copy-start.16 = (f32[128,1024]{1,0:T(8,128)S(1)}, f32[128,1024]{1,0:T(8,128)}, u32[]{:S(2)}) copy-start(f32[128,1024]{1,0:T(8,128)} %get-tuple-element.85._) | copy-start | bytes 1572868
  64.1 29.3 %all-to-all-start = ((bf16[32,8,1792]{2,1,0:T(8,128)(2,1)}), bf16[32,8,1792]{2,1,0:T(8,128)(2,1)S(1)}, u32[]{:S(2)}, u32[]{:S(2)}) async-start(bf16[32,8,1792]{2,1,0:T(8,128)(2,1)} %bitcast.54), calls=%async_computation | async-start | bytes 1835008 | tf_op jit(solution)/shard_map/all_to_all | solution.py:697
  71.8 20.6 %collective-permute-start.4 = (f16[128,1728]{1,0:T(8,128)(2,1)S(1)}, f16[128,1728]{1,0:T(8,128)(2,1)S(1)}, u32[]{:S(2)}, u32[]{:S(2)}) collective-permute-start(f16[128,1728]{1,0:T(8,128)(2,1)S(1)} %convert_element_type.61), channel_id=1, source_target_pairs={{0,64},{64,0},{1,65},{65,1},{2,66},{66,2},{3,67},{67,3},{4,68},{68... | collective-permute-start | bytes 1327112 | tf_op jit(solution)/shard_map/ppermute | solution.py:54
  73.3 18.3 %collective-permute-start.1 = (f16[128,1024]{1,0:T(8,128)(2,1)S(1)}, f16[128,1024]{1,0:T(8,128)(2,1)S(1)}, u32[]{:S(2)}, u32[]{:S(2)}) collective-permute-start(f16[128,1024]{1,0:T(8,128)(2,1)S(1)} %convert_element_type.55), channel_id=1, source_target_pairs={{0,64},{64,0},{1,65},{65,1},{2,66},{66,2},{3,67},{67,3},{4,68},{68... | collective-permute-start | bytes 786440 | tf_op jit(solution)/shard_map/ppermute | solution.py:54
  94.3 10.2 %copy-start.10 = (f32[128,1728]{1,0:T(8,128)S(1)}, f32[128,1728]{1,0:T(8,128)}, u32[]{:S(2)}) copy-start(f32[128,1728]{1,0:T(8,128)} %get-tuple-element.97.refs_2_) | copy-start | bytes 2654212
  96.9 23.0 %all-to-all-start.1 = ((bf16[32,8,1792]{2,1,0:T(8,128)(2,1)}), bf16[32,8,1792]{2,1,0:T(8,128)(2,1)S(1)}, u32[]{:S(2)}, u32[]{:S(2)}) async-start(bf16[32,8,1792]{2,1,0:T(8,128)(2,1)} %shard_map.271), calls=%async_computation.1 | async-start | bytes 1835008 | tf_op jit(solution)/shard_map/all_to_all | solution.py:699
  104.5 14.3 %collective-permute-start.7 = (f16[128,1728]{1,0:T(8,128)(2,1)S(1)}, f16[128,1728]{1,0:T(8,128)(2,1)S(1)}, u32[]{:S(2)}, u32[]{:S(2)}) collective-permute-start(f16[128,1728]{1,0:T(8,128)(2,1)S(1)} %convert_element_type.63), channel_id=1, source_target_pairs={{0,64},{64,0},{1,65},{65,1},{2,66},{66,2},{3,67},{67,3},{4,68},{68... | collective-permute-start | bytes 1327112 | tf_op jit(solution)/shard_map/ppermute | solution.py:54
  128.2 13.4 %collective-permute-start.8 = (bf16[128,2048]{1,0:T(8,128)(2,1)}, bf16[128,2048]{1,0:T(8,128)(2,1)S(1)}, u32[]{:S(2)}, u32[]{:S(2)}) collective-permute-start(bf16[128,2048]{1,0:T(8,128)(2,1)} %get-tuple-element.100.mine), channel_id=1, source_target_pairs={{0,1},{1,0},{2,3},{3,2},{4,5},{5,4},{6,7},{7,6},{8,9},{9,8},{10,11... | collective-permute-start | bytes 1572872 | tf_op jit(solution)/shard_map/ppermute | solution.py:58
  132.1 3.5 collective-permute-start.9
  135.1 1.9 collective-permute-start.10
  156.2 12.7 %collective-permute-start.11 = (bf16[128,2048]{1,0:T(8,128)(2,1)}, bf16[128,2048]{1,0:T(8,128)(2,1)S(1)}, u32[]{:S(2)}, u32[]{:S(2)}) collective-permute-start(bf16[128,2048]{1,0:T(8,128)(2,1)} %get-tuple-element.106.mine), channel_id=1, source_target_pairs={{0,1},{1,0},{2,3},{3,2},{4,5},{5,4},{6,7},{7,6},{8,9},{9,8},{10,11... | collective-permute-start | bytes 1572872 | tf_op jit(solution)/shard_map/ppermute | solution.py:58
  169.7 36.9 %collective-permute-start.12 = (bf16[128,6400]{1,0:T(8,128)(2,1)}, bf16[128,6400]{1,0:T(8,128)(2,1)S(1)}, u32[]{:S(2)}, u32[]{:S(2)}) collective-permute-start(bf16[128,6400]{1,0:T(8,128)(2,1)} %shard_map.278.refs_0_), channel_id=1, source_target_pairs={{0,64},{64,0},{1,65},{65,1},{2,66},{66,2},{3,67},{67,3},{4,68},{68... | collective-permute-start | bytes 4915208 | tf_op jit(solution)/shard_map/ppermute | solution.py:50
  180.6 19.1 %all-to-all-start.2 = ((bf16[32,8,1792]{2,1,0:T(8,128)(2,1)}), bf16[32,8,1792]{2,1,0:T(8,128)(2,1)S(1)}, u32[]{:S(2)}, u32[]{:S(2)}) async-start(bf16[32,8,1792]{2,1,0:T(8,128)(2,1)} %bitcast.55), calls=%async_computation.2 | async-start | bytes 1835008 | tf_op jit(solution)/shard_map/all_to_all | solution.py:697
  207.9 29.7 %collective-permute-start.19 = (bf16[128,6400]{1,0:T(8,128)(2,1)}, bf16[128,6400]{1,0:T(8,128)(2,1)S(1)}, u32[]{:S(2)}, u32[]{:S(2)}) collective-permute-start(bf16[128,6400]{1,0:T(8,128)(2,1)} %get-tuple-element.119.own.refs_6_), channel_id=1, source_target_pairs={{0,2},{2,0},{4,6},{6,4},{8,10},{10,8},{12,14},{14,12},{16,18},{18,... | collective-permute-start | bytes 4915208 | tf_op jit(solution)/shard_map/ppermute | solution.py:62
  207.9 29.7 %collective-permute-start.20 = (bf16[128,6400]{1,0:T(8,128)(2,1)}, bf16[128,6400]{1,0:T(8,128)(2,1)}, u32[]{:S(2)}, u32[]{:S(2)}) collective-permute-start(bf16[128,6400]{1,0:T(8,128)(2,1)} %get-tuple-element.120.theirs.sent.refs_7_), channel_id=1, source_target_pairs={{0,2},{2,0},{4,6},{6,4},{8,10},{10,8},{12,14},{14,12},{16,18},{18,... | collective-permute-start | bytes 4915208 | tf_op jit(solution)/shard_map/ppermute | solution.py:62
  208.4 19.8 %collective-permute-start.17 = (bf16[128,2816]{1,0:T(8,128)(2,1)}, bf16[128,2816]{1,0:T(8,128)(2,1)S(1)}, u32[]{:S(2)}, u32[]{:S(2)}) collective-permute-start(bf16[128,2816]{1,0:T(8,128)(2,1)} %get-tuple-element.130.refs_10_), channel_id=1, source_target_pairs={{0,64},{64,0},{1,65},{65,1},{2,66},{66,2},{3,67},{67,3},{4,68},{68... | collective-permute-start | bytes 2162696 | tf_op jit(solution)/shard_map/ppermute | solution.py:50
  209.9 25.8 %collective-permute-start.21 = (bf16[128,2816]{1,0:T(8,128)(2,1)}, bf16[128,2816]{1,0:T(8,128)(2,1)}, u32[]{:S(2)}, u32[]{:S(2)}) collective-permute-start(bf16[128,2816]{1,0:T(8,128)(2,1)} %get-tuple-element.130.refs_10_), channel_id=1, source_target_pairs={{0,2},{2,0},{4,6},{6,4},{8,10},{10,8},{12,14},{14,12},{16,18},{18,... | collective-permute-start | bytes 2162696 | tf_op jit(solution)/shard_map/ppermute | solution.py:62
  209.9 45.0 %all-to-all-start.3 = ((bf16[32,8,1792]{2,1,0:T(8,128)(2,1)}), bf16[32,8,1792]{2,1,0:T(8,128)(2,1)S(1)}, u32[]{:S(2)}, u32[]{:S(2)}) async-start(bf16[32,8,1792]{2,1,0:T(8,128)(2,1)} %shard_map.281.refs_2_.refs_0_), calls=%async_computation.3 | async-start | bytes 1835008 | tf_op jit(solution)/shard_map/all_to_all | solution.py:699
  217.4 200.1 %reduce-scatter.4.cloned.1.call-start = ((), (), s32[]{:S(2)}) async-start(), calls=%async_computation.8 | async-start | bytes 7798784
  228.2 8.0 %collective-permute-start.22 = (bf16[128,2816]{1,0:T(8,128)(2,1)S(1)}, bf16[128,2816]{1,0:T(8,128)(2,1)S(1)}, u32[]{:S(2)}, u32[]{:S(2)}) collective-permute-start(bf16[128,2816]{1,0:T(8,128)(2,1)S(1)} %collective-permute-done.17.sent.refs_11_), channel_id=1, source_target_pairs={{0,2},{2,0},{4,6},{6,4},{8,10},{10,8},{12,14},{14,12},{16,18},{18,... | collective-permute-start | bytes 2162696 | tf_op jit(solution)/shard_map/ppermute | solution.py:62
  232.2 4.0 collective-permute-start.18
  235.7 1.9 collective-permute-start.16
  256.9 20.2 %collective-permute-start.15 = (bf16[128,2816]{1,0:T(8,128)(2,1)S(1)}, bf16[128,2816]{1,0:T(8,128)(2,1)S(1)}, u32[]{:S(2)}, u32[]{:S(2)}) collective-permute-start(bf16[128,2816]{1,0:T(8,128)(2,1)S(1)} %copy-done.6), channel_id=1, source_target_pairs={{0,64},{64,0},{1,65},{65,1},{2,66},{66,2},{3,67},{67,3},{4,68},{68... | collective-permute-start | bytes 2162696 | tf_op jit(solution)/shard_map/ppermute | solution.py:50
  281.6 2.4 collective-permute-start.32
  281.6 3.4 collective-permute-start.33
  290.7 62.7 %all-to-all-start.4 = ((bf16[16,32,2816]{2,1,0:T(8,128)(2,1)}), bf16[16,32,2816]{2,1,0:T(8,128)(2,1)S(1)}, u32[]{:S(2)}, u32[]{:S(2)}) async-start(bf16[16,32,2816]{2,1,0:T(8,128)(2,1)} %bitcast.51), calls=%async_computation.4 | async-start | bytes 5767168 | tf_op jit(solution)/shard_map/all_to_all | solution.py:617
  297.9 19.4 %collective-permute-start.23 = (bf16[128,2816]{1,0:T(8,128)(2,1)}, bf16[128,2816]{1,0:T(8,128)(2,1)S(1)}, u32[]{:S(2)}, u32[]{:S(2)}) collective-permute-start(bf16[128,2816]{1,0:T(8,128)(2,1)} %shard_map.289.refs_2_.key_value), channel_id=1, source_target_pairs={{0,64},{64,0},{1,65},{65,1},{2,66},{66,2},{3,67},{67,3},{4,68},{68... | collective-permute-start | bytes 2162696 | tf_op jit(solution)/shard_map/ppermute | solution.py:50
  299.4 51.5 %collective-permute-start.27 = (bf16[128,2816]{1,0:T(8,128)(2,1)}, bf16[128,2816]{1,0:T(8,128)(2,1)S(1)}, u32[]{:S(2)}, u32[]{:S(2)}) collective-permute-start(bf16[128,2816]{1,0:T(8,128)(2,1)} %shard_map.289.refs_2_.key_value), channel_id=1, source_target_pairs={{0,2},{2,0},{4,6},{6,4},{8,10},{10,8},{12,14},{14,12},{16,18},{18,... | collective-permute-start | bytes 2162696 | tf_op jit(solution)/shard_map/ppermute | solution.py:62
  317.3 36.0 %collective-permute-start.28 = (bf16[128,2816]{1,0:T(8,128)(2,1)S(1)}, bf16[128,2816]{1,0:T(8,128)(2,1)}, u32[]{:S(2)}, u32[]{:S(2)}) collective-permute-start(bf16[128,2816]{1,0:T(8,128)(2,1)S(1)} %collective-permute-done.23.key_value_theirs.refs_3_), channel_id=1, source_target_pairs={{0,2},{2,0},{4,6},{6,4},{8,10},{10,8},{12,14},{14,12},{16,18},{18,... | collective-permute-start | bytes 2162696 | tf_op jit(solution)/shard_map/ppermute | solution.py:62
  327.4 9.4 %collective-permute-start.24 = (bf16[128,1024]{1,0:T(8,128)(2,1)}, bf16[128,1024]{1,0:T(8,128)(2,1)S(1)}, u32[]{:S(2)}, u32[]{:S(2)}) collective-permute-start(bf16[128,1024]{1,0:T(8,128)(2,1)} %get-tuple-element.135.mine), channel_id=1, source_target_pairs={{0,1},{1,0},{2,3},{3,2},{4,5},{5,4},{6,7},{7,6},{8,9},{9,8},{10,11... | collective-permute-start | bytes 786440 | tf_op jit(solution)/shard_map/ppermute | solution.py:58
  328.1 14.7 %collective-permute-start.26 = (bf16[128,1024]{1,0:T(8,128)(2,1)}, bf16[128,1024]{1,0:T(8,128)(2,1)S(1)}, u32[]{:S(2)}, u32[]{:S(2)}) collective-permute-start(bf16[128,1024]{1,0:T(8,128)(2,1)} %get-tuple-element.136), channel_id=1, source_target_pairs={{0,65},{1,64},{64,1},{65,0},{2,67},{3,66},{66,3},{67,2},{4,69},{5,... | collective-permute-start | bytes 786440 | tf_op jit(solution)/shard_map/ppermute | solution.py:826
  329.4 13.4 %collective-permute-start.25 = (bf16[128,1024]{1,0:T(8,128)(2,1)}, bf16[128,1024]{1,0:T(8,128)(2,1)S(1)}, u32[]{:S(2)}, u32[]{:S(2)}) collective-permute-start(bf16[128,1024]{1,0:T(8,128)(2,1)} %get-tuple-element.136), channel_id=1, source_target_pairs={{0,64},{64,0},{1,65},{65,1},{2,66},{66,2},{3,67},{67,3},{4,68},{68... | collective-permute-start | bytes 786440 | tf_op jit(solution)/shard_map/ppermute | solution.py:50
  347.3 3.7 collective-permute-start.30
  347.3 5.1 %collective-permute-start.31 = (bf16[16,1024]{1,0:T(8,128)(2,1)}, bf16[16,1024]{1,0:T(8,128)(2,1)S(1)}, u32[]{:S(2)}, u32[]{:S(2)}) collective-permute-start(bf16[16,1024]{1,0:T(8,128)(2,1)} %get-tuple-element.144), channel_id=1, source_target_pairs={{0,66},{2,64},{4,70},{6,68},{8,74},{10,72},{12,78},{14,76},{16,82}... | collective-permute-start | bytes 98312 | tf_op jit(solution)/shard_map/ppermute | solution.py:833
  347.8 5.6 %collective-permute-start.29 = (bf16[16,1024]{1,0:T(8,128)(2,1)}, bf16[16,1024]{1,0:T(8,128)(2,1)S(1)}, u32[]{:S(2)}, u32[]{:S(2)}) collective-permute-start(bf16[16,1024]{1,0:T(8,128)(2,1)} %get-tuple-element.144), channel_id=1, source_target_pairs={{0,64},{64,0},{1,65},{65,1},{2,66},{66,2},{3,67},{67,3},{4,68},{68... | collective-permute-start | bytes 98312 | tf_op jit(solution)/shard_map/ppermute | solution.py:50
  361.0 50.5 %all-to-all-start.5 = ((bf16[16,32,2816]{2,1,0:T(8,128)(2,1)}), bf16[16,32,2816]{2,1,0:T(8,128)(2,1)S(1)}, u32[]{:S(2)}, u32[]{:S(2)}) async-start(bf16[16,32,2816]{2,1,0:T(8,128)(2,1)} %bitcast.48), calls=%async_computation.5 | async-start | bytes 5767168 | tf_op jit(solution)/shard_map/all_to_all | solution.py:617
  373.2 27.1 %copy-start.2 = (bf16[16,32,2816]{2,1,0:T(8,128)(2,1)S(1)}, bf16[16,32,2816]{2,1,0:T(8,128)(2,1)}, u32[]{:S(2)}) copy-start(bf16[16,32,2816]{2,1,0:T(8,128)(2,1)} %copy-done.1) | copy-start | bytes 8650756
  373.2 13.0 %collective-permute-start.13 = (bf16[256,1024]{1,0:T(8,128)(2,1)}, bf16[256,1024]{1,0:T(8,128)(2,1)S(1)}, u32[]{:S(2)}, u32[]{:S(2)}) collective-permute-start(bf16[256,1024]{1,0:T(8,128)(2,1)} %shard_map.283.mine), channel_id=1, source_target_pairs={{0,1},{1,0},{2,3},{3,2},{4,5},{5,4},{6,7},{7,6},{8,9},{9,8},{10,11... | collective-permute-start | bytes 1572872 | tf_op jit(solution)/shard_map/ppermute | solution.py:58
  389.1 8.1 %collective-permute-start.14 = (bf16[128,1024]{1,0:T(8,128)(2,1)}, bf16[128,1024]{1,0:T(8,128)(2,1)S(1)}, u32[]{:S(2)}, u32[]{:S(2)}) collective-permute-start(bf16[128,1024]{1,0:T(8,128)(2,1)} %get-tuple-element.122), channel_id=1, source_target_pairs={{0,64},{64,0},{1,65},{65,1},{2,66},{66,2},{3,67},{67,3},{4,68},{68... | collective-permute-start | bytes 786440 | tf_op jit(solution)/shard_map/ppermute | solution.py:50
  (33 other events, 48.8 us)
Sparse Core Ops, SparseCore 0:
  39.0 68.6 all-gather.1
  256.0 117.9 reduce-scatter.3

commit v3 on v2

--- a/solution.py
+++ b/solution.py
@@ -672,14 +672,14 @@
         [],
         [low1_theirs, key_weight, value_turned],
     )
-    helped_key, helped_value = half_from_shard(theirs_key), half_from_shard(theirs_value)
+    helped_key, helped_value = from_shard(theirs_key), half_from_shard(theirs_value)
     theirs_query, theirs_gate = run(
         help_more_kernel,
         (shape(PIECE, HALF, kind=F32), shape(PIECE, VW, kind=F32)),
         [],
         [low1_theirs, query_weight, gate_turned],
     )
-    helped_query, helped_gate = half_from_shard(theirs_query), half_from_shard(theirs_gate)
+    helped_query, helped_gate = from_shard(theirs_query), half_from_shard(theirs_gate)
     base_query, base_key, base_value, base_gate = run(
         base_kernel,
         tuple(shape(PIECE, n, kind=F32) for n in (HALF, HALF, VW, VW)),
@@ -787,6 +787,7 @@
         VPAD,
         4 * VPAD,
     )
+    early_part = after(early_part, outgoing)
     key_value = run(
         later_kernel,
         shape(PIECE, HALF + VPAD),
@@ -797,9 +798,7 @@
     )
     key_value_theirs = from_shard(key_value)
 
-    early = lax.psum_scatter(
-        after(early_part, outgoing), "ctx", scatter_dimension=0, axis_index_groups=PLANE, tiled=False
-    )
+    early = lax.psum_scatter(early_part, "ctx", scatter_dimension=0, axis_index_groups=PLANE, tiled=False)
     early = early.astype(F32)
     gate_query, gate_query_theirs = hold((gate_query, gate_query_theirs), key_value)
     gate_query_parts = sent(
@@ -809,7 +808,7 @@
             [(0, 0, 0), (0, 0, 1)],
             (VPAD + HALF) // 2,
             VPAD + HALF,
-            flops=40 * 10**9,
+            flops=100 * 10**9,
         )
     )
     first_weights = [query_weight, key_weight, value_turned, gate_turned]

time: 435 us -> 425 us (0.977)
  the two profiles are of different devices: /device:TPU:86 before, /device:TPU:8 now
where the time goes in v3:
time: 425 us; the launch traced here: 418 us
  waiting for transfers between devices  147 us (35%)
  Pallas kernels  137 us (32%)
  starting transfers between devices  89.1 us (21%)
  local copies, waits for them, and re-layouts  22.9 us (5%)
  between operations  14.8 us (3%)
  other arithmetic  6.31 us (1%)
    pallas_call x25, Pallas kernels, run(): pl.pallas_call(kernel, out_shape=outs, grid=(1,), in_specs=[SMEM] * len(s...  118 us
    ppermute x12, waiting for transfers between devices, from_shard(): return lax.ppermute(part, 'shard', SWAP)  48.6 us
    ppermute x4, waiting for transfers between devices, from_tp(): return lax.ppermute(part, 'tp', SWAP)  32 us
    ppermute x3, waiting for transfers between devices, half_from_shard(): return lax.ppermute(part.astype(F16), 'shard', SWAP).astype(F32)  31.9 us
    ppermute x12, starting transfers between devices, from_shard(): return lax.ppermute(part, 'shard', SWAP)  30.5 us
    pallas_call x3, Pallas kernels, outer(): pl.pallas_call(kernel, out_shape=shape(HALF // 2, width), grid_spec=pltpu...  19.7 us
    unnamed x78, local copies, waits for them, and re-layouts  18.4 us
    all_to_all x2, starting transfers between devices, exchange(): lax.all_to_all(states.reshape(NC, KH // NC, VPAD), 'ctx', 0, 0, tiled=True)  15.9 us
  transfers between devices with their start and end apart: 42, of which 23 were waited for; matrix products, arithmetic and copies ran while one was open for 2% of the time, Pallas kernels for 26%

profile of v3, /device:TPU:8, one launch (start us, length us, event | category | flops | bytes accessed | tf_op | source)
XLA Modules:
  0.0 417.5 jit_solution(10052959078748784510)
XLA Ops:
  7.2 3.9 shard_map.263
  11.2 3.1 collective-permute-start
  14.3 6.7 %collective-permute-done.low.refs_1_ = bf16[128,1024]{1,0:T(8,128)(2,1)S(1)} collective-permute-done((bf16[128,1024]{1,0:T(8,128)(2,1)}, bf16[128,1024]{1,0:T(8,128)(2,1)S(1)}, u32[]{:S(2)}, u32[]{:S(2)}) %collective-permute-start) | collective-permute-done | bytes 262176 | tf_op jit(solution)/shard_map/ppermute | solution.py:50
  21.7 3.0 collective-permute-start.6
  27.2 5.2 %shard_map.264 = (f32[128,1024]{1,0:T(8,128)}, f32[128,1728]{1,0:T(8,128)}) custom-call(bf16[128,1024]{1,0:T(8,128)(2,1)} %copy-done.8, bf16[1024,1024]{1,0:T(8,128)(2,1)} %key_weight.5, bf16[1728,1024]{1,0:T(8,128)(2,1)} %bitcast.34), custom_call_target="tpu_custom_call" | custom-call | tf_op jit(solution)/shard_map/pallas_call | solution.py:76
  32.4 5.6 %collective-permute-done.5.theirs.refs_2_.refs_1_ = bf16[128,1024]{1,0:T(8,128)(2,1)S(1)} collective-permute-done((bf16[128,1024]{1,0:T(8,128)(2,1)}, bf16[128,1024]{1,0:T(8,128)(2,1)S(1)}, u32[]{:S(2)}, u32[]{:S(2)}) %collective-permute-start.5) | collective-permute-done | bytes 262176 | tf_op jit(solution)/shard_map/ppermute | solution.py:50
  38.9 3.1 collective-permute-start.2
  45.0 8.2 %shard_map.265 = (f32[128,1024]{1,0:T(8,128)}, f32[128,1024]{1,0:T(8,128)}, f32[128,1728]{1,0:T(8,128)}, f32[128,1728]{1,0:T(8,128)}) custom-call(bf16[128,1024]{1,0:T(8,128)(2,1)} %get-tuple-element.81.low.refs_0_, bf16[1024,1024]{1,0:T(8,128)(2,1)} %query_weight.5, bf16[1024,1024]{1,0:T(8,128)(2,1)} %key_weight.5, bf16[1728,1024]{1,0:T(8,128)(2,1)} %bitcast.35, ...), custom_call_target="tpu_custom_call" | custom-call | tf_op jit(solution)/shard_map/pallas_call | solution.py:76
  53.2 5.2 %shard_map.266 = (f32[128,1024]{1,0:T(8,128)}, f32[128,1728]{1,0:T(8,128)}) custom-call(bf16[128,1024]{1,0:T(8,128)(2,1)} %copy-done.8, bf16[1024,1024]{1,0:T(8,128)(2,1)} %query_weight.5, bf16[1728,1024]{1,0:T(8,128)(2,1)} %bitcast.38), custom_call_target="tpu_custom_call" | custom-call | tf_op jit(solution)/shard_map/pallas_call | solution.py:76
  58.5 3.9 collective-permute-done.3
  64.2 3.5 shard_map.267
  67.7 8.5 %all-to-all-start = ((bf16[32,8,1792]{2,1,0:T(8,128)(2,1)}), bf16[32,8,1792]{2,1,0:T(8,128)(2,1)S(1)}, u32[]{:S(2)}, u32[]{:S(2)}) async-start(bf16[32,8,1792]{2,1,0:T(8,128)(2,1)} %bitcast.53), calls=%async_computation | async-start | bytes 1835008 | tf_op jit(solution)/shard_map/all_to_all | solution.py:697
  76.3 3.1 collective-permute-start.1
  80.0 4.8 %shard_map.270 = (f32[128,1728]{1,0:T(8,128)}, f32[128,1728]{1,0:T(8,128)}) custom-call(bf16[128,1024]{1,0:T(8,128)(2,1)} %get-tuple-element.95.own.refs_0_.up_own, bf16[128,1024]{1,0:T(8,128)(2,1)} %copy-done.14, bf16[1728,1024]{1,0:T(8,128)(2,1)} %weight.3), custom_call_target="tpu_custom_call" | custom-call | tf_op jit(solution)/shard_map/pallas_call | solution.py:76
  84.8 16.9 %collective-permute-done.4 = f16[128,1728]{1,0:T(8,128)(2,1)S(1)} collective-permute-done((f16[128,1728]{1,0:T(8,128)(2,1)S(1)}, f16[128,1728]{1,0:T(8,128)(2,1)S(1)}, u32[]{:S(2)}, u32[]{:S(2)}) %collective-permute-start.4) | collective-permute-done | bytes 442400 | tf_op jit(solution)/shard_map/ppermute | solution.py:54
  106.3 7.4 %all-to-all-start.1 = ((bf16[32,8,1792]{2,1,0:T(8,128)(2,1)}), bf16[32,8,1792]{2,1,0:T(8,128)(2,1)S(1)}, u32[]{:S(2)}, u32[]{:S(2)}) async-start(bf16[32,8,1792]{2,1,0:T(8,128)(2,1)} %shard_map.271), calls=%async_computation.1 | async-start | bytes 1835008 | tf_op jit(solution)/shard_map/all_to_all | solution.py:699
  113.8 3.3 collective-permute-start.7
  117.1 11.1 %collective-permute-done.7 = f16[128,1728]{1,0:T(8,128)(2,1)S(1)} collective-permute-done((f16[128,1728]{1,0:T(8,128)(2,1)S(1)}, f16[128,1728]{1,0:T(8,128)(2,1)S(1)}, u32[]{:S(2)}, u32[]{:S(2)}) %collective-permute-start.7) | collective-permute-done | bytes 442400 | tf_op jit(solution)/shard_map/ppermute | solution.py:54
  129.2 3.3 shard_map.268
  133.4 7.4 %shard_map.274 = (f32[128,1728]{1,0:T(8,128)}, f32[128,1792]{1,0:T(8,128)}, f32[128,128]{1,0:T(8,128)}, bf16[128,1792]{1,0:T(8,128)(2,1)}, bf16[128,2048]{1,0:T(8,128)(2,1)}) custom-call(f32[4]{0:T(128)} %rates.15, f32[128,1]{1,0:T(8,128)} %copy.52.seg_column, bf16[128,1024]{1,0:T(8,128)(2,1)} %get-tuple-element.91.queries, ...), custom_call_target="tpu_custom_call" | custom-call | tf_op jit(solution)/shard_map/pallas_call | solution.py:76
  150.2 4.0 collective-permute-done.8.theirs
  155.0 13.8 %shard_map.277 = (f32[128,2048]{1,0:T(8,128)}, f32[128,2048]{1,0:T(8,128)}, f32[128,128]{1,0:T(8,128)}, bf16[128,1024]{1,0:T(8,128)(2,1)}, bf16[128,6400]{1,0:T(8,128)(2,1)}, /*index=5*/bf16[128,2048]{1,0:T(8,128)(2,1)}) custom-call(s32[1]{0:T(128)} %bitcast.shard, bf16[128,2048]{1,0:T(8,128)(2,1)} %bitcast.52, bf16[128,2048]{1,0:T(8,128)(2,1)} %get-tuple-element.100.mine, ...), custom_call_target="tpu_custom_call" | custom-call | tf_op jit(solution)/shard_map/pallas_call | solution.py:76
  170.6 10.9 %collective-permute-done.11.refs_1_.theirs = bf16[128,2048]{1,0:T(8,128)(2,1)S(1)} collective-permute-done((bf16[128,2048]{1,0:T(8,128)(2,1)}, bf16[128,2048]{1,0:T(8,128)(2,1)S(1)}, u32[]{:S(2)}, u32[]{:S(2)}) %collective-permute-start.11) | collective-permute-done | bytes 524320 | tf_op jit(solution)/shard_map/ppermute | solution.py:58
  185.3 9.3 %shard_map.279 = (f32[128,2048]{1,0:T(8,128)}, bf16[128,1024]{1,0:T(8,128)(2,1)}, bf16[128,1024]{1,0:T(8,128)(2,1)}, f32[8,2048]{1,0:T(8,128)}, bf16[128,1792]{1...) custom-call(s32[1]{0:T(128)} %bitcast.shard, f32[4]{0:T(128)} %rates.15, ...), custom_call_target="tpu_custom_call" | custom-call | tf_op jit(solution)/shard_map/pallas_call | solution.py:76
  194.6 7.4 %all-to-all-start.2 = ((bf16[32,8,1792]{2,1,0:T(8,128)(2,1)}), bf16[32,8,1792]{2,1,0:T(8,128)(2,1)S(1)}, u32[]{:S(2)}, u32[]{:S(2)}) async-start(bf16[32,8,1792]{2,1,0:T(8,128)(2,1)} %bitcast.54), calls=%async_computation.2 | async-start | bytes 1835008 | tf_op jit(solution)/shard_map/all_to_all | solution.py:697
  202.0 4.9 %shard_map.280 = (bf16[128,2816]{1,0:T(8,128)(2,1)}, bf16[128,2816]{1,0:T(8,128)(2,1)}, f32[128,1024]{1,0:T(8,128)}, f32[128,1792]{1,0:T(8,128)}) custom-call(f32[4]{0:T(128)} %rates.15, f32[128,1]{1,0:T(8,128)} %copy.52.seg_column, f32[1,128]{1,0:T(1,128)} %get-tuple-element.156.seg_row, bf16[128,1024]{1,0:T(8,128)(2,1)} %get-tuple-element.91.queries, ...), custom_call_target="tpu_custom_call" | custom-call | tf_op jit(solution)/shard_map/pallas_call | solution.py:76
  206.9 8.2 %all-to-all-done.2.states = bf16[32,8,1792]{2,1,0:T(8,128)(2,1)S(1)} async-done(((bf16[32,8,1792]{2,1,0:T(8,128)(2,1)}), bf16[32,8,1792]{2,1,0:T(8,128)(2,1)S(1)}, u32[]{:S(2)}, u32[]{:S(2)}) %all-to-all-start.2) | async-done | bytes 917536 | tf_op jit(solution)/shard_map/all_to_all | solution.py:697
  220.9 3.0 collective-permute-start.17
  223.9 7.5 %all-to-all-start.3 = ((bf16[32,8,1792]{2,1,0:T(8,128)(2,1)}), bf16[32,8,1792]{2,1,0:T(8,128)(2,1)S(1)}, u32[]{:S(2)}, u32[]{:S(2)}) async-start(bf16[32,8,1792]{2,1,0:T(8,128)(2,1)} %shard_map.281.refs_2_.refs_0_), calls=%async_computation.3 | async-start | bytes 1835008 | tf_op jit(solution)/shard_map/all_to_all | solution.py:699
  231.4 9.4 %collective-permute-done.17.sent.refs_11_ = bf16[128,2816]{1,0:T(8,128)(2,1)S(1)} collective-permute-done((bf16[128,2816]{1,0:T(8,128)(2,1)}, bf16[128,2816]{1,0:T(8,128)(2,1)S(1)}, u32[]{:S(2)}, u32[]{:S(2)}) %collective-permute-start.17) | collective-permute-done | bytes 720928 | tf_op jit(solution)/shard_map/ppermute | solution.py:50
  243.7 3.1 shard_map.287
  247.1 3.5 shard_map.286
  253.0 9.4 %shard_map.288 = bf16[512,7168]{1,0:T(8,128)(2,1)} custom-call(s32[1]{0:T(128)} %constant.28.clone.1.core, bf16[512,256]{1,0:T(8,128)(2,1)} %get-tuple-element.125.refs_0_, bf16[512,256]{1,0:T(8,128)(2,1)} %copy-done.18, bf16[512,256]{1,0:T(8,128)(2,1)} %get-tuple-element.127.refs_2_, bf16[512,256]{1,0:T(8,128)(2,1)} %copy-done.28, ...), custom_call_target="tpu_custom_call" | custom-call | tf_op jit(solution)/shard_map/pallas_call | solution.py:592
  264.2 3.4 shard_map.290.refs_2_.key_value
  272.2 4.8 %shard_map.294 = bf16[512,2816]{1,0:T(8,128)(2,1)} custom-call(s32[1]{0:T(128)} %constant.28.clone.1.core, bf16[512,256]{1,0:T(8,128)(2,1)} %get-tuple-element.142.refs_0_, bf16[512,256]{1,0:T(8,128)(2,1)} %copy-done.19, bf16[128,2816]{1,0:T(8,128)(2,1)} %get-tuple-element.133.gate_query.refs_2_, ...), custom_call_target="tpu_custom_call" | custom-call | flops 99999997952 | tf_op jit(solution)/shard_map/pallas_call | solution.py:592
  277.0 7.2 %all-to-all-start.4 = ((bf16[16,32,2816]{2,1,0:T(8,128)(2,1)}), bf16[16,32,2816]{2,1,0:T(8,128)(2,1)S(1)}, u32[]{:S(2)}, u32[]{:S(2)}) async-start(bf16[16,32,2816]{2,1,0:T(8,128)(2,1)} %bitcast.50), calls=%async_computation.4 | async-start | bytes 5767168 | tf_op jit(solution)/shard_map/all_to_all | solution.py:617
  285.0 18.8 %collective-permute-done.23.key_value_theirs.refs_3_ = bf16[128,2816]{1,0:T(8,128)(2,1)S(1)} collective-permute-done((bf16[128,2816]{1,0:T(8,128)(2,1)}, bf16[128,2816]{1,0:T(8,128)(2,1)S(1)}, u32[]{:S(2)}, u32[]{:S(2)}) %collective-permute-start.23) | collective-permute-done | bytes 720928 | tf_op jit(solution)/shard_map/ppermute | solution.py:50
  304.6 9.2 %shard_map.292 = (bf16[128,1024]{1,0:T(8,128)(2,1)}, bf16[128,1024]{1,0:T(8,128)(2,1)}) custom-call(bf16[128,2816]{1,0:T(8,128)(2,1)} %get-tuple-element.133.gate_query.refs_2_, bf16[128,2816]{1,0:T(8,128)(2,1)} %get-tuple-element.134.gate_query_theirs.refs_3_, bf16[128,2816]{1,0:T(8,128)(2,1)} %shard_map.290.refs_2_.key_value, ...), custom_call_target="tpu_custom_call" | custom-call | tf_op jit(solution)/shard_map/pallas_call | solution.py:76
  317.9 5.4 %collective-permute-done.24.theirs = bf16[128,1024]{1,0:T(8,128)(2,1)S(1)} collective-permute-done((bf16[128,1024]{1,0:T(8,128)(2,1)}, bf16[128,1024]{1,0:T(8,128)(2,1)S(1)}, u32[]{:S(2)}, u32[]{:S(2)}) %collective-permute-start.24) | collective-permute-done | bytes 262176 | tf_op jit(solution)/shard_map/ppermute | solution.py:58
  323.2 5.7 %collective-permute-done.26.helped_other = bf16[128,1024]{1,0:T(8,128)(2,1)S(1)} collective-permute-done((bf16[128,1024]{1,0:T(8,128)(2,1)}, bf16[128,1024]{1,0:T(8,128)(2,1)S(1)}, u32[]{:S(2)}, u32[]{:S(2)}) %collective-permute-start.26) | collective-permute-done | bytes 262176 | tf_op jit(solution)/shard_map/ppermute | solution.py:825
  329.7 3.6 shard_map.293
  342.2 5.5 %shard_map.295 = bf16[512,2816]{1,0:T(8,128)(2,1)} custom-call(s32[1]{0:T(128)S(6)} %select_n.7.core, bf16[512,256]{1,0:T(8,128)(2,1)} %get-tuple-element.142.refs_0_, bf16[512,256]{1,0:T(8,128)(2,1)} %copy-done.19, bf16[128,2816]{1,0:T(8,128)(2,1)} %shard_map.290.refs_2_.key_value, bf16[128,2816]{1,0:T(8,128)(2,1)} %copy-done.12, ...), custom_call_target="tpu_custom_call" | custom-call | tf_op jit(solution)/shard_map/pallas_call | solution.py:592
  347.7 7.0 %all-to-all-start.5 = ((bf16[16,32,2816]{2,1,0:T(8,128)(2,1)}), bf16[16,32,2816]{2,1,0:T(8,128)(2,1)S(1)}, u32[]{:S(2)}, u32[]{:S(2)}) async-start(bf16[16,32,2816]{2,1,0:T(8,128)(2,1)} %bitcast.47), calls=%async_computation.5 | async-start | bytes 5767168 | tf_op jit(solution)/shard_map/all_to_all | solution.py:617
  354.8 5.0 %shard_map.283.mine = bf16[256,1024]{1,0:T(8,128)(2,1)} custom-call(bf16[128,6400]{1,0:T(8,128)(2,1)} %get-tuple-element.119.own.refs_6_, bf16[128,6400]{1,0:T(8,128)(2,1)} %get-tuple-element.120.theirs.sent.refs_7_, bf16[1728,1024]{1,0:T(8,128)(2,1)} %weight.3), custom_call_target="tpu_custom_call" | custom-call | tf_op jit(solution)/shard_map/pallas_call | solution.py:76
  360.9 11.7 %collective-permute-done.13.theirs = bf16[256,1024]{1,0:T(8,128)(2,1)S(1)} collective-permute-done((bf16[256,1024]{1,0:T(8,128)(2,1)}, bf16[256,1024]{1,0:T(8,128)(2,1)S(1)}, u32[]{:S(2)}, u32[]{:S(2)}) %collective-permute-start.13) | collective-permute-done | bytes 524320 | tf_op jit(solution)/shard_map/ppermute | solution.py:58
  378.0 5.7 %collective-permute-done.14.oth = bf16[128,1024]{1,0:T(8,128)(2,1)S(1)} collective-permute-done((bf16[128,1024]{1,0:T(8,128)(2,1)}, bf16[128,1024]{1,0:T(8,128)(2,1)S(1)}, u32[]{:S(2)}, u32[]{:S(2)}) %collective-permute-start.14) | collective-permute-done | bytes 262176 | tf_op jit(solution)/shard_map/ppermute | solution.py:50
  388.5 4.6 %all-to-all-done.5.parts = bf16[16,32,2816]{2,1,0:T(8,128)(2,1)S(1)} async-done(((bf16[16,32,2816]{2,1,0:T(8,128)(2,1)}), bf16[16,32,2816]{2,1,0:T(8,128)(2,1)S(1)}, u32[]{:S(2)}, u32[]{:S(2)}) %all-to-all-start.5) | async-done | bytes 2883616 | tf_op jit(solution)/shard_map/all_to_all | solution.py:617
  399.1 9.1 %reduce-scatter.4.cloned.1.call-done = bf16[1,32,7168]{2,1,0:T(8,128)(2,1)} async-done(((bf16[16,32,7168]{2,1,0:T(8,128)(2,1)}), bf16[1,32,7168]{2,1,0:T(8,128)(2,1)}) %reduce-scatter.4.cloned.1.call-update) | async-done | bytes 458768
  (165 shorter events, 84.4 us)
Async XLA Ops:
  7.2 125.3 %all-gather.2.cloned.1.call-start = ((), (), s32[]{:S(2)}) async-start(), calls=%async_computation.7 | async-start | bytes 11354112 | tf_op jit(solution)/shard_map/all_gather | solution.py:693
  11.2 9.8 %collective-permute-start = (bf16[128,1024]{1,0:T(8,128)(2,1)}, bf16[128,1024]{1,0:T(8,128)(2,1)S(1)}, u32[]{:S(2)}, u32[]{:S(2)}) collective-permute-start(bf16[128,1024]{1,0:T(8,128)(2,1)} %get-tuple-element.82), channel_id=1, source_target_pairs={{0,64},{64,0},{1,65},{65,1},{2,66},{66,2},{3,67},{67,3},{4,68},{68... | collective-permute-start | bytes 786440 | tf_op jit(solution)/shard_map/ppermute | solution.py:50
  21.7 16.3 %collective-permute-start.6 = (bf16[32,5376]{1,0:T(8,128)(2,1)}, bf16[32,5376]{1,0:T(8,128)(2,1)S(1)}, u32[]{:S(2)}, u32[]{:S(2)}) collective-permute-start(bf16[32,5376]{1,0:T(8,128)(2,1)} %shard_map.272), channel_id=1, source_target_pairs={{0,64},{64,0},{1,65},{65,1},{2,66},{66,2},{3,67},{67,3},{4,68},{68... | collective-permute-start | bytes 1032200 | tf_op jit(solution)/shard_map/ppermute | solution.py:50
  26.7 11.3 %collective-permute-start.5 = (bf16[128,1024]{1,0:T(8,128)(2,1)}, bf16[128,1024]{1,0:T(8,128)(2,1)S(1)}, u32[]{:S(2)}, u32[]{:S(2)}) collective-permute-start(bf16[128,1024]{1,0:T(8,128)(2,1)} %get-tuple-element.96.up_oth), channel_id=1, source_target_pairs={{0,64},{64,0},{1,65},{65,1},{2,66},{66,2},{3,67},{67,3},{4,68},{68... | collective-permute-start | bytes 786440 | tf_op jit(solution)/shard_map/ppermute | solution.py:50
  32.4 11.4 %copy-start.38 = (s32[1,128]{1,0:T(1,128)S(1)}, s32[1,128]{1,0:T(1,128)}, u32[]{:S(2)}) copy-start(s32[1,128]{1,0:T(1,128)} %param.17) | copy-start | bytes 1540
  38.9 24.5 %collective-permute-start.2 = (f32[128,1024]{1,0:T(8,128)}, f32[128,1024]{1,0:T(8,128)S(1)}, u32[]{:S(2)}, u32[]{:S(2)}) collective-permute-start(f32[128,1024]{1,0:T(8,128)} %get-tuple-element.83._), channel_id=1, source_target_pairs={{0,64},{64,0},{1,65},{65,1},{2,66},{66,2},{3,67},{67,3},{4,68},{68... | collective-permute-start | bytes 1572872 | tf_op jit(solution)/shard_map/ppermute | solution.py:50
  43.2 19.2 %collective-permute-start.3 = (f16[128,1728]{1,0:T(8,128)(2,1)S(1)}, f16[128,1728]{1,0:T(8,128)(2,1)S(1)}, u32[]{:S(2)}, u32[]{:S(2)}) collective-permute-start(f16[128,1728]{1,0:T(8,128)(2,1)S(1)} %convert_element_type.43), channel_id=1, source_target_pairs={{0,64},{64,0},{1,65},{65,1},{2,66},{66,2},{3,67},{67,3},{4,68},{68... | collective-permute-start | bytes 1327112 | tf_op jit(solution)/shard_map/ppermute | solution.py:54
  63.4 12.9 %copy-start.24 = (f32[128,1024]{1,0:T(8,128)S(1)}, f32[128,1024]{1,0:T(8,128)}, u32[]{:S(2)}) copy-start(f32[128,1024]{1,0:T(8,128)} %get-tuple-element.85._) | copy-start | bytes 1572868
  63.4 16.0 %copy-start.20 = (f32[128,1728]{1,0:T(8,128)S(1)}, f32[128,1728]{1,0:T(8,128)}, u32[]{:S(2)}) copy-start(f32[128,1728]{1,0:T(8,128)} %get-tuple-element.94) | copy-start | bytes 2654212
  67.7 35.0 %all-to-all-start = ((bf16[32,8,1792]{2,1,0:T(8,128)(2,1)}), bf16[32,8,1792]{2,1,0:T(8,128)(2,1)S(1)}, u32[]{:S(2)}, u32[]{:S(2)}) async-start(bf16[32,8,1792]{2,1,0:T(8,128)(2,1)} %bitcast.53), calls=%async_computation | async-start | bytes 1835008 | tf_op jit(solution)/shard_map/all_to_all | solution.py:697
  76.3 26.4 %collective-permute-start.1 = (f32[128,1024]{1,0:T(8,128)S(1)}, f32[128,1024]{1,0:T(8,128)S(1)}, u32[]{:S(2)}, u32[]{:S(2)}) collective-permute-start(f32[128,1024]{1,0:T(8,128)S(1)} %copy-done.24), channel_id=1, source_target_pairs={{0,64},{64,0},{1,65},{65,1},{2,66},{66,2},{3,67},{67,3},{4,68},{68... | collective-permute-start | bytes 1572872 | tf_op jit(solution)/shard_map/ppermute | solution.py:50
  79.4 22.2 %collective-permute-start.4 = (f16[128,1728]{1,0:T(8,128)(2,1)S(1)}, f16[128,1728]{1,0:T(8,128)(2,1)S(1)}, u32[]{:S(2)}, u32[]{:S(2)}) collective-permute-start(f16[128,1728]{1,0:T(8,128)(2,1)S(1)} %convert_element_type.45), channel_id=1, source_target_pairs={{0,64},{64,0},{1,65},{65,1},{2,66},{66,2},{3,67},{67,3},{4,68},{68... | collective-permute-start | bytes 1327112 | tf_op jit(solution)/shard_map/ppermute | solution.py:54
  103.8 10.0 %copy-start.10 = (f32[128,1728]{1,0:T(8,128)S(1)}, f32[128,1728]{1,0:T(8,128)}, u32[]{:S(2)}) copy-start(f32[128,1728]{1,0:T(8,128)} %get-tuple-element.97.refs_2_) | copy-start | bytes 2654212
  106.3 26.1 %all-to-all-start.1 = ((bf16[32,8,1792]{2,1,0:T(8,128)(2,1)}), bf16[32,8,1792]{2,1,0:T(8,128)(2,1)S(1)}, u32[]{:S(2)}, u32[]{:S(2)}) async-start(bf16[32,8,1792]{2,1,0:T(8,128)(2,1)} %shard_map.271), calls=%async_computation.1 | async-start | bytes 1835008 | tf_op jit(solution)/shard_map/all_to_all | solution.py:699
  113.8 14.3 %collective-permute-start.7 = (f16[128,1728]{1,0:T(8,128)(2,1)S(1)}, f16[128,1728]{1,0:T(8,128)(2,1)S(1)}, u32[]{:S(2)}, u32[]{:S(2)}) collective-permute-start(f16[128,1728]{1,0:T(8,128)(2,1)S(1)} %convert_element_type.47), channel_id=1, source_target_pairs={{0,64},{64,0},{1,65},{65,1},{2,66},{66,2},{3,67},{67,3},{4,68},{68... | collective-permute-start | bytes 1327112 | tf_op jit(solution)/shard_map/ppermute | solution.py:54
  140.8 13.4 %collective-permute-start.8 = (bf16[128,2048]{1,0:T(8,128)(2,1)}, bf16[128,2048]{1,0:T(8,128)(2,1)S(1)}, u32[]{:S(2)}, u32[]{:S(2)}) collective-permute-start(bf16[128,2048]{1,0:T(8,128)(2,1)} %get-tuple-element.100.mine), channel_id=1, source_target_pairs={{0,1},{1,0},{2,3},{3,2},{4,5},{5,4},{6,7},{7,6},{8,9},{9,8},{10,11... | collective-permute-start | bytes 1572872 | tf_op jit(solution)/shard_map/ppermute | solution.py:58
  145.3 3.5 collective-permute-start.9
  148.3 1.9 collective-permute-start.10
  168.8 12.7 %collective-permute-start.11 = (bf16[128,2048]{1,0:T(8,128)(2,1)}, bf16[128,2048]{1,0:T(8,128)(2,1)S(1)}, u32[]{:S(2)}, u32[]{:S(2)}) collective-permute-start(bf16[128,2048]{1,0:T(8,128)(2,1)} %get-tuple-element.106.mine), channel_id=1, source_target_pairs={{0,1},{1,0},{2,3},{3,2},{4,5},{5,4},{6,7},{7,6},{8,9},{9,8},{10,11... | collective-permute-start | bytes 1572872 | tf_op jit(solution)/shard_map/ppermute | solution.py:58
  182.3 36.9 %collective-permute-start.12 = (bf16[128,6400]{1,0:T(8,128)(2,1)}, bf16[128,6400]{1,0:T(8,128)(2,1)S(1)}, u32[]{:S(2)}, u32[]{:S(2)}) collective-permute-start(bf16[128,6400]{1,0:T(8,128)(2,1)} %shard_map.278.refs_0_), channel_id=1, source_target_pairs={{0,64},{64,0},{1,65},{65,1},{2,66},{66,2},{3,67},{67,3},{4,68},{68... | collective-permute-start | bytes 4915208 | tf_op jit(solution)/shard_map/ppermute | solution.py:50
  194.6 20.5 %all-to-all-start.2 = ((bf16[32,8,1792]{2,1,0:T(8,128)(2,1)}), bf16[32,8,1792]{2,1,0:T(8,128)(2,1)S(1)}, u32[]{:S(2)}, u32[]{:S(2)}) async-start(bf16[32,8,1792]{2,1,0:T(8,128)(2,1)} %bitcast.54), calls=%async_computation.2 | async-start | bytes 1835008 | tf_op jit(solution)/shard_map/all_to_all | solution.py:697
  218.5 22.3 %copy-start.6 = (bf16[128,2816]{1,0:T(8,128)(2,1)S(1)}, bf16[128,2816]{1,0:T(8,128)(2,1)}, u32[]{:S(2)}) copy-start(bf16[128,2816]{1,0:T(8,128)(2,1)} %get-tuple-element.118.refs_0_) | copy-start | bytes 2162692
  220.3 32.0 %collective-permute-start.19 = (bf16[128,6400]{1,0:T(8,128)(2,1)}, bf16[128,6400]{1,0:T(8,128)(2,1)}, u32[]{:S(2)}, u32[]{:S(2)}) collective-permute-start(bf16[128,6400]{1,0:T(8,128)(2,1)} %get-tuple-element.119.own.refs_6_), channel_id=1, source_target_pairs={{0,2},{2,0},{4,6},{6,4},{8,10},{10,8},{12,14},{14,12},{16,18},{18,... | collective-permute-start | bytes 4915208 | tf_op jit(solution)/shard_map/ppermute | solution.py:62
  220.5 31.8 %collective-permute-start.20 = (bf16[128,6400]{1,0:T(8,128)(2,1)}, bf16[128,6400]{1,0:T(8,128)(2,1)}, u32[]{:S(2)}, u32[]{:S(2)}) collective-permute-start(bf16[128,6400]{1,0:T(8,128)(2,1)} %get-tuple-element.120.theirs.sent.refs_7_), channel_id=1, source_target_pairs={{0,2},{2,0},{4,6},{6,4},{8,10},{10,8},{12,14},{14,12},{16,18},{18,... | collective-permute-start | bytes 4915208 | tf_op jit(solution)/shard_map/ppermute | solution.py:62
  220.9 19.9 %collective-permute-start.17 = (bf16[128,2816]{1,0:T(8,128)(2,1)}, bf16[128,2816]{1,0:T(8,128)(2,1)S(1)}, u32[]{:S(2)}, u32[]{:S(2)}) collective-permute-start(bf16[128,2816]{1,0:T(8,128)(2,1)} %get-tuple-element.130.refs_10_), channel_id=1, source_target_pairs={{0,64},{64,0},{1,65},{65,1},{2,66},{66,2},{3,67},{67,3},{4,68},{68... | collective-permute-start | bytes 2162696 | tf_op jit(solution)/shard_map/ppermute | solution.py:50
  223.9 23.0 %collective-permute-start.21 = (bf16[128,2816]{1,0:T(8,128)(2,1)}, bf16[128,2816]{1,0:T(8,128)(2,1)}, u32[]{:S(2)}, u32[]{:S(2)}) collective-permute-start(bf16[128,2816]{1,0:T(8,128)(2,1)} %get-tuple-element.130.refs_10_), channel_id=1, source_target_pairs={{0,2},{2,0},{4,6},{6,4},{8,10},{10,8},{12,14},{14,12},{16,18},{18,... | collective-permute-start | bytes 2162696 | tf_op jit(solution)/shard_map/ppermute | solution.py:62
  223.9 38.5 %all-to-all-start.3 = ((bf16[32,8,1792]{2,1,0:T(8,128)(2,1)}), bf16[32,8,1792]{2,1,0:T(8,128)(2,1)S(1)}, u32[]{:S(2)}, u32[]{:S(2)}) async-start(bf16[32,8,1792]{2,1,0:T(8,128)(2,1)} %shard_map.281.refs_2_.refs_0_), calls=%async_computation.3 | async-start | bytes 1835008 | tf_op jit(solution)/shard_map/all_to_all | solution.py:699
  231.4 176.9 %reduce-scatter.4.cloned.1.call-start = ((), (), s32[]{:S(2)}) async-start(), calls=%async_computation.8 | async-start | bytes 7798784
  240.8 10.1 %collective-permute-start.22 = (bf16[128,2816]{1,0:T(8,128)(2,1)S(1)}, bf16[128,2816]{1,0:T(8,128)(2,1)S(1)}, u32[]{:S(2)}, u32[]{:S(2)}) collective-permute-start(bf16[128,2816]{1,0:T(8,128)(2,1)S(1)} %collective-permute-done.17.sent.refs_11_), channel_id=1, source_target_pairs={{0,2},{2,0},{4,6},{6,4},{8,10},{10,8},{12,14},{14,12},{16,18},{18,... | collective-permute-start | bytes 2162696 | tf_op jit(solution)/shard_map/ppermute | solution.py:62
  240.8 22.6 %collective-permute-start.15 = (bf16[128,2816]{1,0:T(8,128)(2,1)S(1)}, bf16[128,2816]{1,0:T(8,128)(2,1)S(1)}, u32[]{:S(2)}, u32[]{:S(2)}) collective-permute-start(bf16[128,2816]{1,0:T(8,128)(2,1)S(1)} %copy-done.6), channel_id=1, source_target_pairs={{0,64},{64,0},{1,65},{65,1},{2,66},{66,2},{3,67},{67,3},{4,68},{68... | collective-permute-start | bytes 2162696 | tf_op jit(solution)/shard_map/ppermute | solution.py:50
  246.9 3.7 collective-permute-start.18
  250.6 1.7 collective-permute-start.16
  267.6 2.7 collective-permute-start.32
  268.3 3.1 collective-permute-start.33
  277.0 63.0 %all-to-all-start.4 = ((bf16[16,32,2816]{2,1,0:T(8,128)(2,1)}), bf16[16,32,2816]{2,1,0:T(8,128)(2,1)S(1)}, u32[]{:S(2)}, u32[]{:S(2)}) async-start(bf16[16,32,2816]{2,1,0:T(8,128)(2,1)} %bitcast.50), calls=%async_computation.4 | async-start | bytes 5767168 | tf_op jit(solution)/shard_map/all_to_all | solution.py:617
  284.2 19.5 %collective-permute-start.23 = (bf16[128,2816]{1,0:T(8,128)(2,1)}, bf16[128,2816]{1,0:T(8,128)(2,1)S(1)}, u32[]{:S(2)}, u32[]{:S(2)}) collective-permute-start(bf16[128,2816]{1,0:T(8,128)(2,1)} %shard_map.290.refs_2_.key_value), channel_id=1, source_target_pairs={{0,64},{64,0},{1,65},{65,1},{2,66},{66,2},{3,67},{67,3},{4,68},{68... | collective-permute-start | bytes 2162696 | tf_op jit(solution)/shard_map/ppermute | solution.py:50
  285.0 52.0 %collective-permute-start.27 = (bf16[128,2816]{1,0:T(8,128)(2,1)}, bf16[128,2816]{1,0:T(8,128)(2,1)S(1)}, u32[]{:S(2)}, u32[]{:S(2)}) collective-permute-start(bf16[128,2816]{1,0:T(8,128)(2,1)} %shard_map.290.refs_2_.key_value), channel_id=1, source_target_pairs={{0,2},{2,0},{4,6},{6,4},{8,10},{10,8},{12,14},{14,12},{16,18},{18,... | collective-permute-start | bytes 2162696 | tf_op jit(solution)/shard_map/ppermute | solution.py:62
  303.8 36.3 %collective-permute-start.28 = (bf16[128,2816]{1,0:T(8,128)(2,1)S(1)}, bf16[128,2816]{1,0:T(8,128)(2,1)}, u32[]{:S(2)}, u32[]{:S(2)}) collective-permute-start(bf16[128,2816]{1,0:T(8,128)(2,1)S(1)} %collective-permute-done.23.key_value_theirs.refs_3_), channel_id=1, source_target_pairs={{0,2},{2,0},{4,6},{6,4},{8,10},{10,8},{12,14},{14,12},{16,18},{18,... | collective-permute-start | bytes 2162696 | tf_op jit(solution)/shard_map/ppermute | solution.py:62
  313.8 9.4 %collective-permute-start.24 = (bf16[128,1024]{1,0:T(8,128)(2,1)}, bf16[128,1024]{1,0:T(8,128)(2,1)S(1)}, u32[]{:S(2)}, u32[]{:S(2)}) collective-permute-start(bf16[128,1024]{1,0:T(8,128)(2,1)} %get-tuple-element.135.mine), channel_id=1, source_target_pairs={{0,1},{1,0},{2,3},{3,2},{4,5},{5,4},{6,7},{7,6},{8,9},{9,8},{10,11... | collective-permute-start | bytes 786440 | tf_op jit(solution)/shard_map/ppermute | solution.py:58
  314.4 14.5 %collective-permute-start.26 = (bf16[128,1024]{1,0:T(8,128)(2,1)}, bf16[128,1024]{1,0:T(8,128)(2,1)S(1)}, u32[]{:S(2)}, u32[]{:S(2)}) collective-permute-start(bf16[128,1024]{1,0:T(8,128)(2,1)} %get-tuple-element.136), channel_id=1, source_target_pairs={{0,65},{1,64},{64,1},{65,0},{2,67},{3,66},{66,3},{67,2},{4,69},{5,... | collective-permute-start | bytes 786440 | tf_op jit(solution)/shard_map/ppermute | solution.py:825
  314.9 14.0 %collective-permute-start.25 = (bf16[128,1024]{1,0:T(8,128)(2,1)}, bf16[128,1024]{1,0:T(8,128)(2,1)S(1)}, u32[]{:S(2)}, u32[]{:S(2)}) collective-permute-start(bf16[128,1024]{1,0:T(8,128)(2,1)} %get-tuple-element.136), channel_id=1, source_target_pairs={{0,64},{64,0},{1,65},{65,1},{2,66},{66,2},{3,67},{67,3},{4,68},{68... | collective-permute-start | bytes 786440 | tf_op jit(solution)/shard_map/ppermute | solution.py:50
  333.3 3.7 collective-permute-start.30
  333.3 5.1 %collective-permute-start.31 = (bf16[16,1024]{1,0:T(8,128)(2,1)}, bf16[16,1024]{1,0:T(8,128)(2,1)S(1)}, u32[]{:S(2)}, u32[]{:S(2)}) collective-permute-start(bf16[16,1024]{1,0:T(8,128)(2,1)} %get-tuple-element.144), channel_id=1, source_target_pairs={{0,66},{2,64},{4,70},{6,68},{8,74},{10,72},{12,78},{14,76},{16,82}... | collective-permute-start | bytes 98312 | tf_op jit(solution)/shard_map/ppermute | solution.py:832
  334.4 5.6 %collective-permute-start.29 = (bf16[16,1024]{1,0:T(8,128)(2,1)}, bf16[16,1024]{1,0:T(8,128)(2,1)S(1)}, u32[]{:S(2)}, u32[]{:S(2)}) collective-permute-start(bf16[16,1024]{1,0:T(8,128)(2,1)} %get-tuple-element.144), channel_id=1, source_target_pairs={{0,64},{64,0},{1,65},{65,1},{2,66},{66,2},{3,67},{67,3},{4,68},{68... | collective-permute-start | bytes 98312 | tf_op jit(solution)/shard_map/ppermute | solution.py:50
  347.7 45.4 %all-to-all-start.5 = ((bf16[16,32,2816]{2,1,0:T(8,128)(2,1)}), bf16[16,32,2816]{2,1,0:T(8,128)(2,1)S(1)}, u32[]{:S(2)}, u32[]{:S(2)}) async-start(bf16[16,32,2816]{2,1,0:T(8,128)(2,1)} %bitcast.47), calls=%async_computation.5 | async-start | bytes 5767168 | tf_op jit(solution)/shard_map/all_to_all | solution.py:617
  359.8 26.9 %copy-start.2 = (bf16[16,32,2816]{2,1,0:T(8,128)(2,1)S(1)}, bf16[16,32,2816]{2,1,0:T(8,128)(2,1)}, u32[]{:S(2)}) copy-start(bf16[16,32,2816]{2,1,0:T(8,128)(2,1)} %copy-done.1) | copy-start | bytes 8650756
  359.8 12.8 %collective-permute-start.13 = (bf16[256,1024]{1,0:T(8,128)(2,1)}, bf16[256,1024]{1,0:T(8,128)(2,1)S(1)}, u32[]{:S(2)}, u32[]{:S(2)}) collective-permute-start(bf16[256,1024]{1,0:T(8,128)(2,1)} %shard_map.283.mine), channel_id=1, source_target_pairs={{0,1},{1,0},{2,3},{3,2},{4,5},{5,4},{6,7},{7,6},{8,9},{9,8},{10,11... | collective-permute-start | bytes 1572872 | tf_op jit(solution)/shard_map/ppermute | solution.py:58
  375.6 8.1 %collective-permute-start.14 = (bf16[128,1024]{1,0:T(8,128)(2,1)}, bf16[128,1024]{1,0:T(8,128)(2,1)S(1)}, u32[]{:S(2)}, u32[]{:S(2)}) collective-permute-start(bf16[128,1024]{1,0:T(8,128)(2,1)} %get-tuple-element.122), channel_id=1, source_target_pairs={{0,64},{64,0},{1,65},{65,1},{2,66},{66,2},{3,67},{67,3},{4,68},{68... | collective-permute-start | bytes 786440 | tf_op jit(solution)/shard_map/ppermute | solution.py:50
  (33 other events, 50.7 us)
Sparse Core Ops, SparseCore 0:
  39.0 71.2 all-gather.1
  268.6 139.6 reduce-scatter.3

commit v4 on v3

--- a/solution.py
+++ b/solution.py
@@ -690,7 +690,7 @@
 
     up_own, up_oth = run(turn_kernel, (small, small), [shard], [upstream])
     up_theirs = from_shard(up_oth)
-    others = lax.all_gather(after(packed, theirs_value, up_theirs), "ctx", axis=0, tiled=True)
+    others = lax.all_gather(after(packed, theirs_value), "ctx", axis=0, tiled=True)
 
 
     def exchange(states, reverse, *before):
@@ -713,7 +713,7 @@
         [up_own, up_theirs, mlp_down],
     )
     helped_hidden = half_from_shard(theirs_hidden)
-    incoming, _, _ = exchange(local, False, helped_query, helped_gate, theirs_hidden)
+    incoming, _, _ = exchange(local, False, helped_query, theirs_hidden)
     queries, inner, masked = run(
         inner_kernel,
         (small, shape(PIECE, VPAD, kind=F32), shape(HEADS, PIECE, PIECE)),

time: 425 us -> 429 us (level)
    ppermute x12, waiting for transfers between devices: 48.6 us -> 61 us  [from_shard(): return lax.ppermute(part, 'shard', SWAP)]
    ppermute x3, waiting for transfers between devices: 31.9 us -> 23 us  [half_from_shard(): return lax.ppermute(part.astype(F16), 'shard', SWAP).astype(F32)]
  transfers between devices with their start and end apart: 42 -> 42, of which waited for: 23 -> 24; matrix products, arithmetic and copies ran while one was open for 2% -> 2% of each run, Pallas kernels for 26% -> 26%
where the time goes in v4:
time: 429 us; the launch traced here: 421 us
  waiting for transfers between devices  150 us (35%)
  Pallas kernels  137 us (32%)
  starting transfers between devices  89.3 us (21%)
  local copies, waits for them, and re-layouts  23.5 us (5%)
  between operations  14.8 us (3%)
  other arithmetic  6.3 us (1%)
    pallas_call x25, Pallas kernels, run(): pl.pallas_call(kernel, out_shape=outs, grid=(1,), in_specs=[SMEM] * len(s...  117 us
    ppermute x12, waiting for transfers between devices, from_shard(): return lax.ppermute(part, 'shard', SWAP)  61 us
    ppermute x4, waiting for transfers between devices, from_tp(): return lax.ppermute(part, 'tp', SWAP)  32.1 us
    ppermute x12, starting transfers between devices, from_shard(): return lax.ppermute(part, 'shard', SWAP)  30.4 us
    ppermute x3, waiting for transfers between devices, half_from_shard(): return lax.ppermute(part.astype(F16), 'shard', SWAP).astype(F32)  23 us
    pallas_call x3, Pallas kernels, outer(): pl.pallas_call(kernel, out_shape=shape(HALF // 2, width), grid_spec=pltpu...  19.7 us
    unnamed x78, local copies, waits for them, and re-layouts  19 us
    all_to_all x2, starting transfers between devices, exchange(): lax.all_to_all(states.reshape(NC, KH // NC, VPAD), 'ctx', 0, 0, tiled=True)  15.9 us
  transfers between devices with their start and end apart: 42, of which 24 were waited for; matrix products, arithmetic and copies ran while one was open for 2% of the time, Pallas kernels for 26%

profile of v4, /device:TPU:8, one launch (start us, length us, event | category | flops | bytes accessed | tf_op | source)
XLA Modules:
  0.0 420.7 jit_solution(1795317662714347441)
XLA Ops:
  7.2 3.9 shard_map.263
  11.2 3.1 collective-permute-start
  14.3 6.7 %collective-permute-done.low.refs_1_ = bf16[128,1024]{1,0:T(8,128)(2,1)S(1)} collective-permute-done((bf16[128,1024]{1,0:T(8,128)(2,1)}, bf16[128,1024]{1,0:T(8,128)(2,1)S(1)}, u32[]{:S(2)}, u32[]{:S(2)}) %collective-permute-start) | collective-permute-done | bytes 262176 | tf_op jit(solution)/shard_map/ppermute | solution.py:50
  21.7 3.0 collective-permute-start.6
  24.8 5.2 %shard_map.264 = (f32[128,1024]{1,0:T(8,128)}, f32[128,1728]{1,0:T(8,128)}) custom-call(bf16[128,1024]{1,0:T(8,128)(2,1)} %copy-done.8, bf16[1024,1024]{1,0:T(8,128)(2,1)} %key_weight.5, bf16[1728,1024]{1,0:T(8,128)(2,1)} %bitcast.34), custom_call_target="tpu_custom_call" | custom-call | tf_op jit(solution)/shard_map/pallas_call | solution.py:76
  33.1 3.1 collective-permute-start.2
  39.3 8.2 %shard_map.265 = (f32[128,1024]{1,0:T(8,128)}, f32[128,1024]{1,0:T(8,128)}, f32[128,1728]{1,0:T(8,128)}, f32[128,1728]{1,0:T(8,128)}) custom-call(bf16[128,1024]{1,0:T(8,128)(2,1)} %get-tuple-element.81.low.refs_0_, bf16[1024,1024]{1,0:T(8,128)(2,1)} %query_weight.5, bf16[1024,1024]{1,0:T(8,128)(2,1)} %key_weight.5, bf16[1728,1024]{1,0:T(8,128)(2,1)} %bitcast.35, ...), custom_call_target="tpu_custom_call" | custom-call | tf_op jit(solution)/shard_map/pallas_call | solution.py:76
  47.5 5.2 %shard_map.266 = (f32[128,1024]{1,0:T(8,128)}, f32[128,1728]{1,0:T(8,128)}) custom-call(bf16[128,1024]{1,0:T(8,128)(2,1)} %copy-done.8, bf16[1024,1024]{1,0:T(8,128)(2,1)} %query_weight.5, bf16[1728,1024]{1,0:T(8,128)(2,1)} %bitcast.38), custom_call_target="tpu_custom_call" | custom-call | tf_op jit(solution)/shard_map/pallas_call | solution.py:76
  52.8 3.9 collective-permute-done.3
  58.4 3.5 shard_map.267
  61.9 8.5 %all-to-all-start = ((bf16[32,8,1792]{2,1,0:T(8,128)(2,1)}), bf16[32,8,1792]{2,1,0:T(8,128)(2,1)S(1)}, u32[]{:S(2)}, u32[]{:S(2)}) async-start(bf16[32,8,1792]{2,1,0:T(8,128)(2,1)} %bitcast.53), calls=%async_computation | async-start | bytes 1835008 | tf_op jit(solution)/shard_map/all_to_all | solution.py:697
  70.5 3.1 collective-permute-start.1
  76.0 15.7 %collective-permute-done.4.theirs.refs_1_ = bf16[128,1024]{1,0:T(8,128)(2,1)S(1)} collective-permute-done((bf16[128,1024]{1,0:T(8,128)(2,1)}, bf16[128,1024]{1,0:T(8,128)(2,1)S(1)}, u32[]{:S(2)}, u32[]{:S(2)}) %collective-permute-start.4) | collective-permute-done | bytes 262176 | tf_op jit(solution)/shard_map/ppermute | solution.py:50
  92.4 4.5 %shard_map.270 = (f32[128,1728]{1,0:T(8,128)}, f32[128,1728]{1,0:T(8,128)}) custom-call(bf16[128,1024]{1,0:T(8,128)(2,1)} %get-tuple-element.94.own.refs_0_.up_own, bf16[128,1024]{1,0:T(8,128)(2,1)} %copy-done.19, bf16[1728,1024]{1,0:T(8,128)(2,1)} %weight.3), custom_call_target="tpu_custom_call" | custom-call | tf_op jit(solution)/shard_map/pallas_call | solution.py:76
  100.6 7.6 %all-to-all-start.1 = ((bf16[32,8,1792]{2,1,0:T(8,128)(2,1)}), bf16[32,8,1792]{2,1,0:T(8,128)(2,1)S(1)}, u32[]{:S(2)}, u32[]{:S(2)}) async-start(bf16[32,8,1792]{2,1,0:T(8,128)(2,1)} %shard_map.271), calls=%async_computation.1 | async-start | bytes 1835008 | tf_op jit(solution)/shard_map/all_to_all | solution.py:699
  108.2 3.1 collective-permute-start.7
  112.2 11.0 %collective-permute-done.7 = f16[128,1728]{1,0:T(8,128)(2,1)S(1)} collective-permute-done((f16[128,1728]{1,0:T(8,128)(2,1)S(1)}, f16[128,1728]{1,0:T(8,128)(2,1)S(1)}, u32[]{:S(2)}, u32[]{:S(2)}) %collective-permute-start.7) | collective-permute-done | bytes 442400 | tf_op jit(solution)/shard_map/ppermute | solution.py:54
  124.2 8.1 %collective-permute-done.5 = f16[128,1728]{1,0:T(8,128)(2,1)S(1)} collective-permute-done((f16[128,1728]{1,0:T(8,128)(2,1)S(1)}, f16[128,1728]{1,0:T(8,128)(2,1)S(1)}, u32[]{:S(2)}, u32[]{:S(2)}) %collective-permute-start.5) | collective-permute-done | bytes 442400 | tf_op jit(solution)/shard_map/ppermute | solution.py:54
  133.3 3.3 shard_map.268
  137.5 7.4 %shard_map.274 = (f32[128,1728]{1,0:T(8,128)}, f32[128,1792]{1,0:T(8,128)}, f32[128,128]{1,0:T(8,128)}, bf16[128,1792]{1,0:T(8,128)(2,1)}, bf16[128,2048]{1,0:T(8,128)(2,1)}) custom-call(f32[4]{0:T(128)} %rates.15, f32[128,1]{1,0:T(8,128)} %copy.52.seg_column, bf16[128,1024]{1,0:T(8,128)(2,1)} %get-tuple-element.91.queries, ...), custom_call_target="tpu_custom_call" | custom-call | tf_op jit(solution)/shard_map/pallas_call | solution.py:76
  154.3 4.0 collective-permute-done.8.theirs
  159.1 13.8 %shard_map.277 = (f32[128,2048]{1,0:T(8,128)}, f32[128,2048]{1,0:T(8,128)}, f32[128,128]{1,0:T(8,128)}, bf16[128,1024]{1,0:T(8,128)(2,1)}, bf16[128,6400]{1,0:T(8,128)(2,1)}, /*index=5*/bf16[128,2048]{1,0:T(8,128)(2,1)}) custom-call(s32[1]{0:T(128)} %bitcast.shard, bf16[128,2048]{1,0:T(8,128)(2,1)} %bitcast.52, bf16[128,2048]{1,0:T(8,128)(2,1)} %get-tuple-element.100.mine, ...), custom_call_target="tpu_custom_call" | custom-call | tf_op jit(solution)/shard_map/pallas_call | solution.py:76
  174.7 10.9 %collective-permute-done.11.refs_1_.theirs = bf16[128,2048]{1,0:T(8,128)(2,1)S(1)} collective-permute-done((bf16[128,2048]{1,0:T(8,128)(2,1)}, bf16[128,2048]{1,0:T(8,128)(2,1)S(1)}, u32[]{:S(2)}, u32[]{:S(2)}) %collective-permute-start.11) | collective-permute-done | bytes 524320 | tf_op jit(solution)/shard_map/ppermute | solution.py:58
  189.4 9.3 %shard_map.279 = (f32[128,2048]{1,0:T(8,128)}, bf16[128,1024]{1,0:T(8,128)(2,1)}, bf16[128,1024]{1,0:T(8,128)(2,1)}, f32[8,2048]{1,0:T(8,128)}, bf16[128,1792]{1...) custom-call(s32[1]{0:T(128)} %bitcast.shard, f32[4]{0:T(128)} %rates.15, ...), custom_call_target="tpu_custom_call" | custom-call | tf_op jit(solution)/shard_map/pallas_call | solution.py:76
  198.7 7.4 %all-to-all-start.2 = ((bf16[32,8,1792]{2,1,0:T(8,128)(2,1)}), bf16[32,8,1792]{2,1,0:T(8,128)(2,1)S(1)}, u32[]{:S(2)}, u32[]{:S(2)}) async-start(bf16[32,8,1792]{2,1,0:T(8,128)(2,1)} %bitcast.54), calls=%async_computation.2 | async-start | bytes 1835008 | tf_op jit(solution)/shard_map/all_to_all | solution.py:697
  206.1 4.9 %shard_map.280 = (bf16[128,2816]{1,0:T(8,128)(2,1)}, bf16[128,2816]{1,0:T(8,128)(2,1)}, f32[128,1024]{1,0:T(8,128)}, f32[128,1792]{1,0:T(8,128)}) custom-call(f32[4]{0:T(128)} %rates.15, f32[128,1]{1,0:T(8,128)} %copy.52.seg_column, f32[1,128]{1,0:T(1,128)} %get-tuple-element.156.seg_row, bf16[128,1024]{1,0:T(8,128)(2,1)} %get-tuple-element.91.queries, ...), custom_call_target="tpu_custom_call" | custom-call | tf_op jit(solution)/shard_map/pallas_call | solution.py:76
  211.0 8.2 %all-to-all-done.2.states = bf16[32,8,1792]{2,1,0:T(8,128)(2,1)S(1)} async-done(((bf16[32,8,1792]{2,1,0:T(8,128)(2,1)}), bf16[32,8,1792]{2,1,0:T(8,128)(2,1)S(1)}, u32[]{:S(2)}, u32[]{:S(2)}) %all-to-all-start.2) | async-done | bytes 917536 | tf_op jit(solution)/shard_map/all_to_all | solution.py:697
  225.0 3.0 collective-permute-start.17
  228.0 7.5 %all-to-all-start.3 = ((bf16[32,8,1792]{2,1,0:T(8,128)(2,1)}), bf16[32,8,1792]{2,1,0:T(8,128)(2,1)S(1)}, u32[]{:S(2)}, u32[]{:S(2)}) async-start(bf16[32,8,1792]{2,1,0:T(8,128)(2,1)} %shard_map.281.refs_2_.refs_0_), calls=%async_computation.3 | async-start | bytes 1835008 | tf_op jit(solution)/shard_map/all_to_all | solution.py:699
  235.6 9.4 %collective-permute-done.17.sent.refs_11_ = bf16[128,2816]{1,0:T(8,128)(2,1)S(1)} collective-permute-done((bf16[128,2816]{1,0:T(8,128)(2,1)}, bf16[128,2816]{1,0:T(8,128)(2,1)S(1)}, u32[]{:S(2)}, u32[]{:S(2)}) %collective-permute-start.17) | collective-permute-done | bytes 720928 | tf_op jit(solution)/shard_map/ppermute | solution.py:50
  247.9 3.1 shard_map.287
  251.2 3.5 shard_map.286
  257.1 9.4 %shard_map.288 = bf16[512,7168]{1,0:T(8,128)(2,1)} custom-call(s32[1]{0:T(128)} %constant.28.clone.1.core, bf16[512,256]{1,0:T(8,128)(2,1)} %get-tuple-element.125.refs_0_, bf16[512,256]{1,0:T(8,128)(2,1)} %copy-done.17, bf16[512,256]{1,0:T(8,128)(2,1)} %get-tuple-element.127.refs_2_, bf16[512,256]{1,0:T(8,128)(2,1)} %copy-done.28, ...), custom_call_target="tpu_custom_call" | custom-call | tf_op jit(solution)/shard_map/pallas_call | solution.py:592
  268.4 3.4 shard_map.290.refs_2_.key_value
  276.3 4.8 %shard_map.294 = bf16[512,2816]{1,0:T(8,128)(2,1)} custom-call(s32[1]{0:T(128)} %constant.28.clone.1.core, bf16[512,256]{1,0:T(8,128)(2,1)} %get-tuple-element.142.refs_0_, bf16[512,256]{1,0:T(8,128)(2,1)} %copy-done.18, bf16[128,2816]{1,0:T(8,128)(2,1)} %get-tuple-element.133.gate_query.refs_2_, ...), custom_call_target="tpu_custom_call" | custom-call | flops 99999997952 | tf_op jit(solution)/shard_map/pallas_call | solution.py:592
  281.0 7.3 %all-to-all-start.4 = ((bf16[16,32,2816]{2,1,0:T(8,128)(2,1)}), bf16[16,32,2816]{2,1,0:T(8,128)(2,1)S(1)}, u32[]{:S(2)}, u32[]{:S(2)}) async-start(bf16[16,32,2816]{2,1,0:T(8,128)(2,1)} %bitcast.50), calls=%async_computation.4 | async-start | bytes 5767168 | tf_op jit(solution)/shard_map/all_to_all | solution.py:617
  289.1 18.8 %collective-permute-done.23.key_value_theirs.refs_3_ = bf16[128,2816]{1,0:T(8,128)(2,1)S(1)} collective-permute-done((bf16[128,2816]{1,0:T(8,128)(2,1)}, bf16[128,2816]{1,0:T(8,128)(2,1)S(1)}, u32[]{:S(2)}, u32[]{:S(2)}) %collective-permute-start.23) | collective-permute-done | bytes 720928 | tf_op jit(solution)/shard_map/ppermute | solution.py:50
  308.7 9.2 %shard_map.292 = (bf16[128,1024]{1,0:T(8,128)(2,1)}, bf16[128,1024]{1,0:T(8,128)(2,1)}) custom-call(bf16[128,2816]{1,0:T(8,128)(2,1)} %get-tuple-element.133.gate_query.refs_2_, bf16[128,2816]{1,0:T(8,128)(2,1)} %get-tuple-element.134.gate_query_theirs.refs_3_, bf16[128,2816]{1,0:T(8,128)(2,1)} %shard_map.290.refs_2_.key_value, ...), custom_call_target="tpu_custom_call" | custom-call | tf_op jit(solution)/shard_map/pallas_call | solution.py:76
  322.0 5.4 %collective-permute-done.24.theirs = bf16[128,1024]{1,0:T(8,128)(2,1)S(1)} collective-permute-done((bf16[128,1024]{1,0:T(8,128)(2,1)}, bf16[128,1024]{1,0:T(8,128)(2,1)S(1)}, u32[]{:S(2)}, u32[]{:S(2)}) %collective-permute-start.24) | collective-permute-done | bytes 262176 | tf_op jit(solution)/shard_map/ppermute | solution.py:58
  327.4 5.5 %collective-permute-done.26.helped_other = bf16[128,1024]{1,0:T(8,128)(2,1)S(1)} collective-permute-done((bf16[128,1024]{1,0:T(8,128)(2,1)}, bf16[128,1024]{1,0:T(8,128)(2,1)S(1)}, u32[]{:S(2)}, u32[]{:S(2)}) %collective-permute-start.26) | collective-permute-done | bytes 262176 | tf_op jit(solution)/shard_map/ppermute | solution.py:825
  333.7 3.6 shard_map.293
  346.4 5.5 %shard_map.295 = bf16[512,2816]{1,0:T(8,128)(2,1)} custom-call(s32[1]{0:T(128)S(6)} %select_n.7.core, bf16[512,256]{1,0:T(8,128)(2,1)} %get-tuple-element.142.refs_0_, bf16[512,256]{1,0:T(8,128)(2,1)} %copy-done.18, bf16[128,2816]{1,0:T(8,128)(2,1)} %shard_map.290.refs_2_.key_value, bf16[128,2816]{1,0:T(8,128)(2,1)} %copy-done.12, ...), custom_call_target="tpu_custom_call" | custom-call | tf_op jit(solution)/shard_map/pallas_call | solution.py:592
  351.9 7.1 %all-to-all-start.5 = ((bf16[16,32,2816]{2,1,0:T(8,128)(2,1)}), bf16[16,32,2816]{2,1,0:T(8,128)(2,1)S(1)}, u32[]{:S(2)}, u32[]{:S(2)}) async-start(bf16[16,32,2816]{2,1,0:T(8,128)(2,1)} %bitcast.47), calls=%async_computation.5 | async-start | bytes 5767168 | tf_op jit(solution)/shard_map/all_to_all | solution.py:617
  358.9 5.0 %shard_map.283.mine = bf16[256,1024]{1,0:T(8,128)(2,1)} custom-call(bf16[128,6400]{1,0:T(8,128)(2,1)} %get-tuple-element.119.own.refs_6_, bf16[128,6400]{1,0:T(8,128)(2,1)} %get-tuple-element.120.theirs.sent.refs_7_, bf16[1728,1024]{1,0:T(8,128)(2,1)} %weight.3), custom_call_target="tpu_custom_call" | custom-call | tf_op jit(solution)/shard_map/pallas_call | solution.py:76
  364.9 11.8 %collective-permute-done.13.theirs = bf16[256,1024]{1,0:T(8,128)(2,1)S(1)} collective-permute-done((bf16[256,1024]{1,0:T(8,128)(2,1)}, bf16[256,1024]{1,0:T(8,128)(2,1)S(1)}, u32[]{:S(2)}, u32[]{:S(2)}) %collective-permute-start.13) | collective-permute-done | bytes 524320 | tf_op jit(solution)/shard_map/ppermute | solution.py:58
  382.2 5.6 %collective-permute-done.14.oth = bf16[128,1024]{1,0:T(8,128)(2,1)S(1)} collective-permute-done((bf16[128,1024]{1,0:T(8,128)(2,1)}, bf16[128,1024]{1,0:T(8,128)(2,1)S(1)}, u32[]{:S(2)}, u32[]{:S(2)}) %collective-permute-start.14) | collective-permute-done | bytes 262176 | tf_op jit(solution)/shard_map/ppermute | solution.py:50
  392.6 4.3 %all-to-all-done.5.parts = bf16[16,32,2816]{2,1,0:T(8,128)(2,1)S(1)} async-done(((bf16[16,32,2816]{2,1,0:T(8,128)(2,1)}), bf16[16,32,2816]{2,1,0:T(8,128)(2,1)S(1)}, u32[]{:S(2)}, u32[]{:S(2)}) %all-to-all-start.5) | async-done | bytes 2883616 | tf_op jit(solution)/shard_map/all_to_all | solution.py:617
  402.9 8.4 %reduce-scatter.4.cloned.1.call-done = bf16[1,32,7168]{2,1,0:T(8,128)(2,1)} async-done(((bf16[16,32,7168]{2,1,0:T(8,128)(2,1)}), bf16[1,32,7168]{2,1,0:T(8,128)(2,1)}) %reduce-scatter.4.cloned.1.call-update) | async-done | bytes 458768
  (165 shorter events, 87.6 us)
Async XLA Ops:
  7.2 129.4 %all-gather.2.cloned.1.call-start = ((), (), s32[]{:S(2)}) async-start(), calls=%async_computation.7 | async-start | bytes 11354112 | tf_op jit(solution)/shard_map/all_gather | solution.py:693
  11.2 9.8 %collective-permute-start = (bf16[128,1024]{1,0:T(8,128)(2,1)}, bf16[128,1024]{1,0:T(8,128)(2,1)S(1)}, u32[]{:S(2)}, u32[]{:S(2)}) collective-permute-start(bf16[128,1024]{1,0:T(8,128)(2,1)} %get-tuple-element.82), channel_id=1, source_target_pairs={{0,64},{64,0},{1,65},{65,1},{2,66},{66,2},{3,67},{67,3},{4,68},{68... | collective-permute-start | bytes 786440 | tf_op jit(solution)/shard_map/ppermute | solution.py:50
  21.7 10.6 %collective-permute-start.6 = (bf16[32,5376]{1,0:T(8,128)(2,1)}, bf16[32,5376]{1,0:T(8,128)(2,1)S(1)}, u32[]{:S(2)}, u32[]{:S(2)}) collective-permute-start(bf16[32,5376]{1,0:T(8,128)(2,1)} %shard_map.272), channel_id=1, source_target_pairs={{0,64},{64,0},{1,65},{65,1},{2,66},{66,2},{3,67},{67,3},{4,68},{68... | collective-permute-start | bytes 1032200 | tf_op jit(solution)/shard_map/ppermute | solution.py:50
  30.0 8.1 %copy-start.38 = (s32[1,128]{1,0:T(1,128)S(1)}, s32[1,128]{1,0:T(1,128)}, u32[]{:S(2)}) copy-start(s32[1,128]{1,0:T(1,128)} %param.17) | copy-start | bytes 1540
  33.1 24.5 %collective-permute-start.2 = (f32[128,1024]{1,0:T(8,128)}, f32[128,1024]{1,0:T(8,128)S(1)}, u32[]{:S(2)}, u32[]{:S(2)}) collective-permute-start(f32[128,1024]{1,0:T(8,128)} %get-tuple-element.83._), channel_id=1, source_target_pairs={{0,64},{64,0},{1,65},{65,1},{2,66},{66,2},{3,67},{67,3},{4,68},{68... | collective-permute-start | bytes 1572872 | tf_op jit(solution)/shard_map/ppermute | solution.py:50
  37.5 19.2 %collective-permute-start.3 = (f16[128,1728]{1,0:T(8,128)(2,1)S(1)}, f16[128,1728]{1,0:T(8,128)(2,1)S(1)}, u32[]{:S(2)}, u32[]{:S(2)}) collective-permute-start(f16[128,1728]{1,0:T(8,128)(2,1)S(1)} %convert_element_type.43), channel_id=1, source_target_pairs={{0,64},{64,0},{1,65},{65,1},{2,66},{66,2},{3,67},{67,3},{4,68},{68... | collective-permute-start | bytes 1327112 | tf_op jit(solution)/shard_map/ppermute | solution.py:54
  57.6 12.9 %copy-start.24 = (f32[128,1024]{1,0:T(8,128)S(1)}, f32[128,1024]{1,0:T(8,128)}, u32[]{:S(2)}) copy-start(f32[128,1024]{1,0:T(8,128)} %get-tuple-element.85._) | copy-start | bytes 1572868
  61.9 35.0 %all-to-all-start = ((bf16[32,8,1792]{2,1,0:T(8,128)(2,1)}), bf16[32,8,1792]{2,1,0:T(8,128)(2,1)S(1)}, u32[]{:S(2)}, u32[]{:S(2)}) async-start(bf16[32,8,1792]{2,1,0:T(8,128)(2,1)} %bitcast.53), calls=%async_computation | async-start | bytes 1835008 | tf_op jit(solution)/shard_map/all_to_all | solution.py:697
  70.5 26.4 %collective-permute-start.1 = (f32[128,1024]{1,0:T(8,128)S(1)}, f32[128,1024]{1,0:T(8,128)S(1)}, u32[]{:S(2)}, u32[]{:S(2)}) collective-permute-start(f32[128,1024]{1,0:T(8,128)S(1)} %copy-done.24), channel_id=1, source_target_pairs={{0,64},{64,0},{1,65},{65,1},{2,66},{66,2},{3,67},{67,3},{4,68},{68... | collective-permute-start | bytes 1572872 | tf_op jit(solution)/shard_map/ppermute | solution.py:50
  75.6 16.1 %collective-permute-start.4 = (bf16[128,1024]{1,0:T(8,128)(2,1)}, bf16[128,1024]{1,0:T(8,128)(2,1)S(1)}, u32[]{:S(2)}, u32[]{:S(2)}) collective-permute-start(bf16[128,1024]{1,0:T(8,128)(2,1)} %get-tuple-element.95.up_oth), channel_id=1, source_target_pairs={{0,64},{64,0},{1,65},{65,1},{2,66},{66,2},{3,67},{67,3},{4,68},{68... | collective-permute-start | bytes 786440 | tf_op jit(solution)/shard_map/ppermute | solution.py:50
  96.9 11.2 %copy-start.11 = (f32[128,1728]{1,0:T(8,128)S(1)}, f32[128,1728]{1,0:T(8,128)}, u32[]{:S(2)}) copy-start(f32[128,1728]{1,0:T(8,128)} %get-tuple-element.96.refs_1_) | copy-start | bytes 2654212
  98.0 13.3 %copy-start.20 = (f32[128,1728]{1,0:T(8,128)S(1)}, f32[128,1728]{1,0:T(8,128)}, u32[]{:S(2)}) copy-start(f32[128,1728]{1,0:T(8,128)} %get-tuple-element.98) | copy-start | bytes 2654212
  100.6 35.9 %all-to-all-start.1 = ((bf16[32,8,1792]{2,1,0:T(8,128)(2,1)}), bf16[32,8,1792]{2,1,0:T(8,128)(2,1)S(1)}, u32[]{:S(2)}, u32[]{:S(2)}) async-start(bf16[32,8,1792]{2,1,0:T(8,128)(2,1)} %shard_map.271), calls=%async_computation.1 | async-start | bytes 1835008 | tf_op jit(solution)/shard_map/all_to_all | solution.py:699
  108.2 14.9 %collective-permute-start.7 = (f16[128,1728]{1,0:T(8,128)(2,1)S(1)}, f16[128,1728]{1,0:T(8,128)(2,1)S(1)}, u32[]{:S(2)}, u32[]{:S(2)}) collective-permute-start(f16[128,1728]{1,0:T(8,128)(2,1)S(1)} %convert_element_type.47), channel_id=1, source_target_pairs={{0,64},{64,0},{1,65},{65,1},{2,66},{66,2},{3,67},{67,3},{4,68},{68... | collective-permute-start | bytes 1327112 | tf_op jit(solution)/shard_map/ppermute | solution.py:54
  111.4 20.8 %collective-permute-start.5 = (f16[128,1728]{1,0:T(8,128)(2,1)S(1)}, f16[128,1728]{1,0:T(8,128)(2,1)S(1)}, u32[]{:S(2)}, u32[]{:S(2)}) collective-permute-start(f16[128,1728]{1,0:T(8,128)(2,1)S(1)} %convert_element_type.45), channel_id=1, source_target_pairs={{0,64},{64,0},{1,65},{65,1},{2,66},{66,2},{3,67},{67,3},{4,68},{68... | collective-permute-start | bytes 1327112 | tf_op jit(solution)/shard_map/ppermute | solution.py:54
  144.9 13.4 %collective-permute-start.8 = (bf16[128,2048]{1,0:T(8,128)(2,1)}, bf16[128,2048]{1,0:T(8,128)(2,1)S(1)}, u32[]{:S(2)}, u32[]{:S(2)}) collective-permute-start(bf16[128,2048]{1,0:T(8,128)(2,1)} %get-tuple-element.100.mine), channel_id=1, source_target_pairs={{0,1},{1,0},{2,3},{3,2},{4,5},{5,4},{6,7},{7,6},{8,9},{9,8},{10,11... | collective-permute-start | bytes 1572872 | tf_op jit(solution)/shard_map/ppermute | solution.py:58
  149.4 3.5 collective-permute-start.9
  152.4 1.9 collective-permute-start.10
  172.9 12.7 %collective-permute-start.11 = (bf16[128,2048]{1,0:T(8,128)(2,1)}, bf16[128,2048]{1,0:T(8,128)(2,1)S(1)}, u32[]{:S(2)}, u32[]{:S(2)}) collective-permute-start(bf16[128,2048]{1,0:T(8,128)(2,1)} %get-tuple-element.106.mine), channel_id=1, source_target_pairs={{0,1},{1,0},{2,3},{3,2},{4,5},{5,4},{6,7},{7,6},{8,9},{9,8},{10,11... | collective-permute-start | bytes 1572872 | tf_op jit(solution)/shard_map/ppermute | solution.py:58
  186.4 36.9 %collective-permute-start.12 = (bf16[128,6400]{1,0:T(8,128)(2,1)}, bf16[128,6400]{1,0:T(8,128)(2,1)S(1)}, u32[]{:S(2)}, u32[]{:S(2)}) collective-permute-start(bf16[128,6400]{1,0:T(8,128)(2,1)} %shard_map.278.refs_0_), channel_id=1, source_target_pairs={{0,64},{64,0},{1,65},{65,1},{2,66},{66,2},{3,67},{67,3},{4,68},{68... | collective-permute-start | bytes 4915208 | tf_op jit(solution)/shard_map/ppermute | solution.py:50
  198.7 20.5 %all-to-all-start.2 = ((bf16[32,8,1792]{2,1,0:T(8,128)(2,1)}), bf16[32,8,1792]{2,1,0:T(8,128)(2,1)S(1)}, u32[]{:S(2)}, u32[]{:S(2)}) async-start(bf16[32,8,1792]{2,1,0:T(8,128)(2,1)} %bitcast.54), calls=%async_computation.2 | async-start | bytes 1835008 | tf_op jit(solution)/shard_map/all_to_all | solution.py:697
  222.6 22.3 %copy-start.6 = (bf16[128,2816]{1,0:T(8,128)(2,1)S(1)}, bf16[128,2816]{1,0:T(8,128)(2,1)}, u32[]{:S(2)}) copy-start(bf16[128,2816]{1,0:T(8,128)(2,1)} %get-tuple-element.118.refs_0_) | copy-start | bytes 2162692
  224.5 31.9 %collective-permute-start.19 = (bf16[128,6400]{1,0:T(8,128)(2,1)}, bf16[128,6400]{1,0:T(8,128)(2,1)}, u32[]{:S(2)}, u32[]{:S(2)}) collective-permute-start(bf16[128,6400]{1,0:T(8,128)(2,1)} %get-tuple-element.119.own.refs_6_), channel_id=1, source_target_pairs={{0,2},{2,0},{4,6},{6,4},{8,10},{10,8},{12,14},{14,12},{16,18},{18,... | collective-permute-start | bytes 4915208 | tf_op jit(solution)/shard_map/ppermute | solution.py:62
  224.7 31.7 %collective-permute-start.20 = (bf16[128,6400]{1,0:T(8,128)(2,1)}, bf16[128,6400]{1,0:T(8,128)(2,1)}, u32[]{:S(2)}, u32[]{:S(2)}) collective-permute-start(bf16[128,6400]{1,0:T(8,128)(2,1)} %get-tuple-element.120.theirs.sent.refs_7_), channel_id=1, source_target_pairs={{0,2},{2,0},{4,6},{6,4},{8,10},{10,8},{12,14},{14,12},{16,18},{18,... | collective-permute-start | bytes 4915208 | tf_op jit(solution)/shard_map/ppermute | solution.py:62
  225.0 20.0 %collective-permute-start.17 = (bf16[128,2816]{1,0:T(8,128)(2,1)}, bf16[128,2816]{1,0:T(8,128)(2,1)S(1)}, u32[]{:S(2)}, u32[]{:S(2)}) collective-permute-start(bf16[128,2816]{1,0:T(8,128)(2,1)} %get-tuple-element.130.refs_10_), channel_id=1, source_target_pairs={{0,64},{64,0},{1,65},{65,1},{2,66},{66,2},{3,67},{67,3},{4,68},{68... | collective-permute-start | bytes 2162696 | tf_op jit(solution)/shard_map/ppermute | solution.py:50
  228.0 23.0 %collective-permute-start.21 = (bf16[128,2816]{1,0:T(8,128)(2,1)}, bf16[128,2816]{1,0:T(8,128)(2,1)}, u32[]{:S(2)}, u32[]{:S(2)}) collective-permute-start(bf16[128,2816]{1,0:T(8,128)(2,1)} %get-tuple-element.130.refs_10_), channel_id=1, source_target_pairs={{0,2},{2,0},{4,6},{6,4},{8,10},{10,8},{12,14},{14,12},{16,18},{18,... | collective-permute-start | bytes 2162696 | tf_op jit(solution)/shard_map/ppermute | solution.py:62
  228.0 38.5 %all-to-all-start.3 = ((bf16[32,8,1792]{2,1,0:T(8,128)(2,1)}), bf16[32,8,1792]{2,1,0:T(8,128)(2,1)S(1)}, u32[]{:S(2)}, u32[]{:S(2)}) async-start(bf16[32,8,1792]{2,1,0:T(8,128)(2,1)} %shard_map.281.refs_2_.refs_0_), calls=%async_computation.3 | async-start | bytes 1835008 | tf_op jit(solution)/shard_map/all_to_all | solution.py:699
  235.5 175.9 %reduce-scatter.4.cloned.1.call-start = ((), (), s32[]{:S(2)}) async-start(), calls=%async_computation.8 | async-start | bytes 7798784
  244.9 10.1 %collective-permute-start.22 = (bf16[128,2816]{1,0:T(8,128)(2,1)S(1)}, bf16[128,2816]{1,0:T(8,128)(2,1)S(1)}, u32[]{:S(2)}, u32[]{:S(2)}) collective-permute-start(bf16[128,2816]{1,0:T(8,128)(2,1)S(1)} %collective-permute-done.17.sent.refs_11_), channel_id=1, source_target_pairs={{0,2},{2,0},{4,6},{6,4},{8,10},{10,8},{12,14},{14,12},{16,18},{18,... | collective-permute-start | bytes 2162696 | tf_op jit(solution)/shard_map/ppermute | solution.py:62
  245.0 22.5 %collective-permute-start.15 = (bf16[128,2816]{1,0:T(8,128)(2,1)S(1)}, bf16[128,2816]{1,0:T(8,128)(2,1)S(1)}, u32[]{:S(2)}, u32[]{:S(2)}) collective-permute-start(bf16[128,2816]{1,0:T(8,128)(2,1)S(1)} %copy-done.6), channel_id=1, source_target_pairs={{0,64},{64,0},{1,65},{65,1},{2,66},{66,2},{3,67},{67,3},{4,68},{68... | collective-permute-start | bytes 2162696 | tf_op jit(solution)/shard_map/ppermute | solution.py:50
  251.0 3.7 collective-permute-start.18
  254.7 1.7 collective-permute-start.16
  271.7 2.6 collective-permute-start.32
  272.3 3.1 collective-permute-start.33
  281.0 63.1 %all-to-all-start.4 = ((bf16[16,32,2816]{2,1,0:T(8,128)(2,1)}), bf16[16,32,2816]{2,1,0:T(8,128)(2,1)S(1)}, u32[]{:S(2)}, u32[]{:S(2)}) async-start(bf16[16,32,2816]{2,1,0:T(8,128)(2,1)} %bitcast.50), calls=%async_computation.4 | async-start | bytes 5767168 | tf_op jit(solution)/shard_map/all_to_all | solution.py:617
  288.3 19.6 %collective-permute-start.23 = (bf16[128,2816]{1,0:T(8,128)(2,1)}, bf16[128,2816]{1,0:T(8,128)(2,1)S(1)}, u32[]{:S(2)}, u32[]{:S(2)}) collective-permute-start(bf16[128,2816]{1,0:T(8,128)(2,1)} %shard_map.290.refs_2_.key_value), channel_id=1, source_target_pairs={{0,64},{64,0},{1,65},{65,1},{2,66},{66,2},{3,67},{67,3},{4,68},{68... | collective-permute-start | bytes 2162696 | tf_op jit(solution)/shard_map/ppermute | solution.py:50
  289.1 51.9 %collective-permute-start.27 = (bf16[128,2816]{1,0:T(8,128)(2,1)}, bf16[128,2816]{1,0:T(8,128)(2,1)S(1)}, u32[]{:S(2)}, u32[]{:S(2)}) collective-permute-start(bf16[128,2816]{1,0:T(8,128)(2,1)} %shard_map.290.refs_2_.key_value), channel_id=1, source_target_pairs={{0,2},{2,0},{4,6},{6,4},{8,10},{10,8},{12,14},{14,12},{16,18},{18,... | collective-permute-start | bytes 2162696 | tf_op jit(solution)/shard_map/ppermute | solution.py:62
  307.9 36.2 %collective-permute-start.28 = (bf16[128,2816]{1,0:T(8,128)(2,1)S(1)}, bf16[128,2816]{1,0:T(8,128)(2,1)}, u32[]{:S(2)}, u32[]{:S(2)}) collective-permute-start(bf16[128,2816]{1,0:T(8,128)(2,1)S(1)} %collective-permute-done.23.key_value_theirs.refs_3_), channel_id=1, source_target_pairs={{0,2},{2,0},{4,6},{6,4},{8,10},{10,8},{12,14},{14,12},{16,18},{18,... | collective-permute-start | bytes 2162696 | tf_op jit(solution)/shard_map/ppermute | solution.py:62
  317.9 9.4 %collective-permute-start.24 = (bf16[128,1024]{1,0:T(8,128)(2,1)}, bf16[128,1024]{1,0:T(8,128)(2,1)S(1)}, u32[]{:S(2)}, u32[]{:S(2)}) collective-permute-start(bf16[128,1024]{1,0:T(8,128)(2,1)} %get-tuple-element.135.mine), channel_id=1, source_target_pairs={{0,1},{1,0},{2,3},{3,2},{4,5},{5,4},{6,7},{7,6},{8,9},{9,8},{10,11... | collective-permute-start | bytes 786440 | tf_op jit(solution)/shard_map/ppermute | solution.py:58
  318.3 14.6 %collective-permute-start.26 = (bf16[128,1024]{1,0:T(8,128)(2,1)}, bf16[128,1024]{1,0:T(8,128)(2,1)S(1)}, u32[]{:S(2)}, u32[]{:S(2)}) collective-permute-start(bf16[128,1024]{1,0:T(8,128)(2,1)} %get-tuple-element.136), channel_id=1, source_target_pairs={{0,65},{1,64},{64,1},{65,0},{2,67},{3,66},{66,3},{67,2},{4,69},{5,... | collective-permute-start | bytes 786440 | tf_op jit(solution)/shard_map/ppermute | solution.py:825
  319.1 13.8 %collective-permute-start.25 = (bf16[128,1024]{1,0:T(8,128)(2,1)}, bf16[128,1024]{1,0:T(8,128)(2,1)S(1)}, u32[]{:S(2)}, u32[]{:S(2)}) collective-permute-start(bf16[128,1024]{1,0:T(8,128)(2,1)} %get-tuple-element.136), channel_id=1, source_target_pairs={{0,64},{64,0},{1,65},{65,1},{2,66},{66,2},{3,67},{67,3},{4,68},{68... | collective-permute-start | bytes 786440 | tf_op jit(solution)/shard_map/ppermute | solution.py:50
  337.3 3.7 collective-permute-start.30
  337.3 5.1 %collective-permute-start.31 = (bf16[16,1024]{1,0:T(8,128)(2,1)}, bf16[16,1024]{1,0:T(8,128)(2,1)S(1)}, u32[]{:S(2)}, u32[]{:S(2)}) collective-permute-start(bf16[16,1024]{1,0:T(8,128)(2,1)} %get-tuple-element.144), channel_id=1, source_target_pairs={{0,66},{2,64},{4,70},{6,68},{8,74},{10,72},{12,78},{14,76},{16,82}... | collective-permute-start | bytes 98312 | tf_op jit(solution)/shard_map/ppermute | solution.py:832
  338.5 5.6 %collective-permute-start.29 = (bf16[16,1024]{1,0:T(8,128)(2,1)}, bf16[16,1024]{1,0:T(8,128)(2,1)S(1)}, u32[]{:S(2)}, u32[]{:S(2)}) collective-permute-start(bf16[16,1024]{1,0:T(8,128)(2,1)} %get-tuple-element.144), channel_id=1, source_target_pairs={{0,64},{64,0},{1,65},{65,1},{2,66},{66,2},{3,67},{67,3},{4,68},{68... | collective-permute-start | bytes 98312 | tf_op jit(solution)/shard_map/ppermute | solution.py:50
  351.9 45.1 %all-to-all-start.5 = ((bf16[16,32,2816]{2,1,0:T(8,128)(2,1)}), bf16[16,32,2816]{2,1,0:T(8,128)(2,1)S(1)}, u32[]{:S(2)}, u32[]{:S(2)}) async-start(bf16[16,32,2816]{2,1,0:T(8,128)(2,1)} %bitcast.47), calls=%async_computation.5 | async-start | bytes 5767168 | tf_op jit(solution)/shard_map/all_to_all | solution.py:617
  363.9 26.9 %copy-start.2 = (bf16[16,32,2816]{2,1,0:T(8,128)(2,1)S(1)}, bf16[16,32,2816]{2,1,0:T(8,128)(2,1)}, u32[]{:S(2)}) copy-start(bf16[16,32,2816]{2,1,0:T(8,128)(2,1)} %copy-done.1) | copy-start | bytes 8650756
  363.9 12.8 %collective-permute-start.13 = (bf16[256,1024]{1,0:T(8,128)(2,1)}, bf16[256,1024]{1,0:T(8,128)(2,1)S(1)}, u32[]{:S(2)}, u32[]{:S(2)}) collective-permute-start(bf16[256,1024]{1,0:T(8,128)(2,1)} %shard_map.283.mine), channel_id=1, source_target_pairs={{0,1},{1,0},{2,3},{3,2},{4,5},{5,4},{6,7},{7,6},{8,9},{9,8},{10,11... | collective-permute-start | bytes 1572872 | tf_op jit(solution)/shard_map/ppermute | solution.py:58
  379.7 8.1 %collective-permute-start.14 = (bf16[128,1024]{1,0:T(8,128)(2,1)}, bf16[128,1024]{1,0:T(8,128)(2,1)S(1)}, u32[]{:S(2)}, u32[]{:S(2)}) collective-permute-start(bf16[128,1024]{1,0:T(8,128)(2,1)} %get-tuple-element.122), channel_id=1, source_target_pairs={{0,64},{64,0},{1,65},{65,1},{2,66},{66,2},{3,67},{67,3},{4,68},{68... | collective-permute-start | bytes 786440 | tf_op jit(solution)/shard_map/ppermute | solution.py:50
  (33 other events, 50.7 us)
Sparse Core Ops, SparseCore 0:
  33.3 71.2 all-gather.1
  272.6 138.7 reduce-scatter.3
